TPU v7x, 32 devices: a whole 2x2x4 slice. The times are simulated.
32 devices in a mesh: seq: 8 (over z, y), head: 4 (over x, core).
Axes of the slice: x: 2, y: 2, z: 4, core: 2. Of those that a mesh axis runs over, the one named last changes fastest.
Arguments:
- queries: bfloat16 [1, 4096, 1024], P(None, 'seq', 'head'), may hold values from -40 to 40
- key_vectors: bfloat16 [1, 4096, 1024], P(None, 'seq', 'head'), may hold values from -40 to 40
- value_vectors: bfloat16 [1, 4096, 1024], P(None, 'seq', 'head'), may hold values from -6 to 6
- out_weight: bfloat16 [1024, 1024], replicated, may hold values from -0.1875 to 0.1875
Outputs:
- layer_output: bfloat16 [1, 4096, 1024], P(None, ('seq', 'head'))
All inputs are finite; a program needn't handle non-finite values.
Results may differ from a plain program's by a relative error of at most 0.038.
Values may be sent and summed in bfloat16 or wider, within the bound.
No kernel may reach another device: no remote copies, remote signals or barrier semaphores. Data moves between devices by JAX's collectives and lax.ppermute only.
A program may use at most 192 MiB of HBM per device.

v0:
```python
import jax
import jax.numpy as jnp
from jax import lax
from jax.experimental import pallas as pl
from jax.experimental.pallas import tpu as pltpu
from jax.sharding import PartitionSpec as P

HD = 64
BLOCK = 128
LEVELS = 4
SLAB = 8
PAIR = 2 * HD

neg_fill = -1e30
root_half = 0.7071067811865476
log2_e = 1.4426950408889634
log2_scale = HD**-0.5 * log2_e
least_share = 2.0**-100
AHEAD = 3

FAN = 2**LEVELS


def slabs_of(scratch, block):
    return [scratch[pl.ds(BLOCK * block + j, SLAB, stride=FAN), :] for j in range(FAN)]


def pooled_slabs(slabs):
    return [
        ((low + high) * root_half).astype(jnp.bfloat16).astype(jnp.float32)
        for low, high in zip(slabs[0::2], slabs[1::2])
    ]


def joined(slabs):
    return jnp.concatenate(slabs, axis=0).astype(jnp.bfloat16)


def spill(source, scratch):
    for half in range(scratch.shape[0]):
        scratch[half] = source[:, half * PAIR : (half + 1) * PAIR].astype(jnp.float32)


def pool_kernel(
    k_hbm, v_hbm, k_ref, v_ref, first_ref, one_ref, two_ref, scratch, sems
):
    rows = k_ref.shape[0]
    blocks = rows // BLOCK
    arrivals = []
    for half in range(2):
        here = pl.ds(half * rows // 2, rows // 2)
        for which, (source, target) in enumerate(((k_hbm, k_ref), (v_hbm, v_ref))):
            copy = pltpu.make_async_copy(
                source.at[0, here, :], target.at[here, :], sems.at[which, half]
            )
            copy.start()
            for block in range(half * blocks // 2, (half + 1) * blocks // 2):
                arrivals.append((block, which, target, copy))
    even = lax.rem(lax.axis_index("seq"), 2) == 0
    for block, which, ref, copy in arrivals:
        if block % (blocks // 2) == 0:
            copy.wait()
        here = pl.ds(block * BLOCK, BLOCK)
        spill(ref.at[here, :], scratch.at[which, block])
        for half in range(scratch.shape[2]):
            lanes = pl.ds(half * PAIR, PAIR)
            one = pooled_slabs(slabs_of(scratch.at[which, block, half], 0))
            one_ref[which, pl.ds(block * BLOCK // 2, BLOCK // 2), lanes] = joined(one)
            two_ref[which, pl.ds(block * BLOCK // 4, BLOCK // 4), lanes] = joined(pooled_slabs(one))
    inner = rows // 4 - BLOCK // 4
    for which, ref in enumerate((k_ref, v_ref)):
        first_ref[which, :BLOCK, :] = jnp.where(even, ref[rows - BLOCK :, :], ref[:BLOCK, :])
        first_ref[which, BLOCK:, :] = jnp.where(
            even, two_ref[which, :inner, :], two_ref[which, BLOCK // 4 :, :]
        )


def repooled(field):
    rows, lanes = field.shape
    slabs = field.astype(jnp.float32).reshape(rows // (2 * SLAB), 2, SLAB, lanes)
    return ((slabs[:, 0] + slabs[:, 1]) * root_half).reshape(rows // 2, lanes).astype(jnp.bfloat16)


def deeper_kernel(k_ref, v_ref, two_ref, second_ref, three_ref, four_ref):
    rows = k_ref.shape[0]
    even = lax.rem(lax.axis_index("seq"), 2) == 0
    for which, ref in enumerate((k_ref, v_ref)):
        second_ref[which] = jnp.where(even, ref[:BLOCK, :], ref[rows - BLOCK :, :])
        three = repooled(two_ref[which])
        three_ref[which] = three
        four_ref[which] = repooled(three)


def repooled(field):
    rows, lanes = field.shape
    slabs = field.astype(jnp.float32).reshape(rows // (2 * SLAB), 2, SLAB, lanes)
    return ((slabs[:, 0] + slabs[:, 1]) * root_half).reshape(rows // 2, lanes).astype(jnp.bfloat16)


def score(queries, keys, hold, is_open=None):
    rows = queries.shape[0]
    low = lax.broadcasted_iota(jnp.int32, (rows, PAIR), 1) < HD
    zero = jnp.zeros_like(queries)
    both = jnp.concatenate([jnp.where(low, queries, zero), jnp.where(low, zero, queries)], axis=0)
    raw = lax.dot_general(both, keys, (((1,), (1,)), ((), ())), preferred_element_type=jnp.float32)
    if is_open is not None:
        raw = jnp.where(is_open, raw, neg_fill)
    hold[...] = raw
    return jnp.max(raw, axis=1, keepdims=True)


def weigh(hold, top, values):
    rows = top.shape[0] // 2
    low = lax.broadcasted_iota(jnp.int32, (rows, PAIR), 1) < HD
    weights = jnp.exp2((hold[...] - top) * log2_scale).astype(jnp.bfloat16)
    result = jnp.dot(weights, values, preferred_element_type=jnp.float32)
    return (
        log2_scale * jnp.where(low, top[:rows], top[rows:]),
        jnp.where(low, result[:rows, :PAIR], result[rows:, :PAIR]),
        jnp.where(low, result[:rows, PAIR:], result[rows:, PAIR:]),
    )


def merged(fine, coarse):
    top = jnp.maximum(fine[0], coarse[0])
    keep = jnp.exp2(fine[0] - top)
    join = jnp.exp2(coarse[0] - top)
    return top, fine[1] * keep + coarse[1] * join, fine[2] * keep + coarse[2] * join


def doubled(field):
    rows, lanes = field.shape
    slabs = field.reshape(rows // SLAB, 1, SLAB, lanes)
    return jnp.broadcast_to(slabs, (rows // SLAB, 2, SLAB, lanes)).reshape(2 * rows, lanes)


def with_ones(values, weight=1.0):
    if weight != 1.0:
        values = values * jnp.bfloat16(weight)
    return jnp.concatenate([values, jnp.full(values.shape, weight, jnp.bfloat16)], axis=1)


def local_kernel(
    q_ref, k_ref, v_ref, one_ref, four_ref, edge_q, two_q, three_q, four_q, state,
    scratch, near_hold, coarse_hold,
):
    rows = q_ref.shape[0]
    blocks = rows // BLOCK
    pairs = scratch.shape[0]
    spill(q_ref, scratch)
    fine, one_q = [], []
    for pair in range(pairs):
        lanes = pl.ds(pair * PAIR, PAIR)
        ladder = [[], [], [], [], []]
        for block in range(blocks):
            slabs = slabs_of(scratch.at[pair], block)
            ladder[0].append(joined(slabs))
            for level in range(1, LEVELS + 1):
                slabs = pooled_slabs(slabs)
                ladder[level] += slabs
        edge_q[0, :, lanes] = ladder[0][0]
        edge_q[1, :, lanes] = ladder[0][-1]
        two_q[:, lanes] = joined(ladder[2])
        three_q[:, lanes] = joined(ladder[3])
        four_q[:, lanes] = joined(ladder[4])
        fine.append(ladder[0])
        one_q.append([joined(ladder[1][n : n + FAN]) for n in range(0, len(ladder[1]), FAN)])
    windows = [(max(n - 1, 0) * BLOCK, min(n + 2, blocks) * BLOCK) for n in range(blocks)]
    tops = {}
    for pair in range(pairs):
        lanes = pl.ds(pair * PAIR, PAIR)
        for half in range(blocks // 2):
            there = pl.ds((half ^ 1) * BLOCK, BLOCK)
            tops[pair, half] = score(
                one_q[pair][half], one_ref[0, there, lanes], coarse_hold.at[pair, half]
            )
            for block in (2 * half, 2 * half + 1):
                low, high = windows[block]
                hold = near_hold.at[pair, block, :, : high - low]
                tops[pair, half, block] = score(fine[pair][block], k_ref[low:high, lanes], hold)
    for pair in range(pairs):
        lanes = pl.ds(pair * PAIR, PAIR)
        for half in range(blocks // 2):
            there = pl.ds((half ^ 1) * BLOCK, BLOCK)
            coarse = weigh(
                coarse_hold.at[pair, half], tops[pair, half], with_ones(one_ref[1, there, lanes])
            )
            for block in (2 * half, 2 * half + 1):
                low, high = windows[block]
                hold = near_hold.at[pair, block, :, : high - low]
                near = weigh(hold, tops[pair, half, block], with_ones(v_ref[low:high, lanes]))
                part = slice((block - 2 * half) * BLOCK // 2, (block - 2 * half + 1) * BLOCK // 2)
                done = merged(near, [doubled(x[part]) for x in coarse])
                for index, field in enumerate(done):
                    state[index, block * BLOCK : (block + 1) * BLOCK, lanes] = field


def join_kernel(four_ref, six_ref, query_ref, out):
    sixteenth = four_ref.shape[1]
    out[:, :sixteenth, :] = four_ref[...]
    out[:, sixteenth:, :] = six_ref[...]


def coarse_kernel(
    two_q, three_q, first_ref, three_a, three_b, coarse, near_ref, scratch, two_ref, two_hold, three_hold
):
    inner = first_ref.shape[1] - BLOCK
    pairs = scratch.shape[1]
    two_ref[:, :inner, :] = first_ref[:, BLOCK:, :]
    for which in range(2):
        spill(first_ref.at[which, pl.ds(0, BLOCK), :], scratch.at[which])
        for half in range(pairs):
            lanes = pl.ds(half * PAIR, PAIR)
            slabs = slabs_of(scratch.at[which, half], 0)
            two_ref[which, inner:, lanes] = joined(pooled_slabs(pooled_slabs(slabs)))
        near_ref[which] = repooled(repooled(two_ref[which]))
    steps = {}
    for pair in range(pairs):
        lanes = pl.ds(pair * PAIR, PAIR)
        three = [
            jnp.concatenate([three_a[which, :, lanes], three_b[which, :, lanes]], axis=0)
            for which in range(2)
        ]
        steps[pair, 3] = (
            score(three_q[:, lanes], three[0], three_hold.at[pair]), with_ones(three[1])
        )
        steps[pair, 2] = (
            score(two_q[:, lanes], two_ref[0, :, lanes], two_hold.at[pair]),
            with_ones(two_ref[1, :, lanes]),
        )
    for pair in range(pairs):
        three = weigh(three_hold.at[pair], *steps[pair, 3])
        two = merged(weigh(two_hold.at[pair], *steps[pair, 2]), [doubled(x) for x in three])
        for index, field in enumerate(two):
            coarse[index, :, pl.ds(pair * PAIR, PAIR)] = field


def mid_kernel(edge_q, coarse, state, first_ref, second_ref, fine, *refs):
    outs, (ready, holds) = refs[:-2], refs[-2:]
    own = lax.axis_index("head")
    rows = state.shape[1]
    blocks = rows // BLOCK
    position = lax.axis_index("seq")
    last = lax.axis_size("seq") - 1
    even = lax.rem(position, 2) == 0
    opens = (position > 0, position < last)
    pairs = holds.shape[0]
    steps = {}
    for pair in range(pairs):
        lanes = pl.ds(pair * PAIR, PAIR)
        inner = [first_ref[which, :BLOCK, lanes] for which in range(2)]
        outer = [second_ref[which, :, lanes] for which in range(2)]
        for side in range(2):
            halo = [
                jnp.where(even, *((outer[which], inner[which])[:: 1 - 2 * side]))
                for which in range(2)
            ]
            steps[pair, side] = (
                score(edge_q[side, :, lanes], halo[0], holds.at[pair, side], opens[side]),
                with_ones(halo[1]),
            )
    for pair in range(pairs):
        lanes = pl.ds(pair * PAIR, PAIR)
        for block in range(blocks):
            here = slice(block * BLOCK, (block + 1) * BLOCK)
            quarter = slice(block * BLOCK // 4, (block + 1) * BLOCK // 4)
            done = merged(
                [state[index, here, lanes] for index in range(3)],
                [doubled(doubled(coarse[index, quarter, lanes])) for index in range(3)],
            )
            for side, edge in enumerate((0, blocks - 1)):
                if block == edge:
                    done = merged(done, weigh(holds.at[pair, side], *steps[pair, side]))
            result = done[1] / done[2]
            fine[0, here, lanes] = result
            fine[1, here, lanes] = done[0] + jnp.log(done[2]) * log2_e
            ready[block, :, lanes] = result.astype(jnp.bfloat16)
    for step, out in enumerate(outs, AHEAD):
        out[...] = ready[own ^ step]


def repeated(field):
    return jnp.concatenate([field] * FAN, axis=0)


def finish_blocks(fine, coarse, steps):
    own = lax.axis_index("head")
    features = fine.shape[2]
    for step, out in steps:
        block = own ^ step
        here = pl.ds(pl.multiple_of(block * BLOCK, BLOCK), BLOCK)
        few = pl.ds(pl.multiple_of(block * SLAB, SLAB), SLAB)
        shares = []
        for pair in range(features // PAIR):
            lanes = pl.ds(pair * PAIR, PAIR)
            fine_sum, coarse_sum = fine[1, here, lanes], repeated(coarse[1, few, lanes])
            if step < AHEAD:
                keep = 1.0 / (1.0 + jnp.exp2(coarse_sum - fine_sum))
                ours, theirs = fine[0, here, lanes], repeated(coarse[0, few, lanes])
                out[:, lanes] = (theirs + keep * (ours - theirs)).astype(jnp.bfloat16)
            else:
                ratio = jnp.exp2(-jnp.abs(fine_sum - coarse_sum))
                less = jnp.maximum(ratio / (1.0 + ratio), least_share)
                shares.append(jnp.where(fine_sum <= coarse_sum, less, -less).astype(jnp.bfloat16))
        if step >= AHEAD:
            pick = lax.broadcasted_iota(jnp.int32, (2 * SLAB, features), 1) == HD * (
                lax.broadcasted_iota(jnp.int32, (2 * SLAB, features), 0)
            )
            by_head = lax.dot_general(
                pick.astype(jnp.bfloat16),
                jnp.concatenate(shares, axis=1),
                (((1,), (1,)), ((), ())),
                preferred_element_type=jnp.float32,
            )[:SLAB]
            blank = jnp.zeros((SLAB, features - BLOCK), jnp.float32)
            out[...] = jnp.concatenate(
                [coarse[0, few, :], jnp.concatenate([by_head, blank], axis=1)], axis=0
            ).astype(jnp.bfloat16)


def finish_kernel(
    four_q, fine, four_ref, near_ref, three_a, three_b, fours_a, fours_b, *refs
):
    refs, (coarse, four_hold) = refs[:-2], refs[-2:]
    count = AHEAD - 2
    far, outs = refs[:-count], refs[-count:]
    pairs = four_q.shape[1] // PAIR
    steps = {}
    for pair in range(pairs):
        lanes = pl.ds(pair * PAIR, PAIR)
        ours, theirs, beyond = [], [], []
        for which in range(2):
            ours.append(
                [four_ref[which, :, lanes], near_ref[which, :, lanes]]
                + [repooled(field[which, :, lanes]) for field in (three_a, three_b)]
            )
            theirs.append([field[which, :, lanes] for field in (fours_a, fours_b)])
            beyond.append([field[which, :, lanes] for field in far])
        steps[pair] = (
            score(
                four_q[:, lanes],
                jnp.concatenate(ours[0] + theirs[0] + beyond[0], axis=0),
                four_hold.at[pair],
            ),
            jnp.concatenate(
                [with_ones(field) for field in ours[1]]
                + [with_ones(field, 2.0) for field in theirs[1]]
                + [with_ones(field) for field in beyond[1]],
                axis=0,
            ),
        )
    for pair in range(pairs):
        lanes = pl.ds(pair * PAIR, PAIR)
        top, numer, rowsum = weigh(four_hold.at[pair], *steps[pair])
        coarse[0, :, lanes] = numer / rowsum
        coarse[1, :, lanes] = top + jnp.log(rowsum) * log2_e
    finish_blocks(fine, coarse, zip(range(2, AHEAD), outs))


def rest_kernel(fine, coarse, *outs):
    steps = [0, 1, *range(AHEAD, lax.axis_size("head"))]
    finish_blocks(fine, coarse, zip(steps, outs))


def rejoin_kernel(*refs):
    outs = refs[len(refs) // 3 * 2 :]
    for early, late_ref, out in zip(refs, refs[len(outs) :], outs):
        features = early.shape[1]
        late = late_ref[...].astype(jnp.float32)
        spread = lax.broadcasted_iota(jnp.int32, (SLAB, features), 1) // HD == (
            lax.broadcasted_iota(jnp.int32, (SLAB, features), 0)
        )
        signed = lax.dot_general(
            late[SLAB:, :BLOCK].astype(jnp.bfloat16),
            spread.astype(jnp.bfloat16),
            (((0,), (0,)), ((), ())),
            preferred_element_type=jnp.float32,
        )
        keep = jnp.where(signed >= 0, signed, 1.0 + signed)
        join = jnp.where(signed >= 0, 1.0 - signed, -signed)
        result = keep * early[...] + join * repeated(late[:SLAB])
        out[...] = result.astype(jnp.bfloat16)


def widen_kernel(*refs):
    half = len(refs) // 2
    for ref, out in zip(refs[:half], refs[half:]):
        out[...] = ref[...].astype(jnp.float32)


def carry_kernel(whole_ref, *refs):
    half = len(refs) // 2
    for ref, out in zip(refs[:half], refs[half:]):
        out[...] = ref[...]


def partial_kernel(own_ref, weight_ref, out_ref):
    features = own_ref.shape[1]
    start = pl.multiple_of(lax.axis_index("head") * features, features)
    out_ref[...] = jnp.dot(
        own_ref[...], weight_ref[pl.ds(start, features), :], preferred_element_type=jnp.float32
    )


def project_kernel(partial_ref, *refs):
    parts, (weight_ref, out_hbm, scratch, staged, sems) = refs[:-5], refs[-5:]
    own = lax.axis_index("head")
    features = parts[0].shape[1]
    chunk = staged.shape[2]
    copies = []
    for index in range(staged.shape[0]):
        columns = pl.ds(index * chunk, chunk)
        total = partial_ref[:, columns]
        for step, part in zip([*range(2, len(parts) + 1), 1], parts):
            start = pl.multiple_of((own ^ step) * features, features)
            total += jnp.dot(
                part[...],
                weight_ref[pl.ds(start, features), columns],
                preferred_element_type=jnp.float32,
            )
        for half in range(chunk // PAIR):
            lanes = slice(half * PAIR, (half + 1) * PAIR)
            scratch[index, half] = total[:, lanes]
            for i in range(SLAB):
                staged[index, i * FAN : (i + 1) * FAN, lanes] = scratch[
                    index, half, pl.ds(i, FAN, stride=SLAB), :
                ].astype(jnp.bfloat16)
        copy = pltpu.make_async_copy(staged.at[index], out_hbm.at[:, columns], sems.at[index])
        copy.start()
        copies.append(copy)
    for copy in copies:
        copy.wait()


def repool_outside(field):
    which, rows, lanes = field.shape
    slabs = field.astype(jnp.float32).reshape(which, rows // (2 * SLAB), 2, SLAB, lanes)
    sums = (slabs[:, :, 0] + slabs[:, :, 1]) * root_half
    return sums.reshape(which, rows // 2, lanes).astype(jnp.bfloat16)


def swapped(block, axis, mask):
    return lax.ppermute(block, axis, [(i, i ^ mask) for i in range(lax.axis_size(axis))])


def across(block):
    count, heads = lax.axis_size("seq"), lax.axis_size("head")
    route = []
    for seq in range(count):
        end = seq in (0, count - 1)
        other = seq if end else seq + 1 if seq % 2 else seq - 1
        for head in range(heads):
            route.append((seq * heads + head, other * heads + (head ^ 1 if end else head)))
    return lax.ppermute(block, ("seq", "head"), route)


def per_device(queries, key_vectors, value_vectors, out_weight):
    rows, features = queries.shape[1:]
    key_vectors, value_vectors = [
        pltpu.with_memory_space_constraint(x, pltpu.HBM) for x in (key_vectors, value_vectors)
    ]
    pairs = features // PAIR
    seq_count, head_count = lax.axis_size("seq"), lax.axis_size("head")
    bf16 = lambda *shape: jax.ShapeDtypeStruct(shape, jnp.bfloat16)
    params = pltpu.CompilerParams(vmem_limit_bytes=32 * 1024 * 1024)

    hbm = pl.BlockSpec(memory_space=pltpu.HBM)
    vmem = pl.BlockSpec(memory_space=pltpu.VMEM)
    keys, values, first, one, two = pl.pallas_call(
        pool_kernel,
        in_specs=[hbm] * 2,
        out_shape=[
            bf16(rows, features),
            bf16(rows, features),
            bf16(2, BLOCK + rows // 4 - BLOCK // 4, features),
            bf16(2, rows // 2, features),
            bf16(2, rows // 4, features),
        ],
        scratch_shapes=[
            pltpu.VMEM((2, rows // BLOCK, pairs, BLOCK, PAIR), jnp.float32),
            pltpu.SemaphoreType.DMA((2, 2)),
        ],
        compiler_params=params,
        name="pool",
    )(key_vectors, value_vectors)
    second, three, four = pl.pallas_call(
        deeper_kernel,
        out_shape=[
            bf16(2, BLOCK, features),
            bf16(2, rows // 8, features),
            bf16(2, rows // 16, features),
        ],
        compiler_params=params,
        cost_estimate=pl.CostEstimate(flops=2**31, bytes_accessed=2**23, transcendentals=0),
        name="deeper",
    )(keys, values, two)

    first_in = swapped(first, "seq", 1)
    second_in = across(second)
    four_in = swapped(four, "seq", 4)
    six_in = swapped(four, "seq", 6)
    threes_in = [swapped(three, "seq", mask) for mask in (3, 2)]
    edge_q, two_q, three_q, four_q, state = pl.pallas_call(
        local_kernel,
        out_shape=[
            bf16(2, BLOCK, features),
            bf16(rows // 4, features),
            bf16(rows // 8, features),
            bf16(rows // 16, features),
            jax.ShapeDtypeStruct((3, rows, features), jnp.float32),
        ],
        scratch_shapes=[
            pltpu.VMEM((pairs, rows, PAIR), jnp.float32),
            pltpu.VMEM((pairs, rows // BLOCK, 2 * BLOCK, 3 * BLOCK), jnp.float32),
            pltpu.VMEM((pairs, rows // BLOCK // 2, 2 * BLOCK, BLOCK), jnp.float32),
        ],
        compiler_params=params,
        name="local",
    )(queries[0], keys, values, one, four_in)

    fours = pl.pallas_call(
        join_kernel,
        out_shape=bf16(2, rows // 8, features),
        compiler_params=params,
        cost_estimate=pl.CostEstimate(flops=2**29, bytes_accessed=2**20, transcendentals=0),
        name="join",
    )(four_in, six_in, four_q)
    fours_in = swapped(fours, "seq", 1)
    coarse, near = pl.pallas_call(
        coarse_kernel,
        out_shape=[
            jax.ShapeDtypeStruct((3, rows // 4, features), jnp.float32),
            bf16(2, rows // 16, features),
        ],
        scratch_shapes=[
            pltpu.VMEM((2, pairs, BLOCK, PAIR), jnp.float32),
            pltpu.VMEM((2, rows // 4, features), jnp.bfloat16),
            pltpu.VMEM((pairs, rows // 2, BLOCK), jnp.float32),
            pltpu.VMEM((pairs, rows // 4, BLOCK), jnp.float32),
        ],
        compiler_params=params,
        cost_estimate=pl.CostEstimate(flops=2**31, bytes_accessed=2**21, transcendentals=0),
        name="coarse",
    )(two_q, three_q, first_in, *threes_in)
    away = range(AHEAD, head_count)
    fine, *early = pl.pallas_call(
        mid_kernel,
        out_shape=[jax.ShapeDtypeStruct((2, rows, features), jnp.float32)]
        + [bf16(BLOCK, features) for _ in away],
        scratch_shapes=[
            pltpu.VMEM((rows // BLOCK, BLOCK, features), jnp.bfloat16),
            pltpu.VMEM((pairs, 2, 2 * BLOCK, BLOCK), jnp.float32),
        ],
        compiler_params=params,
        name="mid",
    )(edge_q, coarse, state, first_in, second_in)
    early_in = [swapped(part, "head", step) for step, part in zip(away, early)]

    far = []
    known = 8
    if known < seq_count:
        group = [four, near] + [repool_outside(field) for field in threes_in]
        group = jnp.concatenate(group + [fours, fours_in], axis=1)
        while known < seq_count:
            fresh = swapped(group, "seq", known)
            far.append(fresh)
            group = jnp.concatenate([group, fresh], axis=1)
            known *= 2

    parts = [bf16(BLOCK, features) for _ in range(AHEAD)]
    *outs, level_four = pl.pallas_call(
        finish_kernel,
        out_shape=parts[2:] + [jax.ShapeDtypeStruct((2, rows // 16, features), jnp.float32)],
        scratch_shapes=[pltpu.VMEM((pairs, rows // 8, rows // 16 * seq_count), jnp.float32)],
        compiler_params=params,
        name="finish",
    )(four_q, fine, four, near, *threes_in, fours, fours_in, *far)
    whole_in = [swapped(part, "head", step) for step, part in enumerate(outs, 2)]
    own_part, next_part, *late = pl.pallas_call(
        rest_kernel,
        out_shape=parts[:2] + [bf16(2 * SLAB, features) for _ in away],
        compiler_params=params,
        name="rest",
    )(fine, level_four)
    next_in = swapped(next_part, "head", 1)
    late_in = [swapped(part, "head", step) for step, part in zip(away, late)]
    width = out_weight.shape[1]
    partial = pl.pallas_call(
        partial_kernel,
        out_shape=jax.ShapeDtypeStruct((BLOCK, width), jnp.float32),
        compiler_params=params,
        name="partial",
    )(own_part, out_weight)
    heavy = pl.CostEstimate(flops=2**32, bytes_accessed=2**20, transcendentals=0)
    widened = pl.pallas_call(
        widen_kernel,
        out_shape=[jax.ShapeDtypeStruct((BLOCK, features), jnp.float32) for _ in away],
        compiler_params=params,
        cost_estimate=pl.CostEstimate(flops=2**28, bytes_accessed=2**18, transcendentals=0),
        name="widen",
    )(*early_in)
    widened = pl.pallas_call(
        carry_kernel,
        out_shape=[jax.ShapeDtypeStruct((BLOCK, features), jnp.float32) for _ in away],
        compiler_params=params,
        name="carry",
    )(whole_in[0], *widened)
    rejoined = pl.pallas_call(
        rejoin_kernel,
        out_shape=[bf16(BLOCK, features) for _ in away],
        compiler_params=params,
        cost_estimate=heavy,
        name="rejoin",
    )(*widened, *late_in)
    chunk = 2 * PAIR
    result = pl.pallas_call(
        project_kernel,
        in_specs=[vmem] * (head_count + 1),
        out_specs=hbm,
        out_shape=bf16(BLOCK, width),
        scratch_shapes=[
            pltpu.VMEM((width // chunk, 2, BLOCK, PAIR), jnp.float32),
            pltpu.VMEM((width // chunk, BLOCK, chunk), jnp.bfloat16),
            pltpu.SemaphoreType.DMA((width // chunk,)),
        ],
        compiler_params=params,
        name="project",
    )(partial, *whole_in, *rejoined, next_in, out_weight)
    return result[None]


def solution(mesh):
    return jax.shard_map(
        per_device,
        mesh=mesh,
        in_specs=(P(None, "seq", "head"), P(None, "seq", "head"), P(None, "seq", "head"), P()),
        out_specs=P(None, ("seq", "head"), None),
        check_vma=False,
    )
```

profile of v0, /device:TPU:0, one launch (start us, length us, event | category | flops | bytes accessed | tf_op | source)
XLA Modules:
  0.0 24.2 jit_solution(9261113307878807252)
XLA Ops:
  0.0 1.4 %pool.1 = (bf16[512,256]{1,0:T(8,128)(2,1)S(1)}, bf16[512,256]{1,0:T(8,128)(2,1)S(1)}, bf16[2,224,256]{2,1,0:T(8,128)(2,1)S(1)}, bf16[2,256,256]{2,1,0:T(8,128)(2,1)S(1)}, bf16[2,128,256]{2,1,0:T(8,128)(2,1)S(1)}) custom-call(bf16[1,512,256]{2,1,0:T(8,128)(2,1)} %k_hbm.1, bf16[1,512,256]{2,1,0:T(8,128)(2,1)} %v_hbm.1), custom_call_target="tpu_custom_call" | custom-call | tf_op jit(solution)/shard_map/pool/pallas_call | solution.py:469
  1.4 3.0 %collective-permute-start.1 = (bf16[2,224,256]{2,1,0:T(8,128)(2,1)S(1)}, bf16[2,224,256]{2,1,0:T(8,128)(2,1)S(1)}, u32[]{:S(2)}, u32[]{:S(2)}) collective-permute-start(bf16[2,224,256]{2,1,0:T(8,128)(2,1)S(1)} %get-tuple-element.35), channel_id=1, source_target_pairs={{0,4},{4,0},{8,12},{12,8},{16,20},{20,16},{24,28},{28,24},{1,5},{5... | collective-permute-start | bytes 688136 | tf_op jit(solution)/shard_map/ppermute | solution.py:443
  4.4 0.0 copy-start.1
  4.5 2.7 %collective-permute-start = (bf16[2,32,256]{2,1,0:T(8,128)(2,1)S(1)}, bf16[2,32,256]{2,1,0:T(8,128)(2,1)S(1)}, u32[]{:S(2)}, u32[]{:S(2)}) collective-permute-start(bf16[2,32,256]{2,1,0:T(8,128)(2,1)S(1)} %get-tuple-element.31.four_ref), channel_id=1, source_target_pairs={{0,16},{4,20},{8,24},{12,28},{16,0},{20,4},{24,8},{28,12},{1,17},{... | collective-permute-start | bytes 98312 | tf_op jit(solution)/shard_map/ppermute | solution.py:443
  7.1 1.3 %collective-permute-start.5 = (bf16[2,32,256]{2,1,0:T(8,128)(2,1)S(1)}, bf16[2,32,256]{2,1,0:T(8,128)(2,1)S(1)}, u32[]{:S(2)}, u32[]{:S(2)}) collective-permute-start(bf16[2,32,256]{2,1,0:T(8,128)(2,1)S(1)} %get-tuple-element.31.four_ref), channel_id=1, source_target_pairs={{0,24},{4,28},{8,16},{12,20},{16,8},{20,12},{24,0},{28,4},{1,25},{... | collective-permute-start | bytes 98312 | tf_op jit(solution)/shard_map/ppermute | solution.py:443
  8.5 0.2 collective-permute-start.2
  8.7 1.8 %collective-permute-start.3 = (bf16[2,64,256]{2,1,0:T(8,128)(2,1)S(1)}, bf16[2,64,256]{2,1,0:T(8,128)(2,1)S(1)}, u32[]{:S(2)}, u32[]{:S(2)}) collective-permute-start(bf16[2,64,256]{2,1,0:T(8,128)(2,1)S(1)} %get-tuple-element.36), channel_id=1, source_target_pairs={{0,8},{4,12},{8,0},{12,4},{16,24},{20,28},{24,16},{28,20},{1,9},{5... | collective-permute-start | bytes 196616 | tf_op jit(solution)/shard_map/ppermute | solution.py:443
  10.5 0.0 collective-permute-done.four_ref
  10.5 0.0 collective-permute-start.4
  10.5 0.0 copy-done.1
  10.5 1.5 %local.1 = (bf16[2,128,256]{2,1,0:T(8,128)(2,1)S(1)}, bf16[128,256]{1,0:T(8,128)(2,1)S(1)}, bf16[64,256]{1,0:T(8,128)(2,1)S(1)}, bf16[32,256]{1,0:T(8,128)(2,1)S(1)}, f32[3,512,256]{2,1,0:T(8,128)S(1)}) custom-call(bf16[512,256]{1,0:T(8,128)(2,1)S(1)} %bitcast.2, bf16[512,256]{1,0:T(8,128)(2,1)S(1)} %get-tuple-element.27.k_ref, ...), custom_call_target="tpu_custom_call" | custom-call | tf_op jit(solution)/shard_map/local/pallas_call | solution.py:503
  12.0 1.2 %collective-permute-done.5.six_ref = bf16[2,32,256]{2,1,0:T(8,128)(2,1)S(1)} collective-permute-done((bf16[2,32,256]{2,1,0:T(8,128)(2,1)S(1)}, bf16[2,32,256]{2,1,0:T(8,128)(2,1)S(1)}, u32[]{:S(2)}, u32[]{:S(2)}) %collective-permute-start.5) | collective-permute-done | bytes 32800 | tf_op jit(solution)/shard_map/ppermute | solution.py:443
  13.2 0.9 %collective-permute-start.6 = (bf16[2,64,256]{2,1,0:T(8,128)(2,1)S(1)}, bf16[2,64,256]{2,1,0:T(8,128)(2,1)S(1)}, u32[]{:S(2)}, u32[]{:S(2)}) collective-permute-start(bf16[2,64,256]{2,1,0:T(8,128)(2,1)S(1)} %join.1.fours_a), channel_id=1, source_target_pairs={{0,4},{4,0},{8,12},{12,8},{16,20},{20,16},{24,28},{28,24},{1,5},{5... | collective-permute-start | bytes 196616 | tf_op jit(solution)/shard_map/ppermute | solution.py:443
  14.2 0.0 collective-permute-done.2.three_a
  14.2 0.6 %collective-permute-done.3.three_b = bf16[2,64,256]{2,1,0:T(8,128)(2,1)S(1)} collective-permute-done((bf16[2,64,256]{2,1,0:T(8,128)(2,1)S(1)}, bf16[2,64,256]{2,1,0:T(8,128)(2,1)S(1)}, u32[]{:S(2)}, u32[]{:S(2)}) %collective-permute-start.3) | collective-permute-done | bytes 65568 | tf_op jit(solution)/shard_map/ppermute | solution.py:443
  14.8 0.0 collective-permute-done.1.first_ref
  14.8 0.5 %coarse.1 = (f32[3,128,256]{2,1,0:T(8,128)S(1)}, bf16[2,32,256]{2,1,0:T(8,128)(2,1)S(1)}) custom-call(bf16[128,256]{1,0:T(8,128)(2,1)S(1)} %get-tuple-element.33.two_q, bf16[64,256]{1,0:T(8,128)(2,1)S(1)} %get-tuple-element.34.three_q, bf16[2,224,256]{2,1,0:T(8,128)(2,1)S(1)} %collective-permute-done.1.first_ref, ...), custom_call_target="tpu_custom_call" | custom-call | flops 2147483648 | bytes 2097152 | tf_op jit(solution)/shard_map/coarse/pallas_call | solution.py:529
  15.3 0.0 collective-permute-done.4.second_ref
  15.3 0.0 copy-start
  15.3 0.9 %mid.1 = (f32[2,512,256]{2,1,0:T(8,128)S(1)}, bf16[128,256]{1,0:T(8,128)(2,1)S(1)}) custom-call(bf16[2,128,256]{2,1,0:T(8,128)(2,1)S(1)} %get-tuple-element.32.edge_q, f32[3,128,256]{2,1,0:T(8,128)S(1)} %get-tuple-element.37.coarse, f32[3,512,256]{2,1,0:T(8,128)S(1)} %get-tuple-element.38.state, bf16[2,224,256]{2,1,0:T(8,128)(2,1)S(1)} %collective-permute-done.1.first_ref, ...), custom_call_target="tpu_custom_call" | custom-call | tf_op jit(solution)/shard_map/mid/pallas_call | solution.py:546
  16.2 0.1 collective-permute-start.8
  16.3 1.2 %collective-permute-done.6.fours_b = bf16[2,64,256]{2,1,0:T(8,128)(2,1)S(1)} collective-permute-done((bf16[2,64,256]{2,1,0:T(8,128)(2,1)S(1)}, bf16[2,64,256]{2,1,0:T(8,128)(2,1)S(1)}, u32[]{:S(2)}, u32[]{:S(2)}) %collective-permute-start.6) | collective-permute-done | bytes 65568 | tf_op jit(solution)/shard_map/ppermute | solution.py:443
  17.5 0.4 %finish.1 = (bf16[128,256]{1,0:T(8,128)(2,1)S(1)}, f32[2,32,256]{2,1,0:T(8,128)S(1)}) custom-call(bf16[32,256]{1,0:T(8,128)(2,1)S(1)} %get-tuple-element.41.query_ref.four_q, f32[2,512,256]{2,1,0:T(8,128)S(1)} %get-tuple-element.40.fine, bf16[2,32,256]{2,1,0:T(8,128)(2,1)S(1)} %get-tuple-element.31.four_ref, ...), custom_call_target="tpu_custom_call" | custom-call | tf_op jit(solution)/shard_map/finish/pallas_call | solution.py:571
  17.9 1.6 %collective-permute-start.7 = (bf16[128,256]{1,0:T(8,128)(2,1)S(1)}, bf16[128,256]{1,0:T(8,128)(2,1)S(1)}, u32[]{:S(2)}, u32[]{:S(2)}) collective-permute-start(bf16[128,256]{1,0:T(8,128)(2,1)S(1)} %get-tuple-element.45), channel_id=1, source_target_pairs={{0,2},{1,3},{2,0},{3,1},{4,6},{5,7},{6,4},{7,5},{8,10},{9,11},{10,... | collective-permute-start | bytes 196616 | tf_op jit(solution)/shard_map/ppermute | solution.py:443
  19.5 0.3 %rest.1 = (bf16[128,256]{1,0:T(8,128)(2,1)S(1)}, bf16[128,256]{1,0:T(8,128)(2,1)S(1)}, bf16[16,256]{1,0:T(8,128)(2,1)S(1)}) custom-call(f32[2,512,256]{2,1,0:T(8,128)S(1)} %get-tuple-element.40.fine, f32[2,32,256]{2,1,0:T(8,128)S(1)} %get-tuple-element.43.coarse), custom_call_target="tpu_custom_call" | custom-call | tf_op jit(solution)/shard_map/rest/pallas_call | solution.py:579
  19.7 0.3 %collective-permute-start.9 = (bf16[16,256]{1,0:T(8,128)(2,1)S(1)}, bf16[16,256]{1,0:T(8,128)(2,1)S(1)}, u32[]{:S(2)}, u32[]{:S(2)}) collective-permute-start(bf16[16,256]{1,0:T(8,128)(2,1)S(1)} %get-tuple-element.47), channel_id=1, source_target_pairs={{0,3},{1,2},{2,1},{3,0},{4,7},{5,6},{6,5},{7,4},{8,11},{9,10},{10,... | collective-permute-start | bytes 24584 | tf_op jit(solution)/shard_map/ppermute | solution.py:443
  20.0 0.3 %collective-permute-start.10 = (bf16[128,256]{1,0:T(8,128)(2,1)S(1)}, bf16[128,256]{1,0:T(8,128)(2,1)S(1)}, u32[]{:S(2)}, u32[]{:S(2)}) collective-permute-start(bf16[128,256]{1,0:T(8,128)(2,1)S(1)} %get-tuple-element.48), channel_id=1, source_target_pairs={{0,1},{1,0},{2,3},{3,2},{4,5},{5,4},{6,7},{7,6},{8,9},{9,8},{10,11... | collective-permute-start | bytes 196616 | tf_op jit(solution)/shard_map/ppermute | solution.py:443
  20.4 0.0 copy-done
  20.4 0.2 partial.1.partial_ref
  20.6 0.0 collective-permute-done.8.refs_0_
  20.7 1.8 %collective-permute-done.7.whole_ref.refs_0_ = bf16[128,256]{1,0:T(8,128)(2,1)S(1)} collective-permute-done((bf16[128,256]{1,0:T(8,128)(2,1)S(1)}, bf16[128,256]{1,0:T(8,128)(2,1)S(1)}, u32[]{:S(2)}, u32[]{:S(2)}) %collective-permute-start.7) | collective-permute-done | bytes 65568 | tf_op jit(solution)/shard_map/ppermute | solution.py:443
  22.4 0.4 %collective-permute-done.9.refs_1_ = bf16[16,256]{1,0:T(8,128)(2,1)S(1)} collective-permute-done((bf16[16,256]{1,0:T(8,128)(2,1)S(1)}, bf16[16,256]{1,0:T(8,128)(2,1)S(1)}, u32[]{:S(2)}, u32[]{:S(2)}) %collective-permute-start.9) | collective-permute-done | bytes 8224 | tf_op jit(solution)/shard_map/ppermute | solution.py:443
  22.8 0.2 rejoin.1.refs_1_
  23.0 0.0 collective-permute-done.10.refs_2_
  23.1 1.1 %project.1 = bf16[128,1024]{1,0:T(8,128)(2,1)} custom-call(f32[128,1024]{1,0:T(8,128)S(1)} %partial.1.partial_ref, bf16[128,256]{1,0:T(8,128)(2,1)S(1)} %collective-permute-done.7.whole_ref.refs_0_, bf16[128,256]{1,0:T(8,128)(2,1)S(1)} %rejoin.1.refs_1_, bf16[128,256]{1,0:T(8,128)(2,1)S(1)} %collective-permute-done.10.refs_2_, bf16[1024,1024]{1,0:T(8,128)(2,1)S(1)} %copy-done), custom_call_target="tpu_custom_call" | custom-call | tf_op jit(solution)/shard_map/project/pallas_call | solution.py:616
  (4 shorter events, 0.1 us)
Async XLA Ops:
  1.4 13.4 %collective-permute-start.1 = (bf16[2,224,256]{2,1,0:T(8,128)(2,1)S(1)}, bf16[2,224,256]{2,1,0:T(8,128)(2,1)S(1)}, u32[]{:S(2)}, u32[]{:S(2)}) collective-permute-start(bf16[2,224,256]{2,1,0:T(8,128)(2,1)S(1)} %get-tuple-element.35), channel_id=1, source_target_pairs={{0,4},{4,0},{8,12},{12,8},{16,20},{20,16},{24,28},{28,24},{1,5},{5... | collective-permute-start | bytes 688136 | tf_op jit(solution)/shard_map/ppermute | solution.py:443
  4.4 6.0 %copy-start.1 = (bf16[1,512,256]{2,1,0:T(8,128)(2,1)S(1)}, bf16[1,512,256]{2,1,0:T(8,128)(2,1)}, u32[]{:S(2)}) copy-start(bf16[1,512,256]{2,1,0:T(8,128)(2,1)} %param.4) | copy-start | bytes 786436
  4.5 6.0 %collective-permute-start = (bf16[2,32,256]{2,1,0:T(8,128)(2,1)S(1)}, bf16[2,32,256]{2,1,0:T(8,128)(2,1)S(1)}, u32[]{:S(2)}, u32[]{:S(2)}) collective-permute-start(bf16[2,32,256]{2,1,0:T(8,128)(2,1)S(1)} %get-tuple-element.31.four_ref), channel_id=1, source_target_pairs={{0,16},{4,20},{8,24},{12,28},{16,0},{20,4},{24,8},{28,12},{1,17},{... | collective-permute-start | bytes 98312 | tf_op jit(solution)/shard_map/ppermute | solution.py:443
  7.1 6.1 %collective-permute-start.5 = (bf16[2,32,256]{2,1,0:T(8,128)(2,1)S(1)}, bf16[2,32,256]{2,1,0:T(8,128)(2,1)S(1)}, u32[]{:S(2)}, u32[]{:S(2)}) collective-permute-start(bf16[2,32,256]{2,1,0:T(8,128)(2,1)S(1)} %get-tuple-element.31.four_ref), channel_id=1, source_target_pairs={{0,24},{4,28},{8,16},{12,20},{16,8},{20,12},{24,0},{28,4},{1,25},{... | collective-permute-start | bytes 98312 | tf_op jit(solution)/shard_map/ppermute | solution.py:443
  8.5 5.7 %collective-permute-start.2 = (bf16[2,64,256]{2,1,0:T(8,128)(2,1)S(1)}, bf16[2,64,256]{2,1,0:T(8,128)(2,1)S(1)}, u32[]{:S(2)}, u32[]{:S(2)}) collective-permute-start(bf16[2,64,256]{2,1,0:T(8,128)(2,1)S(1)} %get-tuple-element.36), channel_id=1, source_target_pairs={{0,12},{4,8},{8,4},{12,0},{16,28},{20,24},{24,20},{28,16},{1,13},{... | collective-permute-start | bytes 196616 | tf_op jit(solution)/shard_map/ppermute | solution.py:443
  8.7 6.1 %collective-permute-start.3 = (bf16[2,64,256]{2,1,0:T(8,128)(2,1)S(1)}, bf16[2,64,256]{2,1,0:T(8,128)(2,1)S(1)}, u32[]{:S(2)}, u32[]{:S(2)}) collective-permute-start(bf16[2,64,256]{2,1,0:T(8,128)(2,1)S(1)} %get-tuple-element.36), channel_id=1, source_target_pairs={{0,8},{4,12},{8,0},{12,4},{16,24},{20,28},{24,16},{28,20},{1,9},{5... | collective-permute-start | bytes 196616 | tf_op jit(solution)/shard_map/ppermute | solution.py:443
  10.5 4.8 %collective-permute-start.4 = (bf16[2,128,256]{2,1,0:T(8,128)(2,1)S(1)}, bf16[2,128,256]{2,1,0:T(8,128)(2,1)S(1)}, u32[]{:S(2)}, u32[]{:S(2)}) collective-permute-start(bf16[2,128,256]{2,1,0:T(8,128)(2,1)S(1)} %get-tuple-element.39), channel_id=1, source_target_pairs={{0,1},{1,0},{2,3},{3,2},{4,8},{5,9},{6,10},{7,11},{8,4},{9,5},{10,... | collective-permute-start | bytes 393224 | tf_op jit(solution)/shard_map/ppermute | solution.py:454
  13.2 4.3 %collective-permute-start.6 = (bf16[2,64,256]{2,1,0:T(8,128)(2,1)S(1)}, bf16[2,64,256]{2,1,0:T(8,128)(2,1)S(1)}, u32[]{:S(2)}, u32[]{:S(2)}) collective-permute-start(bf16[2,64,256]{2,1,0:T(8,128)(2,1)S(1)} %join.1.fours_a), channel_id=1, source_target_pairs={{0,4},{4,0},{8,12},{12,8},{16,20},{20,16},{24,28},{28,24},{1,5},{5... | collective-permute-start | bytes 196616 | tf_op jit(solution)/shard_map/ppermute | solution.py:443
  15.3 5.1 %copy-start = (bf16[1024,1024]{1,0:T(8,128)(2,1)S(1)}, bf16[1024,1024]{1,0:T(8,128)(2,1)}, u32[]{:S(2)}) copy-start(bf16[1024,1024]{1,0:T(8,128)(2,1)} %refs_3_.1) | copy-start | bytes 6291460
  16.2 4.4 %collective-permute-start.8 = (bf16[128,256]{1,0:T(8,128)(2,1)S(1)}, bf16[128,256]{1,0:T(8,128)(2,1)S(1)}, u32[]{:S(2)}, u32[]{:S(2)}) collective-permute-start(bf16[128,256]{1,0:T(8,128)(2,1)S(1)} %get-tuple-element.46), channel_id=1, source_target_pairs={{0,3},{1,2},{2,1},{3,0},{4,7},{5,6},{6,5},{7,4},{8,11},{9,10},{10,... | collective-permute-start | bytes 196616 | tf_op jit(solution)/shard_map/ppermute | solution.py:443
  17.9 4.5 %collective-permute-start.7 = (bf16[128,256]{1,0:T(8,128)(2,1)S(1)}, bf16[128,256]{1,0:T(8,128)(2,1)S(1)}, u32[]{:S(2)}, u32[]{:S(2)}) collective-permute-start(bf16[128,256]{1,0:T(8,128)(2,1)S(1)} %get-tuple-element.45), channel_id=1, source_target_pairs={{0,2},{1,3},{2,0},{3,1},{4,6},{5,7},{6,4},{7,5},{8,10},{9,11},{10,... | collective-permute-start | bytes 196616 | tf_op jit(solution)/shard_map/ppermute | solution.py:443
  19.7 3.1 %collective-permute-start.9 = (bf16[16,256]{1,0:T(8,128)(2,1)S(1)}, bf16[16,256]{1,0:T(8,128)(2,1)S(1)}, u32[]{:S(2)}, u32[]{:S(2)}) collective-permute-start(bf16[16,256]{1,0:T(8,128)(2,1)S(1)} %get-tuple-element.47), channel_id=1, source_target_pairs={{0,3},{1,2},{2,1},{3,0},{4,7},{5,6},{6,5},{7,4},{8,11},{9,10},{10,... | collective-permute-start | bytes 24584 | tf_op jit(solution)/shard_map/ppermute | solution.py:443
  20.0 3.0 %collective-permute-start.10 = (bf16[128,256]{1,0:T(8,128)(2,1)S(1)}, bf16[128,256]{1,0:T(8,128)(2,1)S(1)}, u32[]{:S(2)}, u32[]{:S(2)}) collective-permute-start(bf16[128,256]{1,0:T(8,128)(2,1)S(1)} %get-tuple-element.48), channel_id=1, source_target_pairs={{0,1},{1,0},{2,3},{3,2},{4,5},{5,4},{6,7},{7,6},{8,9},{9,8},{10,11... | collective-permute-start | bytes 196616 | tf_op jit(solution)/shard_map/ppermute | solution.py:443
where the time goes:
time: 24.3 us; the launch traced here: 24.2 us
  starting transfers between devices  12.2 us (50%)
  Pallas kernels  6.7 us (28%)
  waiting for transfers between devices  5.12 us (21%)
    ppermute x10, starting transfers between devices, swapped(): lax.ppermute(block, axis, [(i, i ^ mask) for i in range(lax.axis_size(axi...  12.2 us
    ppermute x10, waiting for transfers between devices, swapped(): lax.ppermute(block, axis, [(i, i ^ mask) for i in range(lax.axis_size(axi...  5.12 us
    pallas_call x1, Pallas kernels, per_device(): pl.pallas_call(local_kernel, out_shape=[bf16(2, BLOCK, features), bf16(ro...  1.54 us
    pallas_call x1, Pallas kernels, per_device(): pl.pallas_call(pool_kernel, in_specs=[hbm] * 2, out_shape=[bf16(rows, fea...  1.39 us
    pallas_call x1, Pallas kernels, per_device(): pl.pallas_call(project_kernel, in_specs=[vmem] * (head_count + 1), out_sp...  1.13 us
    pallas_call x1, Pallas kernels, per_device(): pl.pallas_call(mid_kernel, out_shape=[jax.ShapeDtypeStruct((2, rows, feat...  0.93 us
    pallas_call x1, Pallas kernels, per_device(): pl.pallas_call(coarse_kernel, out_shape=[jax.ShapeDtypeStruct((3, rows //...  0.5 us
  transfers between devices with their start and end apart: 11, of which 5 were waited for; matrix products, arithmetic and copies ran while one was open for 0% of the time, Pallas kernels for 17%

commit v1 on v0

--- a/solution.py
+++ b/solution.py
@@ -322,8 +322,8 @@
     four_q, fine, four_ref, near_ref, three_a, three_b, fours_a, fours_b, *refs
 ):
     refs, (coarse, four_hold) = refs[:-2], refs[-2:]
-    count = AHEAD - 2
-    far, outs = refs[:-count], refs[-count:]
+    steps_out = range(2, lax.axis_size("head"))
+    far, outs = refs[: -len(steps_out)], refs[-len(steps_out) :]
     pairs = four_q.shape[1] // PAIR
     steps = {}
     for pair in range(pairs):
@@ -354,12 +354,11 @@
         top, numer, rowsum = weigh(four_hold.at[pair], *steps[pair])
         coarse[0, :, lanes] = numer / rowsum
         coarse[1, :, lanes] = top + jnp.log(rowsum) * log2_e
-    finish_blocks(fine, coarse, zip(range(2, AHEAD), outs))
+    finish_blocks(fine, coarse, zip(steps_out, outs))
 
 
 def rest_kernel(fine, coarse, *outs):
-    steps = [0, 1, *range(AHEAD, lax.axis_size("head"))]
-    finish_blocks(fine, coarse, zip(steps, outs))
+    finish_blocks(fine, coarse, enumerate(outs))
 
 
 def rejoin_kernel(*refs):
@@ -570,20 +569,22 @@
     parts = [bf16(BLOCK, features) for _ in range(AHEAD)]
     *outs, level_four = pl.pallas_call(
         finish_kernel,
-        out_shape=parts[2:] + [jax.ShapeDtypeStruct((2, rows // 16, features), jnp.float32)],
+        out_shape=parts[2:]
+        + [bf16(2 * SLAB, features) for _ in away]
+        + [jax.ShapeDtypeStruct((2, rows // 16, features), jnp.float32)],
         scratch_shapes=[pltpu.VMEM((pairs, rows // 8, rows // 16 * seq_count), jnp.float32)],
         compiler_params=params,
         name="finish",
     )(four_q, fine, four, near, *threes_in, fours, fours_in, *far)
-    whole_in = [swapped(part, "head", step) for step, part in enumerate(outs, 2)]
-    own_part, next_part, *late = pl.pallas_call(
+    whole_in = [swapped(part, "head", step) for step, part in zip(range(2, AHEAD), outs)]
+    late_in = [swapped(part, "head", step) for step, part in zip(away, outs[AHEAD - 2 :])]
+    own_part, next_part = pl.pallas_call(
         rest_kernel,
-        out_shape=parts[:2] + [bf16(2 * SLAB, features) for _ in away],
+        out_shape=parts[:2],
         compiler_params=params,
         name="rest",
     )(fine, level_four)
     next_in = swapped(next_part, "head", 1)
-    late_in = [swapped(part, "head", step) for step, part in zip(away, late)]
     width = out_weight.shape[1]
     partial = pl.pallas_call(
         partial_kernel,
@@ -596,7 +597,7 @@
         widen_kernel,
         out_shape=[jax.ShapeDtypeStruct((BLOCK, features), jnp.float32) for _ in away],
         compiler_params=params,
-        cost_estimate=pl.CostEstimate(flops=2**28, bytes_accessed=2**18, transcendentals=0),
+        cost_estimate=pl.CostEstimate(flops=2**22, bytes_accessed=2**10, transcendentals=0),
         name="widen",
     )(*early_in)
     widened = pl.pallas_call(

time: 24.3 us -> 24.2 us (level)
  no operation moved by 1% of the time
where the time goes in v1:
time: 24.2 us; the launch traced here: 24.1 us
  starting transfers between devices  12.2 us (50%)
  Pallas kernels  6.69 us (28%)
  waiting for transfers between devices  5.02 us (21%)
    ppermute x10, starting transfers between devices, swapped(): lax.ppermute(block, axis, [(i, i ^ mask) for i in range(lax.axis_size(axi...  12.2 us
    ppermute x10, waiting for transfers between devices, swapped(): lax.ppermute(block, axis, [(i, i ^ mask) for i in range(lax.axis_size(axi...  5.02 us
    pallas_call x1, Pallas kernels, per_device(): pl.pallas_call(local_kernel, out_shape=[bf16(2, BLOCK, features), bf16(ro...  1.54 us
    pallas_call x1, Pallas kernels, per_device(): pl.pallas_call(pool_kernel, in_specs=[hbm] * 2, out_shape=[bf16(rows, fea...  1.39 us
    pallas_call x1, Pallas kernels, per_device(): pl.pallas_call(project_kernel, in_specs=[vmem] * (head_count + 1), out_sp...  1.12 us
    pallas_call x1, Pallas kernels, per_device(): pl.pallas_call(mid_kernel, out_shape=[jax.ShapeDtypeStruct((2, rows, feat...  0.93 us
    pallas_call x1, Pallas kernels, per_device(): pl.pallas_call(finish_kernel, out_shape=parts[2:] + [bf16(2 * SLAB, featu...  0.61 us
    pallas_call x1, Pallas kernels, per_device(): pl.pallas_call(coarse_kernel, out_shape=[jax.ShapeDtypeStruct((3, rows //...  0.5 us
  transfers between devices with their start and end apart: 11, of which 5 were waited for; matrix products, arithmetic and copies ran while one was open for 0% of the time, Pallas kernels for 17%

profile of v1, /device:TPU:0, one launch (start us, length us, event | category | flops | bytes accessed | tf_op | source)
XLA Modules:
  0.0 24.1 jit_solution(10091216942729208119)
XLA Ops:
  0.0 1.4 %pool.1 = (bf16[512,256]{1,0:T(8,128)(2,1)S(1)}, bf16[512,256]{1,0:T(8,128)(2,1)S(1)}, bf16[2,224,256]{2,1,0:T(8,128)(2,1)S(1)}, bf16[2,256,256]{2,1,0:T(8,128)(2,1)S(1)}, bf16[2,128,256]{2,1,0:T(8,128)(2,1)S(1)}) custom-call(bf16[1,512,256]{2,1,0:T(8,128)(2,1)} %k_hbm.1, bf16[1,512,256]{2,1,0:T(8,128)(2,1)} %v_hbm.1), custom_call_target="tpu_custom_call" | custom-call | tf_op jit(solution)/shard_map/pool/pallas_call | solution.py:468
  1.4 3.0 %collective-permute-start.1 = (bf16[2,224,256]{2,1,0:T(8,128)(2,1)S(1)}, bf16[2,224,256]{2,1,0:T(8,128)(2,1)S(1)}, u32[]{:S(2)}, u32[]{:S(2)}) collective-permute-start(bf16[2,224,256]{2,1,0:T(8,128)(2,1)S(1)} %get-tuple-element.35), channel_id=1, source_target_pairs={{0,4},{4,0},{8,12},{12,8},{16,20},{20,16},{24,28},{28,24},{1,5},{5... | collective-permute-start | bytes 688136 | tf_op jit(solution)/shard_map/ppermute | solution.py:442
  4.4 0.0 copy-start.1
  4.5 2.7 %collective-permute-start = (bf16[2,32,256]{2,1,0:T(8,128)(2,1)S(1)}, bf16[2,32,256]{2,1,0:T(8,128)(2,1)S(1)}, u32[]{:S(2)}, u32[]{:S(2)}) collective-permute-start(bf16[2,32,256]{2,1,0:T(8,128)(2,1)S(1)} %get-tuple-element.31.four_ref), channel_id=1, source_target_pairs={{0,16},{4,20},{8,24},{12,28},{16,0},{20,4},{24,8},{28,12},{1,17},{... | collective-permute-start | bytes 98312 | tf_op jit(solution)/shard_map/ppermute | solution.py:442
  7.1 1.3 %collective-permute-start.5 = (bf16[2,32,256]{2,1,0:T(8,128)(2,1)S(1)}, bf16[2,32,256]{2,1,0:T(8,128)(2,1)S(1)}, u32[]{:S(2)}, u32[]{:S(2)}) collective-permute-start(bf16[2,32,256]{2,1,0:T(8,128)(2,1)S(1)} %get-tuple-element.31.four_ref), channel_id=1, source_target_pairs={{0,24},{4,28},{8,16},{12,20},{16,8},{20,12},{24,0},{28,4},{1,25},{... | collective-permute-start | bytes 98312 | tf_op jit(solution)/shard_map/ppermute | solution.py:442
  8.5 0.2 collective-permute-start.2
  8.7 1.8 %collective-permute-start.3 = (bf16[2,64,256]{2,1,0:T(8,128)(2,1)S(1)}, bf16[2,64,256]{2,1,0:T(8,128)(2,1)S(1)}, u32[]{:S(2)}, u32[]{:S(2)}) collective-permute-start(bf16[2,64,256]{2,1,0:T(8,128)(2,1)S(1)} %get-tuple-element.36), channel_id=1, source_target_pairs={{0,8},{4,12},{8,0},{12,4},{16,24},{20,28},{24,16},{28,20},{1,9},{5... | collective-permute-start | bytes 196616 | tf_op jit(solution)/shard_map/ppermute | solution.py:442
  10.5 0.0 collective-permute-done.four_ref
  10.5 0.0 collective-permute-start.4
  10.5 0.0 copy-done.1
  10.5 1.5 %local.1 = (bf16[2,128,256]{2,1,0:T(8,128)(2,1)S(1)}, bf16[128,256]{1,0:T(8,128)(2,1)S(1)}, bf16[64,256]{1,0:T(8,128)(2,1)S(1)}, bf16[32,256]{1,0:T(8,128)(2,1)S(1)}, f32[3,512,256]{2,1,0:T(8,128)S(1)}) custom-call(bf16[512,256]{1,0:T(8,128)(2,1)S(1)} %bitcast.2, bf16[512,256]{1,0:T(8,128)(2,1)S(1)} %get-tuple-element.27.k_ref, ...), custom_call_target="tpu_custom_call" | custom-call | tf_op jit(solution)/shard_map/local/pallas_call | solution.py:502
  12.0 1.2 %collective-permute-done.5.six_ref = bf16[2,32,256]{2,1,0:T(8,128)(2,1)S(1)} collective-permute-done((bf16[2,32,256]{2,1,0:T(8,128)(2,1)S(1)}, bf16[2,32,256]{2,1,0:T(8,128)(2,1)S(1)}, u32[]{:S(2)}, u32[]{:S(2)}) %collective-permute-start.5) | collective-permute-done | bytes 32800 | tf_op jit(solution)/shard_map/ppermute | solution.py:442
  13.2 0.9 %collective-permute-start.6 = (bf16[2,64,256]{2,1,0:T(8,128)(2,1)S(1)}, bf16[2,64,256]{2,1,0:T(8,128)(2,1)S(1)}, u32[]{:S(2)}, u32[]{:S(2)}) collective-permute-start(bf16[2,64,256]{2,1,0:T(8,128)(2,1)S(1)} %join.1.fours_a), channel_id=1, source_target_pairs={{0,4},{4,0},{8,12},{12,8},{16,20},{20,16},{24,28},{28,24},{1,5},{5... | collective-permute-start | bytes 196616 | tf_op jit(solution)/shard_map/ppermute | solution.py:442
  14.2 0.0 collective-permute-done.2.three_a
  14.2 0.6 %collective-permute-done.3.three_b = bf16[2,64,256]{2,1,0:T(8,128)(2,1)S(1)} collective-permute-done((bf16[2,64,256]{2,1,0:T(8,128)(2,1)S(1)}, bf16[2,64,256]{2,1,0:T(8,128)(2,1)S(1)}, u32[]{:S(2)}, u32[]{:S(2)}) %collective-permute-start.3) | collective-permute-done | bytes 65568 | tf_op jit(solution)/shard_map/ppermute | solution.py:442
  14.8 0.0 collective-permute-done.1.first_ref
  14.8 0.5 %coarse.1 = (f32[3,128,256]{2,1,0:T(8,128)S(1)}, bf16[2,32,256]{2,1,0:T(8,128)(2,1)S(1)}) custom-call(bf16[128,256]{1,0:T(8,128)(2,1)S(1)} %get-tuple-element.33.two_q, bf16[64,256]{1,0:T(8,128)(2,1)S(1)} %get-tuple-element.34.three_q, bf16[2,224,256]{2,1,0:T(8,128)(2,1)S(1)} %collective-permute-done.1.first_ref, ...), custom_call_target="tpu_custom_call" | custom-call | flops 2147483648 | bytes 2097152 | tf_op jit(solution)/shard_map/coarse/pallas_call | solution.py:528
  15.3 0.0 collective-permute-done.4.second_ref
  15.3 0.0 copy-start
  15.3 0.9 %mid.1 = (f32[2,512,256]{2,1,0:T(8,128)S(1)}, bf16[128,256]{1,0:T(8,128)(2,1)S(1)}) custom-call(bf16[2,128,256]{2,1,0:T(8,128)(2,1)S(1)} %get-tuple-element.32.edge_q, f32[3,128,256]{2,1,0:T(8,128)S(1)} %get-tuple-element.37.coarse, f32[3,512,256]{2,1,0:T(8,128)S(1)} %get-tuple-element.38.state, bf16[2,224,256]{2,1,0:T(8,128)(2,1)S(1)} %collective-permute-done.1.first_ref, ...), custom_call_target="tpu_custom_call" | custom-call | tf_op jit(solution)/shard_map/mid/pallas_call | solution.py:545
  16.2 0.1 collective-permute-start.8
  16.3 1.2 %collective-permute-done.6.fours_b = bf16[2,64,256]{2,1,0:T(8,128)(2,1)S(1)} collective-permute-done((bf16[2,64,256]{2,1,0:T(8,128)(2,1)S(1)}, bf16[2,64,256]{2,1,0:T(8,128)(2,1)S(1)}, u32[]{:S(2)}, u32[]{:S(2)}) %collective-permute-start.6) | collective-permute-done | bytes 65568 | tf_op jit(solution)/shard_map/ppermute | solution.py:442
  17.5 0.6 %finish.1 = (bf16[128,256]{1,0:T(8,128)(2,1)S(1)}, bf16[16,256]{1,0:T(8,128)(2,1)S(1)}, f32[2,32,256]{2,1,0:T(8,128)S(1)}) custom-call(bf16[32,256]{1,0:T(8,128)(2,1)S(1)} %get-tuple-element.41.query_ref.four_q, f32[2,512,256]{2,1,0:T(8,128)S(1)} %get-tuple-element.40.fine, bf16[2,32,256]{2,1,0:T(8,128)(2,1)S(1)} %get-tuple-element.31.four_ref, ...), custom_call_target="tpu_custom_call" | custom-call | tf_op jit(solution)/shard_map/finish/pallas_call | solution.py:570
  18.1 1.5 %collective-permute-start.7 = (bf16[128,256]{1,0:T(8,128)(2,1)S(1)}, bf16[128,256]{1,0:T(8,128)(2,1)S(1)}, u32[]{:S(2)}, u32[]{:S(2)}) collective-permute-start(bf16[128,256]{1,0:T(8,128)(2,1)S(1)} %get-tuple-element.45), channel_id=1, source_target_pairs={{0,2},{1,3},{2,0},{3,1},{4,6},{5,7},{6,4},{7,5},{8,10},{9,11},{10,... | collective-permute-start | bytes 196616 | tf_op jit(solution)/shard_map/ppermute | solution.py:442
  19.6 0.3 %collective-permute-start.9 = (bf16[16,256]{1,0:T(8,128)(2,1)S(1)}, bf16[16,256]{1,0:T(8,128)(2,1)S(1)}, u32[]{:S(2)}, u32[]{:S(2)}) collective-permute-start(bf16[16,256]{1,0:T(8,128)(2,1)S(1)} %get-tuple-element.47), channel_id=1, source_target_pairs={{0,3},{1,2},{2,1},{3,0},{4,7},{5,6},{6,5},{7,4},{8,11},{9,10},{10,... | collective-permute-start | bytes 24584 | tf_op jit(solution)/shard_map/ppermute | solution.py:442
  19.9 0.1 rest.1
  20.0 0.4 %collective-permute-start.10 = (bf16[128,256]{1,0:T(8,128)(2,1)S(1)}, bf16[128,256]{1,0:T(8,128)(2,1)S(1)}, u32[]{:S(2)}, u32[]{:S(2)}) collective-permute-start(bf16[128,256]{1,0:T(8,128)(2,1)S(1)} %get-tuple-element.48), channel_id=1, source_target_pairs={{0,1},{1,0},{2,3},{3,2},{4,5},{5,4},{6,7},{7,6},{8,9},{9,8},{10,11... | collective-permute-start | bytes 196616 | tf_op jit(solution)/shard_map/ppermute | solution.py:442
  20.4 0.0 copy-done
  20.4 0.2 partial.1.partial_ref
  20.6 0.0 collective-permute-done.8.refs_0_
  20.7 1.9 %collective-permute-done.7.whole_ref.refs_0_ = bf16[128,256]{1,0:T(8,128)(2,1)S(1)} collective-permute-done((bf16[128,256]{1,0:T(8,128)(2,1)S(1)}, bf16[128,256]{1,0:T(8,128)(2,1)S(1)}, u32[]{:S(2)}, u32[]{:S(2)}) %collective-permute-start.7) | collective-permute-done | bytes 65568 | tf_op jit(solution)/shard_map/ppermute | solution.py:442
  22.5 0.2 collective-permute-done.9.refs_1_
  22.7 0.2 rejoin.1.refs_1_
  22.9 0.0 collective-permute-done.10.refs_2_
  22.9 1.1 %project.1 = bf16[128,1024]{1,0:T(8,128)(2,1)} custom-call(f32[128,1024]{1,0:T(8,128)S(1)} %partial.1.partial_ref, bf16[128,256]{1,0:T(8,128)(2,1)S(1)} %collective-permute-done.7.whole_ref.refs_0_, bf16[128,256]{1,0:T(8,128)(2,1)S(1)} %rejoin.1.refs_1_, bf16[128,256]{1,0:T(8,128)(2,1)S(1)} %collective-permute-done.10.refs_2_, bf16[1024,1024]{1,0:T(8,128)(2,1)S(1)} %copy-done), custom_call_target="tpu_custom_call" | custom-call | tf_op jit(solution)/shard_map/project/pallas_call | solution.py:617
  (4 shorter events, 0.1 us)
Async XLA Ops:
  1.4 13.4 %collective-permute-start.1 = (bf16[2,224,256]{2,1,0:T(8,128)(2,1)S(1)}, bf16[2,224,256]{2,1,0:T(8,128)(2,1)S(1)}, u32[]{:S(2)}, u32[]{:S(2)}) collective-permute-start(bf16[2,224,256]{2,1,0:T(8,128)(2,1)S(1)} %get-tuple-element.35), channel_id=1, source_target_pairs={{0,4},{4,0},{8,12},{12,8},{16,20},{20,16},{24,28},{28,24},{1,5},{5... | collective-permute-start | bytes 688136 | tf_op jit(solution)/shard_map/ppermute | solution.py:442
  4.4 6.0 %copy-start.1 = (bf16[1,512,256]{2,1,0:T(8,128)(2,1)S(1)}, bf16[1,512,256]{2,1,0:T(8,128)(2,1)}, u32[]{:S(2)}) copy-start(bf16[1,512,256]{2,1,0:T(8,128)(2,1)} %param.4) | copy-start | bytes 786436
  4.5 6.0 %collective-permute-start = (bf16[2,32,256]{2,1,0:T(8,128)(2,1)S(1)}, bf16[2,32,256]{2,1,0:T(8,128)(2,1)S(1)}, u32[]{:S(2)}, u32[]{:S(2)}) collective-permute-start(bf16[2,32,256]{2,1,0:T(8,128)(2,1)S(1)} %get-tuple-element.31.four_ref), channel_id=1, source_target_pairs={{0,16},{4,20},{8,24},{12,28},{16,0},{20,4},{24,8},{28,12},{1,17},{... | collective-permute-start | bytes 98312 | tf_op jit(solution)/shard_map/ppermute | solution.py:442
  7.1 6.1 %collective-permute-start.5 = (bf16[2,32,256]{2,1,0:T(8,128)(2,1)S(1)}, bf16[2,32,256]{2,1,0:T(8,128)(2,1)S(1)}, u32[]{:S(2)}, u32[]{:S(2)}) collective-permute-start(bf16[2,32,256]{2,1,0:T(8,128)(2,1)S(1)} %get-tuple-element.31.four_ref), channel_id=1, source_target_pairs={{0,24},{4,28},{8,16},{12,20},{16,8},{20,12},{24,0},{28,4},{1,25},{... | collective-permute-start | bytes 98312 | tf_op jit(solution)/shard_map/ppermute | solution.py:442
  8.5 5.7 %collective-permute-start.2 = (bf16[2,64,256]{2,1,0:T(8,128)(2,1)S(1)}, bf16[2,64,256]{2,1,0:T(8,128)(2,1)S(1)}, u32[]{:S(2)}, u32[]{:S(2)}) collective-permute-start(bf16[2,64,256]{2,1,0:T(8,128)(2,1)S(1)} %get-tuple-element.36), channel_id=1, source_target_pairs={{0,12},{4,8},{8,4},{12,0},{16,28},{20,24},{24,20},{28,16},{1,13},{... | collective-permute-start | bytes 196616 | tf_op jit(solution)/shard_map/ppermute | solution.py:442
  8.7 6.1 %collective-permute-start.3 = (bf16[2,64,256]{2,1,0:T(8,128)(2,1)S(1)}, bf16[2,64,256]{2,1,0:T(8,128)(2,1)S(1)}, u32[]{:S(2)}, u32[]{:S(2)}) collective-permute-start(bf16[2,64,256]{2,1,0:T(8,128)(2,1)S(1)} %get-tuple-element.36), channel_id=1, source_target_pairs={{0,8},{4,12},{8,0},{12,4},{16,24},{20,28},{24,16},{28,20},{1,9},{5... | collective-permute-start | bytes 196616 | tf_op jit(solution)/shard_map/ppermute | solution.py:442
  10.5 4.8 %collective-permute-start.4 = (bf16[2,128,256]{2,1,0:T(8,128)(2,1)S(1)}, bf16[2,128,256]{2,1,0:T(8,128)(2,1)S(1)}, u32[]{:S(2)}, u32[]{:S(2)}) collective-permute-start(bf16[2,128,256]{2,1,0:T(8,128)(2,1)S(1)} %get-tuple-element.39), channel_id=1, source_target_pairs={{0,1},{1,0},{2,3},{3,2},{4,8},{5,9},{6,10},{7,11},{8,4},{9,5},{10,... | collective-permute-start | bytes 393224 | tf_op jit(solution)/shard_map/ppermute | solution.py:453
  13.2 4.3 %collective-permute-start.6 = (bf16[2,64,256]{2,1,0:T(8,128)(2,1)S(1)}, bf16[2,64,256]{2,1,0:T(8,128)(2,1)S(1)}, u32[]{:S(2)}, u32[]{:S(2)}) collective-permute-start(bf16[2,64,256]{2,1,0:T(8,128)(2,1)S(1)} %join.1.fours_a), channel_id=1, source_target_pairs={{0,4},{4,0},{8,12},{12,8},{16,20},{20,16},{24,28},{28,24},{1,5},{5... | collective-permute-start | bytes 196616 | tf_op jit(solution)/shard_map/ppermute | solution.py:442
  15.3 5.1 %copy-start = (bf16[1024,1024]{1,0:T(8,128)(2,1)S(1)}, bf16[1024,1024]{1,0:T(8,128)(2,1)}, u32[]{:S(2)}) copy-start(bf16[1024,1024]{1,0:T(8,128)(2,1)} %refs_3_.1) | copy-start | bytes 6291460
  16.2 4.4 %collective-permute-start.8 = (bf16[128,256]{1,0:T(8,128)(2,1)S(1)}, bf16[128,256]{1,0:T(8,128)(2,1)S(1)}, u32[]{:S(2)}, u32[]{:S(2)}) collective-permute-start(bf16[128,256]{1,0:T(8,128)(2,1)S(1)} %get-tuple-element.46), channel_id=1, source_target_pairs={{0,3},{1,2},{2,1},{3,0},{4,7},{5,6},{6,5},{7,4},{8,11},{9,10},{10,... | collective-permute-start | bytes 196616 | tf_op jit(solution)/shard_map/ppermute | solution.py:442
  18.1 4.4 %collective-permute-start.7 = (bf16[128,256]{1,0:T(8,128)(2,1)S(1)}, bf16[128,256]{1,0:T(8,128)(2,1)S(1)}, u32[]{:S(2)}, u32[]{:S(2)}) collective-permute-start(bf16[128,256]{1,0:T(8,128)(2,1)S(1)} %get-tuple-element.45), channel_id=1, source_target_pairs={{0,2},{1,3},{2,0},{3,1},{4,6},{5,7},{6,4},{7,5},{8,10},{9,11},{10,... | collective-permute-start | bytes 196616 | tf_op jit(solution)/shard_map/ppermute | solution.py:442
  19.6 3.1 %collective-permute-start.9 = (bf16[16,256]{1,0:T(8,128)(2,1)S(1)}, bf16[16,256]{1,0:T(8,128)(2,1)S(1)}, u32[]{:S(2)}, u32[]{:S(2)}) collective-permute-start(bf16[16,256]{1,0:T(8,128)(2,1)S(1)} %get-tuple-element.47), channel_id=1, source_target_pairs={{0,3},{1,2},{2,1},{3,0},{4,7},{5,6},{6,5},{7,4},{8,11},{9,10},{10,... | collective-permute-start | bytes 24584 | tf_op jit(solution)/shard_map/ppermute | solution.py:442
  20.0 3.0 %collective-permute-start.10 = (bf16[128,256]{1,0:T(8,128)(2,1)S(1)}, bf16[128,256]{1,0:T(8,128)(2,1)S(1)}, u32[]{:S(2)}, u32[]{:S(2)}) collective-permute-start(bf16[128,256]{1,0:T(8,128)(2,1)S(1)} %get-tuple-element.48), channel_id=1, source_target_pairs={{0,1},{1,0},{2,3},{3,2},{4,5},{5,4},{6,7},{7,6},{8,9},{9,8},{10,11... | collective-permute-start | bytes 196616 | tf_op jit(solution)/shard_map/ppermute | solution.py:442

commit v2 on v1

--- a/solution.py
+++ b/solution.py
@@ -235,7 +235,7 @@
             coarse[index, :, pl.ds(pair * PAIR, PAIR)] = field
 
 
-def mid_kernel(edge_q, coarse, state, first_ref, second_ref, fine, *refs):
+def mid_kernel(edge_q, coarse, state, first_ref, second_ref, known, fine, *refs):
     outs, (ready, holds) = refs[:-2], refs[-2:]
     own = lax.axis_index("head")
     rows = state.shape[1]
@@ -318,50 +318,58 @@
             ).astype(jnp.bfloat16)
 
 
-def finish_kernel(
-    four_q, fine, four_ref, near_ref, three_a, three_b, fours_a, fours_b, *refs
-):
-    refs, (coarse, four_hold) = refs[:-2], refs[-2:]
-    steps_out = range(2, lax.axis_size("head"))
-    far, outs = refs[: -len(steps_out)], refs[-len(steps_out) :]
+def known_kernel(four_q, four_ref, near_ref, three_a, three_b, fours_ref, *refs):
+    far, (known, hold) = refs[:-2], refs[-2:]
     pairs = four_q.shape[1] // PAIR
     steps = {}
     for pair in range(pairs):
         lanes = pl.ds(pair * PAIR, PAIR)
-        ours, theirs, beyond = [], [], []
+        ours, beyond = [], []
         for which in range(2):
             ours.append(
                 [four_ref[which, :, lanes], near_ref[which, :, lanes]]
                 + [repooled(field[which, :, lanes]) for field in (three_a, three_b)]
             )
-            theirs.append([field[which, :, lanes] for field in (fours_a, fours_b)])
             beyond.append([field[which, :, lanes] for field in far])
+        keys = jnp.concatenate(ours[0] + [fours_ref[0, :, lanes]] + beyond[0], axis=0)
         steps[pair] = (
-            score(
-                four_q[:, lanes],
-                jnp.concatenate(ours[0] + theirs[0] + beyond[0], axis=0),
-                four_hold.at[pair],
-            ),
+            score(four_q[:, lanes], keys, hold.at[pair]),
             jnp.concatenate(
                 [with_ones(field) for field in ours[1]]
-                + [with_ones(field, 2.0) for field in theirs[1]]
+                + [with_ones(fours_ref[1, :, lanes], 2.0)]
                 + [with_ones(field) for field in beyond[1]],
                 axis=0,
             ),
         )
     for pair in range(pairs):
-        lanes = pl.ds(pair * PAIR, PAIR)
-        top, numer, rowsum = weigh(four_hold.at[pair], *steps[pair])
-        coarse[0, :, lanes] = numer / rowsum
-        coarse[1, :, lanes] = top + jnp.log(rowsum) * log2_e
-    finish_blocks(fine, coarse, zip(steps_out, outs))
+        for index, field in enumerate(weigh(hold.at[pair], *steps[pair])):
+            known[index, :, pl.ds(pair * PAIR, PAIR)] = field
+
+
+def finish_kernel(four_q, fours_ref, known, fine, *refs):
+    outs, (coarse, hold) = refs[:-2], refs[-2:]
+    pairs = four_q.shape[1] // PAIR
+    lanes = [pl.ds(pair * PAIR, PAIR) for pair in range(pairs)]
+    tops = [
+        score(four_q[:, lanes[pair]], fours_ref[0, :, lanes[pair]], hold.at[pair])
+        for pair in range(pairs)
+    ]
+    for pair in range(pairs):
+        values = with_ones(fours_ref[1, :, lanes[pair]], 2.0)
+        top, numer, rowsum = merged(
+            weigh(hold.at[pair], tops[pair], values),
+            [known[index, :, lanes[pair]] for index in range(3)],
+        )
+        coarse[0, :, lanes[pair]] = numer / rowsum
+        coarse[1, :, lanes[pair]] = top + jnp.log(rowsum) * log2_e
+    finish_blocks(fine, coarse, zip(range(2, lax.axis_size("head")), outs))
 
 
 def rest_kernel(fine, coarse, *outs):
     finish_blocks(fine, coarse, enumerate(outs))
 
 
-def rejoin_kernel(*refs):
+def rejoin_kernel(further_ref, *refs):
     outs = refs[len(refs) // 3 * 2 :]
     for early, late_ref, out in zip(refs, refs[len(outs) :], outs):
         features = early.shape[1]
@@ -387,18 +395,25 @@
         out[...] = ref[...].astype(jnp.float32)
 
 
-def carry_kernel(whole_ref, *refs):
-    half = len(refs) // 2
-    for ref, out in zip(refs[:half], refs[half:]):
-        out[...] = ref[...]
-
-
 def partial_kernel(own_ref, weight_ref, out_ref):
     features = own_ref.shape[1]
     start = pl.multiple_of(lax.axis_index("head") * features, features)
     out_ref[...] = jnp.dot(
         own_ref[...], weight_ref[pl.ds(start, features), :], preferred_element_type=jnp.float32
     )
+
+
+def further_kernel(widened_ref, partial_ref, weight_ref, *refs):
+    parts, out_ref = refs[:-1], refs[-1]
+    own = lax.axis_index("head")
+    total = partial_ref[...]
+    for step, part in enumerate(parts, 2):
+        features = part.shape[1]
+        start = pl.multiple_of((own ^ step) * features, features)
+        total += jnp.dot(
+            part[...], weight_ref[pl.ds(start, features), :], preferred_element_type=jnp.float32
+        )
+    out_ref[...] = total
 
 
 def project_kernel(partial_ref, *refs):
@@ -410,7 +425,7 @@
     for index in range(staged.shape[0]):
         columns = pl.ds(index * chunk, chunk)
         total = partial_ref[:, columns]
-        for step, part in zip([*range(2, len(parts) + 1), 1], parts):
+        for step, part in zip([*range(AHEAD, AHEAD + len(parts) - 1), 1], parts):
             start = pl.multiple_of((own ^ step) * features, features)
             total += jnp.dot(
                 part[...],
@@ -498,7 +513,7 @@
     second_in = across(second)
     four_in = swapped(four, "seq", 4)
     six_in = swapped(four, "seq", 6)
-    threes_in = [swapped(three, "seq", mask) for mask in (3, 2)]
+    threes_in = [swapped(three, "seq", mask) for mask in (2, 3)]
     edge_q, two_q, three_q, four_q, state = pl.pallas_call(
         local_kernel,
         out_shape=[
@@ -541,6 +556,24 @@
         cost_estimate=pl.CostEstimate(flops=2**31, bytes_accessed=2**21, transcendentals=0),
         name="coarse",
     )(two_q, three_q, first_in, *threes_in)
+    far = []
+    reach = 8
+    if reach < seq_count:
+        group = [four, near] + [repool_outside(field) for field in threes_in]
+        group = jnp.concatenate(group + [fours, fours_in], axis=1)
+        while reach < seq_count:
+            fresh = swapped(group, "seq", reach)
+            far.append(fresh)
+            group = jnp.concatenate([group, fresh], axis=1)
+            reach *= 2
+
+    known = pl.pallas_call(
+        known_kernel,
+        out_shape=jax.ShapeDtypeStruct((3, rows // 16, features), jnp.float32),
+        scratch_shapes=[pltpu.VMEM((pairs, rows // 8, rows // 16 * (seq_count - 2)), jnp.float32)],
+        compiler_params=params,
+        name="known",
+    )(four_q, four, near, *threes_in, fours, *far)
     away = range(AHEAD, head_count)
     fine, *early = pl.pallas_call(
         mid_kernel,
@@ -552,19 +585,8 @@
         ],
         compiler_params=params,
         name="mid",
-    )(edge_q, coarse, state, first_in, second_in)
+    )(edge_q, coarse, state, first_in, second_in, known)
     early_in = [swapped(part, "head", step) for step, part in zip(away, early)]
-
-    far = []
-    known = 8
-    if known < seq_count:
-        group = [four, near] + [repool_outside(field) for field in threes_in]
-        group = jnp.concatenate(group + [fours, fours_in], axis=1)
-        while known < seq_count:
-            fresh = swapped(group, "seq", known)
-            far.append(fresh)
-            group = jnp.concatenate([group, fresh], axis=1)
-            known *= 2
 
     parts = [bf16(BLOCK, features) for _ in range(AHEAD)]
     *outs, level_four = pl.pallas_call(
@@ -572,10 +594,10 @@
         out_shape=parts[2:]
         + [bf16(2 * SLAB, features) for _ in away]
         + [jax.ShapeDtypeStruct((2, rows // 16, features), jnp.float32)],
-        scratch_shapes=[pltpu.VMEM((pairs, rows // 8, rows // 16 * seq_count), jnp.float32)],
+        scratch_shapes=[pltpu.VMEM((pairs, rows // 8, rows // 8), jnp.float32)],
         compiler_params=params,
         name="finish",
-    )(four_q, fine, four, near, *threes_in, fours, fours_in, *far)
+    )(four_q, fours_in, known, fine)
     whole_in = [swapped(part, "head", step) for step, part in zip(range(2, AHEAD), outs)]
     late_in = [swapped(part, "head", step) for step, part in zip(away, outs[AHEAD - 2 :])]
     own_part, next_part = pl.pallas_call(
@@ -600,23 +622,23 @@
         cost_estimate=pl.CostEstimate(flops=2**22, bytes_accessed=2**10, transcendentals=0),
         name="widen",
     )(*early_in)
-    widened = pl.pallas_call(
-        carry_kernel,
-        out_shape=[jax.ShapeDtypeStruct((BLOCK, features), jnp.float32) for _ in away],
-        compiler_params=params,
-        name="carry",
-    )(whole_in[0], *widened)
+    further = pl.pallas_call(
+        further_kernel,
+        out_shape=jax.ShapeDtypeStruct((BLOCK, width), jnp.float32),
+        compiler_params=params,
+        name="further",
+    )(widened[0], partial, out_weight, *whole_in)
     rejoined = pl.pallas_call(
         rejoin_kernel,
         out_shape=[bf16(BLOCK, features) for _ in away],
         compiler_params=params,
         cost_estimate=heavy,
         name="rejoin",
-    )(*widened, *late_in)
+    )(further, *widened, *late_in)
     chunk = 2 * PAIR
     result = pl.pallas_call(
         project_kernel,
-        in_specs=[vmem] * (head_count + 1),
+        in_specs=[vmem] * (len(rejoined) + 3),
         out_specs=hbm,
         out_shape=bf16(BLOCK, width),
         scratch_shapes=[
@@ -626,7 +648,7 @@
         ],
         compiler_params=params,
         name="project",
-    )(partial, *whole_in, *rejoined, next_in, out_weight)
+    )(further, *rejoined, next_in, out_weight)
     return result[None]
 
 

time: 24.2 us -> 24.7 us (1.021)
  Pallas kernels: 6.69 us -> 7.22 us
    pallas_call x2 -> x3, Pallas kernels: 1.13 us -> 1.67 us  [the longest x1 1.05 us: per_device(): pl.pallas_call(project_kernel, in_specs=[vmem] * (len(rejoined) + 3), out...]
  transfers between devices with their start and end apart: 11 -> 11, of which waited for: 5 -> 5; matrix products, arithmetic and copies ran while one was open for 0% -> 0% of each run, Pallas kernels for 17% -> 20%
where the time goes in v2:
time: 24.7 us; the launch traced here: 24.5 us
  starting transfers between devices  12.3 us (50%)
  Pallas kernels  7.22 us (29%)
  waiting for transfers between devices  4.88 us (20%)
    ppermute x10, starting transfers between devices, swapped(): lax.ppermute(block, axis, [(i, i ^ mask) for i in range(lax.axis_size(axi...  12.3 us
    ppermute x10, waiting for transfers between devices, swapped(): lax.ppermute(block, axis, [(i, i ^ mask) for i in range(lax.axis_size(axi...  4.87 us
    pallas_call x1, Pallas kernels, per_device(): pl.pallas_call(local_kernel, out_shape=[bf16(2, BLOCK, features), bf16(ro...  1.54 us
    pallas_call x1, Pallas kernels, per_device(): pl.pallas_call(pool_kernel, in_specs=[hbm] * 2, out_shape=[bf16(rows, fea...  1.39 us
    pallas_call x1, Pallas kernels, per_device(): pl.pallas_call(project_kernel, in_specs=[vmem] * (len(rejoined) + 3), out...  1.05 us
    pallas_call x1, Pallas kernels, per_device(): pl.pallas_call(mid_kernel, out_shape=[jax.ShapeDtypeStruct((2, rows, feat...  0.93 us
    pallas_call x1, Pallas kernels, per_device(): pl.pallas_call(finish_kernel, out_shape=parts[2:] + [bf16(2 * SLAB, featu...  0.59 us
    pallas_call x1, Pallas kernels, per_device(): pl.pallas_call(coarse_kernel, out_shape=[jax.ShapeDtypeStruct((3, rows //...  0.5 us
  transfers between devices with their start and end apart: 11, of which 5 were waited for; matrix products, arithmetic and copies ran while one was open for 0% of the time, Pallas kernels for 20%

profile of v2, /device:TPU:0, one launch (start us, length us, event | category | flops | bytes accessed | tf_op | source)
XLA Modules:
  0.0 24.5 jit_solution(5115952091159805858)
XLA Ops:
  0.0 1.4 %pool.1 = (bf16[512,256]{1,0:T(8,128)(2,1)S(1)}, bf16[512,256]{1,0:T(8,128)(2,1)S(1)}, bf16[2,224,256]{2,1,0:T(8,128)(2,1)S(1)}, bf16[2,256,256]{2,1,0:T(8,128)(2,1)S(1)}, bf16[2,128,256]{2,1,0:T(8,128)(2,1)S(1)}) custom-call(bf16[1,512,256]{2,1,0:T(8,128)(2,1)} %k_hbm.1, bf16[1,512,256]{2,1,0:T(8,128)(2,1)} %v_hbm.1), custom_call_target="tpu_custom_call" | custom-call | tf_op jit(solution)/shard_map/pool/pallas_call | solution.py:483
  1.4 3.0 %collective-permute-start.1 = (bf16[2,224,256]{2,1,0:T(8,128)(2,1)S(1)}, bf16[2,224,256]{2,1,0:T(8,128)(2,1)S(1)}, u32[]{:S(2)}, u32[]{:S(2)}) collective-permute-start(bf16[2,224,256]{2,1,0:T(8,128)(2,1)S(1)} %get-tuple-element.35), channel_id=1, source_target_pairs={{0,4},{4,0},{8,12},{12,8},{16,20},{20,16},{24,28},{28,24},{1,5},{5... | collective-permute-start | bytes 688136 | tf_op jit(solution)/shard_map/ppermute | solution.py:457
  4.4 0.0 copy-start.1
  4.5 2.7 %collective-permute-start = (bf16[2,32,256]{2,1,0:T(8,128)(2,1)S(1)}, bf16[2,32,256]{2,1,0:T(8,128)(2,1)S(1)}, u32[]{:S(2)}, u32[]{:S(2)}) collective-permute-start(bf16[2,32,256]{2,1,0:T(8,128)(2,1)S(1)} %get-tuple-element.31.four_ref), channel_id=1, source_target_pairs={{0,16},{4,20},{8,24},{12,28},{16,0},{20,4},{24,8},{28,12},{1,17},{... | collective-permute-start | bytes 98312 | tf_op jit(solution)/shard_map/ppermute | solution.py:457
  7.1 1.3 %collective-permute-start.5 = (bf16[2,32,256]{2,1,0:T(8,128)(2,1)S(1)}, bf16[2,32,256]{2,1,0:T(8,128)(2,1)S(1)}, u32[]{:S(2)}, u32[]{:S(2)}) collective-permute-start(bf16[2,32,256]{2,1,0:T(8,128)(2,1)S(1)} %get-tuple-element.31.four_ref), channel_id=1, source_target_pairs={{0,24},{4,28},{8,16},{12,20},{16,8},{20,12},{24,0},{28,4},{1,25},{... | collective-permute-start | bytes 98312 | tf_op jit(solution)/shard_map/ppermute | solution.py:457
  8.5 0.2 collective-permute-start.3
  8.7 1.8 %collective-permute-start.2 = (bf16[2,64,256]{2,1,0:T(8,128)(2,1)S(1)}, bf16[2,64,256]{2,1,0:T(8,128)(2,1)S(1)}, u32[]{:S(2)}, u32[]{:S(2)}) collective-permute-start(bf16[2,64,256]{2,1,0:T(8,128)(2,1)S(1)} %get-tuple-element.36), channel_id=1, source_target_pairs={{0,8},{4,12},{8,0},{12,4},{16,24},{20,28},{24,16},{28,20},{1,9},{5... | collective-permute-start | bytes 196616 | tf_op jit(solution)/shard_map/ppermute | solution.py:457
  10.5 0.0 collective-permute-done.four_ref
  10.5 0.0 collective-permute-start.4
  10.5 0.0 copy-done.1
  10.5 1.5 %local.1 = (bf16[2,128,256]{2,1,0:T(8,128)(2,1)S(1)}, bf16[128,256]{1,0:T(8,128)(2,1)S(1)}, bf16[64,256]{1,0:T(8,128)(2,1)S(1)}, bf16[32,256]{1,0:T(8,128)(2,1)S(1)}, f32[3,512,256]{2,1,0:T(8,128)S(1)}) custom-call(bf16[512,256]{1,0:T(8,128)(2,1)S(1)} %bitcast.2, bf16[512,256]{1,0:T(8,128)(2,1)S(1)} %get-tuple-element.27.k_ref, ...), custom_call_target="tpu_custom_call" | custom-call | tf_op jit(solution)/shard_map/local/pallas_call | solution.py:517
  12.0 1.2 %collective-permute-done.5.six_ref = bf16[2,32,256]{2,1,0:T(8,128)(2,1)S(1)} collective-permute-done((bf16[2,32,256]{2,1,0:T(8,128)(2,1)S(1)}, bf16[2,32,256]{2,1,0:T(8,128)(2,1)S(1)}, u32[]{:S(2)}, u32[]{:S(2)}) %collective-permute-start.5) | collective-permute-done | bytes 32800 | tf_op jit(solution)/shard_map/ppermute | solution.py:457
  13.2 0.9 %collective-permute-start.7 = (bf16[2,64,256]{2,1,0:T(8,128)(2,1)S(1)}, bf16[2,64,256]{2,1,0:T(8,128)(2,1)S(1)}, u32[]{:S(2)}, u32[]{:S(2)}) collective-permute-start(bf16[2,64,256]{2,1,0:T(8,128)(2,1)S(1)} %join.1.fours_ref), channel_id=1, source_target_pairs={{0,4},{4,0},{8,12},{12,8},{16,20},{20,16},{24,28},{28,24},{1,5},{5... | collective-permute-start | bytes 196616 | tf_op jit(solution)/shard_map/ppermute | solution.py:457
  14.2 0.0 collective-permute-done.3.three_b
  14.2 0.6 %collective-permute-done.2.three_a = bf16[2,64,256]{2,1,0:T(8,128)(2,1)S(1)} collective-permute-done((bf16[2,64,256]{2,1,0:T(8,128)(2,1)S(1)}, bf16[2,64,256]{2,1,0:T(8,128)(2,1)S(1)}, u32[]{:S(2)}, u32[]{:S(2)}) %collective-permute-start.2) | collective-permute-done | bytes 65568 | tf_op jit(solution)/shard_map/ppermute | solution.py:457
  14.8 0.0 collective-permute-done.1.first_ref
  14.8 0.5 %coarse.1 = (f32[3,128,256]{2,1,0:T(8,128)S(1)}, bf16[2,32,256]{2,1,0:T(8,128)(2,1)S(1)}) custom-call(bf16[128,256]{1,0:T(8,128)(2,1)S(1)} %get-tuple-element.33.two_q, bf16[64,256]{1,0:T(8,128)(2,1)S(1)} %get-tuple-element.34.three_q, bf16[2,224,256]{2,1,0:T(8,128)(2,1)S(1)} %collective-permute-done.1.first_ref, ...), custom_call_target="tpu_custom_call" | custom-call | flops 2147483648 | bytes 2097152 | tf_op jit(solution)/shard_map/coarse/pallas_call | solution.py:543
  15.3 0.4 %known.1 = f32[3,32,256]{2,1,0:T(8,128)S(1)} custom-call(bf16[32,256]{1,0:T(8,128)(2,1)S(1)} %get-tuple-element.40.query_ref.four_q, bf16[2,32,256]{2,1,0:T(8,128)(2,1)S(1)} %get-tuple-element.31.four_ref, bf16[2,32,256]{2,1,0:T(8,128)(2,1)S(1)} %get-tuple-element.41.near_ref, bf16[2,64,256]{2,1,0:T(8,128)(2,1)S(1)} %collective-permute-done.2.three_a, ...), custom_call_target="tpu_custom_call" | custom-call | tf_op jit(solution)/shard_map/known/pallas_call | solution.py:570
  15.7 0.0 collective-permute-done.4.second_ref
  15.7 0.0 copy-start
  15.7 0.9 %mid.1 = (f32[2,512,256]{2,1,0:T(8,128)S(1)}, bf16[128,256]{1,0:T(8,128)(2,1)S(1)}) custom-call(bf16[2,128,256]{2,1,0:T(8,128)(2,1)S(1)} %get-tuple-element.32.edge_q, f32[3,128,256]{2,1,0:T(8,128)S(1)} %get-tuple-element.37.coarse, f32[3,512,256]{2,1,0:T(8,128)S(1)} %get-tuple-element.38.state, bf16[2,224,256]{2,1,0:T(8,128)(2,1)S(1)} %collective-permute-done.1.first_ref, ...), custom_call_target="tpu_custom_call" | custom-call | tf_op jit(solution)/shard_map/mid/pallas_call | solution.py:578
  16.6 0.1 collective-permute-start.6
  16.7 0.8 %collective-permute-done.7.fours_ref = bf16[2,64,256]{2,1,0:T(8,128)(2,1)S(1)} collective-permute-done((bf16[2,64,256]{2,1,0:T(8,128)(2,1)S(1)}, bf16[2,64,256]{2,1,0:T(8,128)(2,1)S(1)}, u32[]{:S(2)}, u32[]{:S(2)}) %collective-permute-start.7) | collective-permute-done | bytes 65568 | tf_op jit(solution)/shard_map/ppermute | solution.py:457
  17.5 0.6 %finish.1 = (bf16[128,256]{1,0:T(8,128)(2,1)S(1)}, bf16[16,256]{1,0:T(8,128)(2,1)S(1)}, f32[2,32,256]{2,1,0:T(8,128)S(1)}) custom-call(bf16[32,256]{1,0:T(8,128)(2,1)S(1)} %get-tuple-element.40.query_ref.four_q, bf16[2,64,256]{2,1,0:T(8,128)(2,1)S(1)} %collective-permute-done.7.fours_ref, f32[3,32,256]{2,1,0:T(8,128)S(1)} %known.1, ...), custom_call_target="tpu_custom_call" | custom-call | tf_op jit(solution)/shard_map/finish/pallas_call | solution.py:592
  18.1 1.5 %collective-permute-start.8 = (bf16[128,256]{1,0:T(8,128)(2,1)S(1)}, bf16[128,256]{1,0:T(8,128)(2,1)S(1)}, u32[]{:S(2)}, u32[]{:S(2)}) collective-permute-start(bf16[128,256]{1,0:T(8,128)(2,1)S(1)} %get-tuple-element.46), channel_id=1, source_target_pairs={{0,2},{1,3},{2,0},{3,1},{4,6},{5,7},{6,4},{7,5},{8,10},{9,11},{10,... | collective-permute-start | bytes 196616 | tf_op jit(solution)/shard_map/ppermute | solution.py:457
  19.6 0.7 %collective-permute-start.9 = (bf16[16,256]{1,0:T(8,128)(2,1)S(1)}, bf16[16,256]{1,0:T(8,128)(2,1)S(1)}, u32[]{:S(2)}, u32[]{:S(2)}) collective-permute-start(bf16[16,256]{1,0:T(8,128)(2,1)S(1)} %get-tuple-element.47), channel_id=1, source_target_pairs={{0,3},{1,2},{2,1},{3,0},{4,7},{5,6},{6,5},{7,4},{8,11},{9,10},{10,... | collective-permute-start | bytes 24584 | tf_op jit(solution)/shard_map/ppermute | solution.py:457
  20.3 0.1 rest.1
  20.3 0.1 collective-permute-start.10
  20.4 0.0 copy-done
  20.4 0.2 partial.1.partial_ref
  20.7 0.4 %collective-permute-done.6.refs_0_ = bf16[128,256]{1,0:T(8,128)(2,1)S(1)} collective-permute-done((bf16[128,256]{1,0:T(8,128)(2,1)S(1)}, bf16[128,256]{1,0:T(8,128)(2,1)S(1)}, u32[]{:S(2)}, u32[]{:S(2)}) %collective-permute-start.6) | collective-permute-done | bytes 65568 | tf_op jit(solution)/shard_map/ppermute | solution.py:457
  21.0 1.9 %collective-permute-done.8.refs_0_ = bf16[128,256]{1,0:T(8,128)(2,1)S(1)} collective-permute-done((bf16[128,256]{1,0:T(8,128)(2,1)S(1)}, bf16[128,256]{1,0:T(8,128)(2,1)S(1)}, u32[]{:S(2)}, u32[]{:S(2)}) %collective-permute-start.8) | collective-permute-done | bytes 65568 | tf_op jit(solution)/shard_map/ppermute | solution.py:457
  23.0 0.2 further.1.further_ref.partial_ref
  23.2 0.0 collective-permute-done.9.refs_1_
  23.2 0.2 rejoin.1.refs_0_
  23.5 0.0 collective-permute-done.10.refs_1_
  23.5 1.0 %project.1 = bf16[128,1024]{1,0:T(8,128)(2,1)} custom-call(f32[128,1024]{1,0:T(8,128)S(1)} %further.1.further_ref.partial_ref, bf16[128,256]{1,0:T(8,128)(2,1)S(1)} %rejoin.1.refs_0_, bf16[128,256]{1,0:T(8,128)(2,1)S(1)} %collective-permute-done.10.refs_1_, bf16[1024,1024]{1,0:T(8,128)(2,1)S(1)} %copy-done), custom_call_target="tpu_custom_call" | custom-call | tf_op jit(solution)/shard_map/project/pallas_call | solution.py:639
  (3 shorter events, 0.1 us)
Async XLA Ops:
  1.4 13.4 %collective-permute-start.1 = (bf16[2,224,256]{2,1,0:T(8,128)(2,1)S(1)}, bf16[2,224,256]{2,1,0:T(8,128)(2,1)S(1)}, u32[]{:S(2)}, u32[]{:S(2)}) collective-permute-start(bf16[2,224,256]{2,1,0:T(8,128)(2,1)S(1)} %get-tuple-element.35), channel_id=1, source_target_pairs={{0,4},{4,0},{8,12},{12,8},{16,20},{20,16},{24,28},{28,24},{1,5},{5... | collective-permute-start | bytes 688136 | tf_op jit(solution)/shard_map/ppermute | solution.py:457
  4.4 6.0 %copy-start.1 = (bf16[1,512,256]{2,1,0:T(8,128)(2,1)S(1)}, bf16[1,512,256]{2,1,0:T(8,128)(2,1)}, u32[]{:S(2)}) copy-start(bf16[1,512,256]{2,1,0:T(8,128)(2,1)} %param.4) | copy-start | bytes 786436
  4.5 6.0 %collective-permute-start = (bf16[2,32,256]{2,1,0:T(8,128)(2,1)S(1)}, bf16[2,32,256]{2,1,0:T(8,128)(2,1)S(1)}, u32[]{:S(2)}, u32[]{:S(2)}) collective-permute-start(bf16[2,32,256]{2,1,0:T(8,128)(2,1)S(1)} %get-tuple-element.31.four_ref), channel_id=1, source_target_pairs={{0,16},{4,20},{8,24},{12,28},{16,0},{20,4},{24,8},{28,12},{1,17},{... | collective-permute-start | bytes 98312 | tf_op jit(solution)/shard_map/ppermute | solution.py:457
  7.1 6.1 %collective-permute-start.5 = (bf16[2,32,256]{2,1,0:T(8,128)(2,1)S(1)}, bf16[2,32,256]{2,1,0:T(8,128)(2,1)S(1)}, u32[]{:S(2)}, u32[]{:S(2)}) collective-permute-start(bf16[2,32,256]{2,1,0:T(8,128)(2,1)S(1)} %get-tuple-element.31.four_ref), channel_id=1, source_target_pairs={{0,24},{4,28},{8,16},{12,20},{16,8},{20,12},{24,0},{28,4},{1,25},{... | collective-permute-start | bytes 98312 | tf_op jit(solution)/shard_map/ppermute | solution.py:457
  8.5 5.7 %collective-permute-start.3 = (bf16[2,64,256]{2,1,0:T(8,128)(2,1)S(1)}, bf16[2,64,256]{2,1,0:T(8,128)(2,1)S(1)}, u32[]{:S(2)}, u32[]{:S(2)}) collective-permute-start(bf16[2,64,256]{2,1,0:T(8,128)(2,1)S(1)} %get-tuple-element.36), channel_id=1, source_target_pairs={{0,12},{4,8},{8,4},{12,0},{16,28},{20,24},{24,20},{28,16},{1,13},{... | collective-permute-start | bytes 196616 | tf_op jit(solution)/shard_map/ppermute | solution.py:457
  8.7 6.1 %collective-permute-start.2 = (bf16[2,64,256]{2,1,0:T(8,128)(2,1)S(1)}, bf16[2,64,256]{2,1,0:T(8,128)(2,1)S(1)}, u32[]{:S(2)}, u32[]{:S(2)}) collective-permute-start(bf16[2,64,256]{2,1,0:T(8,128)(2,1)S(1)} %get-tuple-element.36), channel_id=1, source_target_pairs={{0,8},{4,12},{8,0},{12,4},{16,24},{20,28},{24,16},{28,20},{1,9},{5... | collective-permute-start | bytes 196616 | tf_op jit(solution)/shard_map/ppermute | solution.py:457
  10.5 5.2 %collective-permute-start.4 = (bf16[2,128,256]{2,1,0:T(8,128)(2,1)S(1)}, bf16[2,128,256]{2,1,0:T(8,128)(2,1)S(1)}, u32[]{:S(2)}, u32[]{:S(2)}) collective-permute-start(bf16[2,128,256]{2,1,0:T(8,128)(2,1)S(1)} %get-tuple-element.39), channel_id=1, source_target_pairs={{0,1},{1,0},{2,3},{3,2},{4,8},{5,9},{6,10},{7,11},{8,4},{9,5},{10,... | collective-permute-start | bytes 393224 | tf_op jit(solution)/shard_map/ppermute | solution.py:468
  13.2 4.3 %collective-permute-start.7 = (bf16[2,64,256]{2,1,0:T(8,128)(2,1)S(1)}, bf16[2,64,256]{2,1,0:T(8,128)(2,1)S(1)}, u32[]{:S(2)}, u32[]{:S(2)}) collective-permute-start(bf16[2,64,256]{2,1,0:T(8,128)(2,1)S(1)} %join.1.fours_ref), channel_id=1, source_target_pairs={{0,4},{4,0},{8,12},{12,8},{16,20},{20,16},{24,28},{28,24},{1,5},{5... | collective-permute-start | bytes 196616 | tf_op jit(solution)/shard_map/ppermute | solution.py:457
  15.7 4.7 %copy-start = (bf16[1024,1024]{1,0:T(8,128)(2,1)S(1)}, bf16[1024,1024]{1,0:T(8,128)(2,1)}, u32[]{:S(2)}) copy-start(bf16[1024,1024]{1,0:T(8,128)(2,1)} %refs_2_.1) | copy-start | bytes 6291460
  16.6 4.4 %collective-permute-start.6 = (bf16[128,256]{1,0:T(8,128)(2,1)S(1)}, bf16[128,256]{1,0:T(8,128)(2,1)S(1)}, u32[]{:S(2)}, u32[]{:S(2)}) collective-permute-start(bf16[128,256]{1,0:T(8,128)(2,1)S(1)} %get-tuple-element.42), channel_id=1, source_target_pairs={{0,3},{1,2},{2,1},{3,0},{4,7},{5,6},{6,5},{7,4},{8,11},{9,10},{10,... | collective-permute-start | bytes 196616 | tf_op jit(solution)/shard_map/ppermute | solution.py:457
  18.1 4.9 %collective-permute-start.8 = (bf16[128,256]{1,0:T(8,128)(2,1)S(1)}, bf16[128,256]{1,0:T(8,128)(2,1)S(1)}, u32[]{:S(2)}, u32[]{:S(2)}) collective-permute-start(bf16[128,256]{1,0:T(8,128)(2,1)S(1)} %get-tuple-element.46), channel_id=1, source_target_pairs={{0,2},{1,3},{2,0},{3,1},{4,6},{5,7},{6,4},{7,5},{8,10},{9,11},{10,... | collective-permute-start | bytes 196616 | tf_op jit(solution)/shard_map/ppermute | solution.py:457
  19.6 3.7 %collective-permute-start.9 = (bf16[16,256]{1,0:T(8,128)(2,1)S(1)}, bf16[16,256]{1,0:T(8,128)(2,1)S(1)}, u32[]{:S(2)}, u32[]{:S(2)}) collective-permute-start(bf16[16,256]{1,0:T(8,128)(2,1)S(1)} %get-tuple-element.47), channel_id=1, source_target_pairs={{0,3},{1,2},{2,1},{3,0},{4,7},{5,6},{6,5},{7,4},{8,11},{9,10},{10,... | collective-permute-start | bytes 24584 | tf_op jit(solution)/shard_map/ppermute | solution.py:457
  20.3 3.1 %collective-permute-start.10 = (bf16[128,256]{1,0:T(8,128)(2,1)S(1)}, bf16[128,256]{1,0:T(8,128)(2,1)S(1)}, u32[]{:S(2)}, u32[]{:S(2)}) collective-permute-start(bf16[128,256]{1,0:T(8,128)(2,1)S(1)} %get-tuple-element.48), channel_id=1, source_target_pairs={{0,1},{1,0},{2,3},{3,2},{4,5},{5,4},{6,7},{7,6},{8,9},{9,8},{10,11... | collective-permute-start | bytes 196616 | tf_op jit(solution)/shard_map/ppermute | solution.py:457

commit v3 on v1

--- a/solution.py
+++ b/solution.py
@@ -361,7 +361,7 @@
     finish_blocks(fine, coarse, enumerate(outs))
 
 
-def rejoin_kernel(*refs):
+def rejoin_kernel(further_ref, *refs):
     outs = refs[len(refs) // 3 * 2 :]
     for early, late_ref, out in zip(refs, refs[len(outs) :], outs):
         features = early.shape[1]
@@ -387,18 +387,25 @@
         out[...] = ref[...].astype(jnp.float32)
 
 
-def carry_kernel(whole_ref, *refs):
-    half = len(refs) // 2
-    for ref, out in zip(refs[:half], refs[half:]):
-        out[...] = ref[...]
-
-
 def partial_kernel(own_ref, weight_ref, out_ref):
     features = own_ref.shape[1]
     start = pl.multiple_of(lax.axis_index("head") * features, features)
     out_ref[...] = jnp.dot(
         own_ref[...], weight_ref[pl.ds(start, features), :], preferred_element_type=jnp.float32
     )
+
+
+def further_kernel(widened_ref, partial_ref, weight_ref, *refs):
+    parts, out_ref = refs[:-1], refs[-1]
+    own = lax.axis_index("head")
+    total = partial_ref[...]
+    for step, part in enumerate(parts, 2):
+        features = part.shape[1]
+        start = pl.multiple_of((own ^ step) * features, features)
+        total += jnp.dot(
+            part[...], weight_ref[pl.ds(start, features), :], preferred_element_type=jnp.float32
+        )
+    out_ref[...] = total
 
 
 def project_kernel(partial_ref, *refs):
@@ -410,7 +417,7 @@
     for index in range(staged.shape[0]):
         columns = pl.ds(index * chunk, chunk)
         total = partial_ref[:, columns]
-        for step, part in zip([*range(2, len(parts) + 1), 1], parts):
+        for step, part in zip([*range(AHEAD, AHEAD + len(parts) - 1), 1], parts):
             start = pl.multiple_of((own ^ step) * features, features)
             total += jnp.dot(
                 part[...],
@@ -600,23 +607,23 @@
         cost_estimate=pl.CostEstimate(flops=2**22, bytes_accessed=2**10, transcendentals=0),
         name="widen",
     )(*early_in)
-    widened = pl.pallas_call(
-        carry_kernel,
-        out_shape=[jax.ShapeDtypeStruct((BLOCK, features), jnp.float32) for _ in away],
-        compiler_params=params,
-        name="carry",
-    )(whole_in[0], *widened)
+    further = pl.pallas_call(
+        further_kernel,
+        out_shape=jax.ShapeDtypeStruct((BLOCK, width), jnp.float32),
+        compiler_params=params,
+        name="further",
+    )(widened[0], partial, out_weight, *whole_in)
     rejoined = pl.pallas_call(
         rejoin_kernel,
         out_shape=[bf16(BLOCK, features) for _ in away],
         compiler_params=params,
         cost_estimate=heavy,
         name="rejoin",
-    )(*widened, *late_in)
+    )(further, *widened, *late_in)
     chunk = 2 * PAIR
     result = pl.pallas_call(
         project_kernel,
-        in_specs=[vmem] * (head_count + 1),
+        in_specs=[vmem] * (len(rejoined) + 3),
         out_specs=hbm,
         out_shape=bf16(BLOCK, width),
         scratch_shapes=[
@@ -626,7 +633,7 @@
         ],
         compiler_params=params,
         name="project",
-    )(partial, *whole_in, *rejoined, next_in, out_weight)
+    )(further, *rejoined, next_in, out_weight)
     return result[None]
 
 

time: 24.2 us -> 24.2 us (level)
  transfers between devices with their start and end apart: 11 -> 11, of which waited for: 5 -> 4; matrix products, arithmetic and copies ran while one was open for 0% -> 0% of each run, Pallas kernels for 17% -> 18%
where the time goes in v3:
time: 24.2 us; the launch traced here: 24.1 us
  starting transfers between devices  12.2 us (50%)
  Pallas kernels  6.84 us (28%)
  waiting for transfers between devices  4.86 us (20%)
    ppermute x10, starting transfers between devices, swapped(): lax.ppermute(block, axis, [(i, i ^ mask) for i in range(lax.axis_size(axi...  12.2 us
    ppermute x10, waiting for transfers between devices, swapped(): lax.ppermute(block, axis, [(i, i ^ mask) for i in range(lax.axis_size(axi...  4.86 us
    pallas_call x1, Pallas kernels, per_device(): pl.pallas_call(local_kernel, out_shape=[bf16(2, BLOCK, features), bf16(ro...  1.54 us
    pallas_call x1, Pallas kernels, per_device(): pl.pallas_call(pool_kernel, in_specs=[hbm] * 2, out_shape=[bf16(rows, fea...  1.39 us
    pallas_call x1, Pallas kernels, per_device(): pl.pallas_call(project_kernel, in_specs=[vmem] * (len(rejoined) + 3), out...  1.05 us
    pallas_call x1, Pallas kernels, per_device(): pl.pallas_call(mid_kernel, out_shape=[jax.ShapeDtypeStruct((2, rows, feat...  0.93 us
    pallas_call x1, Pallas kernels, per_device(): pl.pallas_call(finish_kernel, out_shape=parts[2:] + [bf16(2 * SLAB, featu...  0.61 us
    pallas_call x1, Pallas kernels, per_device(): pl.pallas_call(coarse_kernel, out_shape=[jax.ShapeDtypeStruct((3, rows //...  0.5 us
  transfers between devices with their start and end apart: 11, of which 4 were waited for; matrix products, arithmetic and copies ran while one was open for 0% of the time, Pallas kernels for 18%

profile of v3, /device:TPU:0, one launch (start us, length us, event | category | flops | bytes accessed | tf_op | source)
XLA Modules:
  0.0 24.1 jit_solution(14105190472883081037)
XLA Ops:
  0.0 1.4 %pool.1 = (bf16[512,256]{1,0:T(8,128)(2,1)S(1)}, bf16[512,256]{1,0:T(8,128)(2,1)S(1)}, bf16[2,224,256]{2,1,0:T(8,128)(2,1)S(1)}, bf16[2,256,256]{2,1,0:T(8,128)(2,1)S(1)}, bf16[2,128,256]{2,1,0:T(8,128)(2,1)S(1)}) custom-call(bf16[1,512,256]{2,1,0:T(8,128)(2,1)} %k_hbm.1, bf16[1,512,256]{2,1,0:T(8,128)(2,1)} %v_hbm.1), custom_call_target="tpu_custom_call" | custom-call | tf_op jit(solution)/shard_map/pool/pallas_call | solution.py:475
  1.4 3.0 %collective-permute-start.1 = (bf16[2,224,256]{2,1,0:T(8,128)(2,1)S(1)}, bf16[2,224,256]{2,1,0:T(8,128)(2,1)S(1)}, u32[]{:S(2)}, u32[]{:S(2)}) collective-permute-start(bf16[2,224,256]{2,1,0:T(8,128)(2,1)S(1)} %get-tuple-element.35), channel_id=1, source_target_pairs={{0,4},{4,0},{8,12},{12,8},{16,20},{20,16},{24,28},{28,24},{1,5},{5... | collective-permute-start | bytes 688136 | tf_op jit(solution)/shard_map/ppermute | solution.py:449
  4.4 0.0 copy-start.1
  4.5 2.7 %collective-permute-start = (bf16[2,32,256]{2,1,0:T(8,128)(2,1)S(1)}, bf16[2,32,256]{2,1,0:T(8,128)(2,1)S(1)}, u32[]{:S(2)}, u32[]{:S(2)}) collective-permute-start(bf16[2,32,256]{2,1,0:T(8,128)(2,1)S(1)} %get-tuple-element.31.four_ref), channel_id=1, source_target_pairs={{0,16},{4,20},{8,24},{12,28},{16,0},{20,4},{24,8},{28,12},{1,17},{... | collective-permute-start | bytes 98312 | tf_op jit(solution)/shard_map/ppermute | solution.py:449
  7.1 1.3 %collective-permute-start.6 = (bf16[2,32,256]{2,1,0:T(8,128)(2,1)S(1)}, bf16[2,32,256]{2,1,0:T(8,128)(2,1)S(1)}, u32[]{:S(2)}, u32[]{:S(2)}) collective-permute-start(bf16[2,32,256]{2,1,0:T(8,128)(2,1)S(1)} %get-tuple-element.31.four_ref), channel_id=1, source_target_pairs={{0,24},{4,28},{8,16},{12,20},{16,8},{20,12},{24,0},{28,4},{1,25},{... | collective-permute-start | bytes 98312 | tf_op jit(solution)/shard_map/ppermute | solution.py:449
  8.5 0.2 collective-permute-start.2
  8.7 1.8 %collective-permute-start.3 = (bf16[2,64,256]{2,1,0:T(8,128)(2,1)S(1)}, bf16[2,64,256]{2,1,0:T(8,128)(2,1)S(1)}, u32[]{:S(2)}, u32[]{:S(2)}) collective-permute-start(bf16[2,64,256]{2,1,0:T(8,128)(2,1)S(1)} %get-tuple-element.36), channel_id=1, source_target_pairs={{0,8},{4,12},{8,0},{12,4},{16,24},{20,28},{24,16},{28,20},{1,9},{5... | collective-permute-start | bytes 196616 | tf_op jit(solution)/shard_map/ppermute | solution.py:449
  10.5 0.0 collective-permute-done.four_ref
  10.5 0.0 collective-permute-start.4
  10.5 0.0 copy-done.1
  10.5 1.5 %local.1 = (bf16[2,128,256]{2,1,0:T(8,128)(2,1)S(1)}, bf16[128,256]{1,0:T(8,128)(2,1)S(1)}, bf16[64,256]{1,0:T(8,128)(2,1)S(1)}, bf16[32,256]{1,0:T(8,128)(2,1)S(1)}, f32[3,512,256]{2,1,0:T(8,128)S(1)}) custom-call(bf16[512,256]{1,0:T(8,128)(2,1)S(1)} %bitcast.2, bf16[512,256]{1,0:T(8,128)(2,1)S(1)} %get-tuple-element.27.k_ref, ...), custom_call_target="tpu_custom_call" | custom-call | tf_op jit(solution)/shard_map/local/pallas_call | solution.py:509
  12.0 1.2 %collective-permute-done.6.six_ref = bf16[2,32,256]{2,1,0:T(8,128)(2,1)S(1)} collective-permute-done((bf16[2,32,256]{2,1,0:T(8,128)(2,1)S(1)}, bf16[2,32,256]{2,1,0:T(8,128)(2,1)S(1)}, u32[]{:S(2)}, u32[]{:S(2)}) %collective-permute-start.6) | collective-permute-done | bytes 32800 | tf_op jit(solution)/shard_map/ppermute | solution.py:449
  13.2 0.9 %collective-permute-start.7 = (bf16[2,64,256]{2,1,0:T(8,128)(2,1)S(1)}, bf16[2,64,256]{2,1,0:T(8,128)(2,1)S(1)}, u32[]{:S(2)}, u32[]{:S(2)}) collective-permute-start(bf16[2,64,256]{2,1,0:T(8,128)(2,1)S(1)} %join.1.fours_a), channel_id=1, source_target_pairs={{0,4},{4,0},{8,12},{12,8},{16,20},{20,16},{24,28},{28,24},{1,5},{5... | collective-permute-start | bytes 196616 | tf_op jit(solution)/shard_map/ppermute | solution.py:449
  14.2 0.0 collective-permute-done.2.three_a
  14.2 0.6 %collective-permute-done.3.three_b = bf16[2,64,256]{2,1,0:T(8,128)(2,1)S(1)} collective-permute-done((bf16[2,64,256]{2,1,0:T(8,128)(2,1)S(1)}, bf16[2,64,256]{2,1,0:T(8,128)(2,1)S(1)}, u32[]{:S(2)}, u32[]{:S(2)}) %collective-permute-start.3) | collective-permute-done | bytes 65568 | tf_op jit(solution)/shard_map/ppermute | solution.py:449
  14.8 0.0 collective-permute-done.1.first_ref
  14.8 0.5 %coarse.1 = (f32[3,128,256]{2,1,0:T(8,128)S(1)}, bf16[2,32,256]{2,1,0:T(8,128)(2,1)S(1)}) custom-call(bf16[128,256]{1,0:T(8,128)(2,1)S(1)} %get-tuple-element.33.two_q, bf16[64,256]{1,0:T(8,128)(2,1)S(1)} %get-tuple-element.34.three_q, bf16[2,224,256]{2,1,0:T(8,128)(2,1)S(1)} %collective-permute-done.1.first_ref, ...), custom_call_target="tpu_custom_call" | custom-call | flops 2147483648 | bytes 2097152 | tf_op jit(solution)/shard_map/coarse/pallas_call | solution.py:535
  15.3 0.0 collective-permute-done.4.second_ref
  15.3 0.0 copy-start
  15.3 0.9 %mid.1 = (f32[2,512,256]{2,1,0:T(8,128)S(1)}, bf16[128,256]{1,0:T(8,128)(2,1)S(1)}) custom-call(bf16[2,128,256]{2,1,0:T(8,128)(2,1)S(1)} %get-tuple-element.32.edge_q, f32[3,128,256]{2,1,0:T(8,128)S(1)} %get-tuple-element.37.coarse, f32[3,512,256]{2,1,0:T(8,128)S(1)} %get-tuple-element.38.state, bf16[2,224,256]{2,1,0:T(8,128)(2,1)S(1)} %collective-permute-done.1.first_ref, ...), custom_call_target="tpu_custom_call" | custom-call | tf_op jit(solution)/shard_map/mid/pallas_call | solution.py:552
  16.2 0.1 collective-permute-start.5
  16.3 1.2 %collective-permute-done.7.fours_b = bf16[2,64,256]{2,1,0:T(8,128)(2,1)S(1)} collective-permute-done((bf16[2,64,256]{2,1,0:T(8,128)(2,1)S(1)}, bf16[2,64,256]{2,1,0:T(8,128)(2,1)S(1)}, u32[]{:S(2)}, u32[]{:S(2)}) %collective-permute-start.7) | collective-permute-done | bytes 65568 | tf_op jit(solution)/shard_map/ppermute | solution.py:449
  17.5 0.6 %finish.1 = (bf16[128,256]{1,0:T(8,128)(2,1)S(1)}, bf16[16,256]{1,0:T(8,128)(2,1)S(1)}, f32[2,32,256]{2,1,0:T(8,128)S(1)}) custom-call(bf16[32,256]{1,0:T(8,128)(2,1)S(1)} %get-tuple-element.42.query_ref.four_q, f32[2,512,256]{2,1,0:T(8,128)S(1)} %get-tuple-element.41.fine, bf16[2,32,256]{2,1,0:T(8,128)(2,1)S(1)} %get-tuple-element.31.four_ref, ...), custom_call_target="tpu_custom_call" | custom-call | tf_op jit(solution)/shard_map/finish/pallas_call | solution.py:577
  18.1 1.5 %collective-permute-start.8 = (bf16[128,256]{1,0:T(8,128)(2,1)S(1)}, bf16[128,256]{1,0:T(8,128)(2,1)S(1)}, u32[]{:S(2)}, u32[]{:S(2)}) collective-permute-start(bf16[128,256]{1,0:T(8,128)(2,1)S(1)} %get-tuple-element.46), channel_id=1, source_target_pairs={{0,2},{1,3},{2,0},{3,1},{4,6},{5,7},{6,4},{7,5},{8,10},{9,11},{10,... | collective-permute-start | bytes 196616 | tf_op jit(solution)/shard_map/ppermute | solution.py:449
  19.6 0.3 %collective-permute-start.9 = (bf16[16,256]{1,0:T(8,128)(2,1)S(1)}, bf16[16,256]{1,0:T(8,128)(2,1)S(1)}, u32[]{:S(2)}, u32[]{:S(2)}) collective-permute-start(bf16[16,256]{1,0:T(8,128)(2,1)S(1)} %get-tuple-element.47), channel_id=1, source_target_pairs={{0,3},{1,2},{2,1},{3,0},{4,7},{5,6},{6,5},{7,4},{8,11},{9,10},{10,... | collective-permute-start | bytes 24584 | tf_op jit(solution)/shard_map/ppermute | solution.py:449
  19.9 0.1 rest.1
  20.0 0.4 %collective-permute-start.10 = (bf16[128,256]{1,0:T(8,128)(2,1)S(1)}, bf16[128,256]{1,0:T(8,128)(2,1)S(1)}, u32[]{:S(2)}, u32[]{:S(2)}) collective-permute-start(bf16[128,256]{1,0:T(8,128)(2,1)S(1)} %get-tuple-element.48), channel_id=1, source_target_pairs={{0,1},{1,0},{2,3},{3,2},{4,5},{5,4},{6,7},{7,6},{8,9},{9,8},{10,11... | collective-permute-start | bytes 196616 | tf_op jit(solution)/shard_map/ppermute | solution.py:449
  20.4 0.0 copy-done
  20.4 0.2 partial.1.partial_ref
  20.6 0.0 collective-permute-done.5.refs_0_
  20.7 1.9 %collective-permute-done.8.refs_0_ = bf16[128,256]{1,0:T(8,128)(2,1)S(1)} collective-permute-done((bf16[128,256]{1,0:T(8,128)(2,1)S(1)}, bf16[128,256]{1,0:T(8,128)(2,1)S(1)}, u32[]{:S(2)}, u32[]{:S(2)}) %collective-permute-start.8) | collective-permute-done | bytes 65568 | tf_op jit(solution)/shard_map/ppermute | solution.py:449
  22.5 0.2 further.1.further_ref.partial_ref
  22.8 0.0 collective-permute-done.9.refs_1_
  22.8 0.2 rejoin.1.refs_0_
  23.0 0.0 collective-permute-done.10.refs_1_
  23.0 1.0 %project.1 = bf16[128,1024]{1,0:T(8,128)(2,1)} custom-call(f32[128,1024]{1,0:T(8,128)S(1)} %further.1.further_ref.partial_ref, bf16[128,256]{1,0:T(8,128)(2,1)S(1)} %rejoin.1.refs_0_, bf16[128,256]{1,0:T(8,128)(2,1)S(1)} %collective-permute-done.10.refs_1_, bf16[1024,1024]{1,0:T(8,128)(2,1)S(1)} %copy-done), custom_call_target="tpu_custom_call" | custom-call | tf_op jit(solution)/shard_map/project/pallas_call | solution.py:624
  (3 shorter events, 0.1 us)
Async XLA Ops:
  1.4 13.4 %collective-permute-start.1 = (bf16[2,224,256]{2,1,0:T(8,128)(2,1)S(1)}, bf16[2,224,256]{2,1,0:T(8,128)(2,1)S(1)}, u32[]{:S(2)}, u32[]{:S(2)}) collective-permute-start(bf16[2,224,256]{2,1,0:T(8,128)(2,1)S(1)} %get-tuple-element.35), channel_id=1, source_target_pairs={{0,4},{4,0},{8,12},{12,8},{16,20},{20,16},{24,28},{28,24},{1,5},{5... | collective-permute-start | bytes 688136 | tf_op jit(solution)/shard_map/ppermute | solution.py:449
  4.4 6.0 %copy-start.1 = (bf16[1,512,256]{2,1,0:T(8,128)(2,1)S(1)}, bf16[1,512,256]{2,1,0:T(8,128)(2,1)}, u32[]{:S(2)}) copy-start(bf16[1,512,256]{2,1,0:T(8,128)(2,1)} %param.4) | copy-start | bytes 786436
  4.5 6.0 %collective-permute-start = (bf16[2,32,256]{2,1,0:T(8,128)(2,1)S(1)}, bf16[2,32,256]{2,1,0:T(8,128)(2,1)S(1)}, u32[]{:S(2)}, u32[]{:S(2)}) collective-permute-start(bf16[2,32,256]{2,1,0:T(8,128)(2,1)S(1)} %get-tuple-element.31.four_ref), channel_id=1, source_target_pairs={{0,16},{4,20},{8,24},{12,28},{16,0},{20,4},{24,8},{28,12},{1,17},{... | collective-permute-start | bytes 98312 | tf_op jit(solution)/shard_map/ppermute | solution.py:449
  7.1 6.1 %collective-permute-start.6 = (bf16[2,32,256]{2,1,0:T(8,128)(2,1)S(1)}, bf16[2,32,256]{2,1,0:T(8,128)(2,1)S(1)}, u32[]{:S(2)}, u32[]{:S(2)}) collective-permute-start(bf16[2,32,256]{2,1,0:T(8,128)(2,1)S(1)} %get-tuple-element.31.four_ref), channel_id=1, source_target_pairs={{0,24},{4,28},{8,16},{12,20},{16,8},{20,12},{24,0},{28,4},{1,25},{... | collective-permute-start | bytes 98312 | tf_op jit(solution)/shard_map/ppermute | solution.py:449
  8.5 5.7 %collective-permute-start.2 = (bf16[2,64,256]{2,1,0:T(8,128)(2,1)S(1)}, bf16[2,64,256]{2,1,0:T(8,128)(2,1)S(1)}, u32[]{:S(2)}, u32[]{:S(2)}) collective-permute-start(bf16[2,64,256]{2,1,0:T(8,128)(2,1)S(1)} %get-tuple-element.36), channel_id=1, source_target_pairs={{0,12},{4,8},{8,4},{12,0},{16,28},{20,24},{24,20},{28,16},{1,13},{... | collective-permute-start | bytes 196616 | tf_op jit(solution)/shard_map/ppermute | solution.py:449
  8.7 6.1 %collective-permute-start.3 = (bf16[2,64,256]{2,1,0:T(8,128)(2,1)S(1)}, bf16[2,64,256]{2,1,0:T(8,128)(2,1)S(1)}, u32[]{:S(2)}, u32[]{:S(2)}) collective-permute-start(bf16[2,64,256]{2,1,0:T(8,128)(2,1)S(1)} %get-tuple-element.36), channel_id=1, source_target_pairs={{0,8},{4,12},{8,0},{12,4},{16,24},{20,28},{24,16},{28,20},{1,9},{5... | collective-permute-start | bytes 196616 | tf_op jit(solution)/shard_map/ppermute | solution.py:449
  10.5 4.8 %collective-permute-start.4 = (bf16[2,128,256]{2,1,0:T(8,128)(2,1)S(1)}, bf16[2,128,256]{2,1,0:T(8,128)(2,1)S(1)}, u32[]{:S(2)}, u32[]{:S(2)}) collective-permute-start(bf16[2,128,256]{2,1,0:T(8,128)(2,1)S(1)} %get-tuple-element.39), channel_id=1, source_target_pairs={{0,1},{1,0},{2,3},{3,2},{4,8},{5,9},{6,10},{7,11},{8,4},{9,5},{10,... | collective-permute-start | bytes 393224 | tf_op jit(solution)/shard_map/ppermute | solution.py:460
  13.2 4.3 %collective-permute-start.7 = (bf16[2,64,256]{2,1,0:T(8,128)(2,1)S(1)}, bf16[2,64,256]{2,1,0:T(8,128)(2,1)S(1)}, u32[]{:S(2)}, u32[]{:S(2)}) collective-permute-start(bf16[2,64,256]{2,1,0:T(8,128)(2,1)S(1)} %join.1.fours_a), channel_id=1, source_target_pairs={{0,4},{4,0},{8,12},{12,8},{16,20},{20,16},{24,28},{28,24},{1,5},{5... | collective-permute-start | bytes 196616 | tf_op jit(solution)/shard_map/ppermute | solution.py:449
  15.3 5.1 %copy-start = (bf16[1024,1024]{1,0:T(8,128)(2,1)S(1)}, bf16[1024,1024]{1,0:T(8,128)(2,1)}, u32[]{:S(2)}) copy-start(bf16[1024,1024]{1,0:T(8,128)(2,1)} %refs_2_.1) | copy-start | bytes 6291460
  16.2 4.4 %collective-permute-start.5 = (bf16[128,256]{1,0:T(8,128)(2,1)S(1)}, bf16[128,256]{1,0:T(8,128)(2,1)S(1)}, u32[]{:S(2)}, u32[]{:S(2)}) collective-permute-start(bf16[128,256]{1,0:T(8,128)(2,1)S(1)} %get-tuple-element.40), channel_id=1, source_target_pairs={{0,3},{1,2},{2,1},{3,0},{4,7},{5,6},{6,5},{7,4},{8,11},{9,10},{10,... | collective-permute-start | bytes 196616 | tf_op jit(solution)/shard_map/ppermute | solution.py:449
  18.1 4.4 %collective-permute-start.8 = (bf16[128,256]{1,0:T(8,128)(2,1)S(1)}, bf16[128,256]{1,0:T(8,128)(2,1)S(1)}, u32[]{:S(2)}, u32[]{:S(2)}) collective-permute-start(bf16[128,256]{1,0:T(8,128)(2,1)S(1)} %get-tuple-element.46), channel_id=1, source_target_pairs={{0,2},{1,3},{2,0},{3,1},{4,6},{5,7},{6,4},{7,5},{8,10},{9,11},{10,... | collective-permute-start | bytes 196616 | tf_op jit(solution)/shard_map/ppermute | solution.py:449
  19.6 3.2 %collective-permute-start.9 = (bf16[16,256]{1,0:T(8,128)(2,1)S(1)}, bf16[16,256]{1,0:T(8,128)(2,1)S(1)}, u32[]{:S(2)}, u32[]{:S(2)}) collective-permute-start(bf16[16,256]{1,0:T(8,128)(2,1)S(1)} %get-tuple-element.47), channel_id=1, source_target_pairs={{0,3},{1,2},{2,1},{3,0},{4,7},{5,6},{6,5},{7,4},{8,11},{9,10},{10,... | collective-permute-start | bytes 24584 | tf_op jit(solution)/shard_map/ppermute | solution.py:449
  20.0 3.0 %collective-permute-start.10 = (bf16[128,256]{1,0:T(8,128)(2,1)S(1)}, bf16[128,256]{1,0:T(8,128)(2,1)S(1)}, u32[]{:S(2)}, u32[]{:S(2)}) collective-permute-start(bf16[128,256]{1,0:T(8,128)(2,1)S(1)} %get-tuple-element.48), channel_id=1, source_target_pairs={{0,1},{1,0},{2,3},{3,2},{4,5},{5,4},{6,7},{7,6},{8,9},{9,8},{10,11... | collective-permute-start | bytes 196616 | tf_op jit(solution)/shard_map/ppermute | solution.py:449

commit v4 on v3

--- a/solution.py
+++ b/solution.py
@@ -41,9 +41,15 @@
         scratch[half] = source[:, half * PAIR : (half + 1) * PAIR].astype(jnp.float32)
 
 
-def pool_kernel(
-    k_hbm, v_hbm, k_ref, v_ref, first_ref, one_ref, two_ref, scratch, sems
-):
+def first_level(block):
+    row = lax.broadcasted_iota(jnp.int32, (BLOCK // 2, BLOCK), 0)
+    column = lax.broadcasted_iota(jnp.int32, (BLOCK // 2, BLOCK), 1)
+    pairs = column // 2 == FAN // 2 * (row % SLAB) + row // SLAB
+    sums = jnp.dot(pairs.astype(jnp.bfloat16), block, preferred_element_type=jnp.float32)
+    return (sums * root_half).astype(jnp.bfloat16)
+
+
+def pool_kernel(k_hbm, v_hbm, k_ref, v_ref, first_ref, one_ref, two_ref, sems):
     rows = k_ref.shape[0]
     blocks = rows // BLOCK
     arrivals = []
@@ -60,13 +66,9 @@
     for block, which, ref, copy in arrivals:
         if block % (blocks // 2) == 0:
             copy.wait()
-        here = pl.ds(block * BLOCK, BLOCK)
-        spill(ref.at[here, :], scratch.at[which, block])
-        for half in range(scratch.shape[2]):
-            lanes = pl.ds(half * PAIR, PAIR)
-            one = pooled_slabs(slabs_of(scratch.at[which, block, half], 0))
-            one_ref[which, pl.ds(block * BLOCK // 2, BLOCK // 2), lanes] = joined(one)
-            two_ref[which, pl.ds(block * BLOCK // 4, BLOCK // 4), lanes] = joined(pooled_slabs(one))
+        one = first_level(ref[pl.ds(block * BLOCK, BLOCK), :])
+        one_ref[which, pl.ds(block * BLOCK // 2, BLOCK // 2), :] = one
+        two_ref[which, pl.ds(block * BLOCK // 4, BLOCK // 4), :] = repooled(one)
     inner = rows // 4 - BLOCK // 4
     for which, ref in enumerate((k_ref, v_ref)):
         first_ref[which, :BLOCK, :] = jnp.where(even, ref[rows - BLOCK :, :], ref[:BLOCK, :])
@@ -202,17 +204,13 @@
 
 
 def coarse_kernel(
-    two_q, three_q, first_ref, three_a, three_b, coarse, near_ref, scratch, two_ref, two_hold, three_hold
+    two_q, three_q, first_ref, three_a, three_b, coarse, near_ref, two_ref, two_hold, three_hold
 ):
     inner = first_ref.shape[1] - BLOCK
-    pairs = scratch.shape[1]
+    pairs = two_q.shape[1] // PAIR
     two_ref[:, :inner, :] = first_ref[:, BLOCK:, :]
     for which in range(2):
-        spill(first_ref.at[which, pl.ds(0, BLOCK), :], scratch.at[which])
-        for half in range(pairs):
-            lanes = pl.ds(half * PAIR, PAIR)
-            slabs = slabs_of(scratch.at[which, half], 0)
-            two_ref[which, inner:, lanes] = joined(pooled_slabs(pooled_slabs(slabs)))
+        two_ref[which, inner:, :] = repooled(first_level(first_ref[which, :BLOCK, :]))
         near_ref[which] = repooled(repooled(two_ref[which]))
     steps = {}
     for pair in range(pairs):
@@ -483,7 +481,6 @@
             bf16(2, rows // 4, features),
         ],
         scratch_shapes=[
-            pltpu.VMEM((2, rows // BLOCK, pairs, BLOCK, PAIR), jnp.float32),
             pltpu.SemaphoreType.DMA((2, 2)),
         ],
         compiler_params=params,
@@ -539,7 +536,6 @@
             bf16(2, rows // 16, features),
         ],
         scratch_shapes=[
-            pltpu.VMEM((2, pairs, BLOCK, PAIR), jnp.float32),
             pltpu.VMEM((2, rows // 4, features), jnp.bfloat16),
             pltpu.VMEM((pairs, rows // 2, BLOCK), jnp.float32),
             pltpu.VMEM((pairs, rows // 4, BLOCK), jnp.float32),

time: 24.2 us -> 24.6 us (1.017)
  Pallas kernels: 6.84 us -> 7.16 us
  transfers between devices with their start and end apart: 11 -> 11, of which waited for: 4 -> 5; matrix products, arithmetic and copies ran while one was open for 0% -> 0% of each run, Pallas kernels for 18% -> 19%
where the time goes in v4:
time: 24.6 us; the launch traced here: 24.4 us
  starting transfers between devices  12.2 us (50%)
  Pallas kernels  7.16 us (29%)
  waiting for transfers between devices  4.91 us (20%)
    ppermute x10, starting transfers between devices, swapped(): lax.ppermute(block, axis, [(i, i ^ mask) for i in range(lax.axis_size(axi...  12.2 us
    ppermute x10, waiting for transfers between devices, swapped(): lax.ppermute(block, axis, [(i, i ^ mask) for i in range(lax.axis_size(axi...  4.91 us
    pallas_call x1, Pallas kernels, per_device(): pl.pallas_call(pool_kernel, in_specs=[hbm] * 2, out_shape=[bf16(rows, fea...  1.59 us
    pallas_call x1, Pallas kernels, per_device(): pl.pallas_call(local_kernel, out_shape=[bf16(2, BLOCK, features), bf16(ro...  1.55 us
    pallas_call x1, Pallas kernels, per_device(): pl.pallas_call(project_kernel, in_specs=[vmem] * (len(rejoined) + 3), out...  1.05 us
    pallas_call x1, Pallas kernels, per_device(): pl.pallas_call(mid_kernel, out_shape=[jax.ShapeDtypeStruct((2, rows, feat...  0.93 us
    pallas_call x1, Pallas kernels, per_device(): pl.pallas_call(coarse_kernel, out_shape=[jax.ShapeDtypeStruct((3, rows //...  0.62 us
    pallas_call x1, Pallas kernels, per_device(): pl.pallas_call(finish_kernel, out_shape=parts[2:] + [bf16(2 * SLAB, featu...  0.61 us
  transfers between devices with their start and end apart: 11, of which 5 were waited for; matrix products, arithmetic and copies ran while one was open for 0% of the time, Pallas kernels for 19%

profile of v4, /device:TPU:0, one launch (start us, length us, event | category | flops | bytes accessed | tf_op | source)
XLA Modules:
  0.0 24.4 jit_solution(7038342392866557932)
XLA Ops:
  0.0 1.6 %pool.1 = (bf16[512,256]{1,0:T(8,128)(2,1)S(1)}, bf16[512,256]{1,0:T(8,128)(2,1)S(1)}, bf16[2,224,256]{2,1,0:T(8,128)(2,1)S(1)}, bf16[2,256,256]{2,1,0:T(8,128)(2,1)S(1)}, bf16[2,128,256]{2,1,0:T(8,128)(2,1)S(1)}) custom-call(bf16[1,512,256]{2,1,0:T(8,128)(2,1)} %k_hbm.1, bf16[1,512,256]{2,1,0:T(8,128)(2,1)} %v_hbm.1), custom_call_target="tpu_custom_call" | custom-call | tf_op jit(solution)/shard_map/pool/pallas_call | solution.py:473
  1.6 3.0 %collective-permute-start.1 = (bf16[2,224,256]{2,1,0:T(8,128)(2,1)S(1)}, bf16[2,224,256]{2,1,0:T(8,128)(2,1)S(1)}, u32[]{:S(2)}, u32[]{:S(2)}) collective-permute-start(bf16[2,224,256]{2,1,0:T(8,128)(2,1)S(1)} %get-tuple-element.35), channel_id=1, source_target_pairs={{0,4},{4,0},{8,12},{12,8},{16,20},{20,16},{24,28},{28,24},{1,5},{5... | collective-permute-start | bytes 688136 | tf_op jit(solution)/shard_map/ppermute | solution.py:447
  4.6 0.0 copy-start.1
  4.7 2.7 %collective-permute-start = (bf16[2,32,256]{2,1,0:T(8,128)(2,1)S(1)}, bf16[2,32,256]{2,1,0:T(8,128)(2,1)S(1)}, u32[]{:S(2)}, u32[]{:S(2)}) collective-permute-start(bf16[2,32,256]{2,1,0:T(8,128)(2,1)S(1)} %get-tuple-element.31.four_ref), channel_id=1, source_target_pairs={{0,16},{4,20},{8,24},{12,28},{16,0},{20,4},{24,8},{28,12},{1,17},{... | collective-permute-start | bytes 98312 | tf_op jit(solution)/shard_map/ppermute | solution.py:447
  7.3 1.3 %collective-permute-start.6 = (bf16[2,32,256]{2,1,0:T(8,128)(2,1)S(1)}, bf16[2,32,256]{2,1,0:T(8,128)(2,1)S(1)}, u32[]{:S(2)}, u32[]{:S(2)}) collective-permute-start(bf16[2,32,256]{2,1,0:T(8,128)(2,1)S(1)} %get-tuple-element.31.four_ref), channel_id=1, source_target_pairs={{0,24},{4,28},{8,16},{12,20},{16,8},{20,12},{24,0},{28,4},{1,25},{... | collective-permute-start | bytes 98312 | tf_op jit(solution)/shard_map/ppermute | solution.py:447
  8.7 0.2 collective-permute-start.2
  8.9 1.8 %collective-permute-start.3 = (bf16[2,64,256]{2,1,0:T(8,128)(2,1)S(1)}, bf16[2,64,256]{2,1,0:T(8,128)(2,1)S(1)}, u32[]{:S(2)}, u32[]{:S(2)}) collective-permute-start(bf16[2,64,256]{2,1,0:T(8,128)(2,1)S(1)} %get-tuple-element.36), channel_id=1, source_target_pairs={{0,8},{4,12},{8,0},{12,4},{16,24},{20,28},{24,16},{28,20},{1,9},{5... | collective-permute-start | bytes 196616 | tf_op jit(solution)/shard_map/ppermute | solution.py:447
  10.7 0.0 collective-permute-done.four_ref
  10.7 0.0 collective-permute-start.4
  10.7 0.0 copy-done.1
  10.7 1.5 %local.1 = (bf16[2,128,256]{2,1,0:T(8,128)(2,1)S(1)}, bf16[128,256]{1,0:T(8,128)(2,1)S(1)}, bf16[64,256]{1,0:T(8,128)(2,1)S(1)}, bf16[32,256]{1,0:T(8,128)(2,1)S(1)}, f32[3,512,256]{2,1,0:T(8,128)S(1)}) custom-call(bf16[512,256]{1,0:T(8,128)(2,1)S(1)} %bitcast.2, bf16[512,256]{1,0:T(8,128)(2,1)S(1)} %get-tuple-element.27.k_ref, ...), custom_call_target="tpu_custom_call" | custom-call | tf_op jit(solution)/shard_map/local/pallas_call | solution.py:506
  12.2 1.2 %collective-permute-done.6.six_ref = bf16[2,32,256]{2,1,0:T(8,128)(2,1)S(1)} collective-permute-done((bf16[2,32,256]{2,1,0:T(8,128)(2,1)S(1)}, bf16[2,32,256]{2,1,0:T(8,128)(2,1)S(1)}, u32[]{:S(2)}, u32[]{:S(2)}) %collective-permute-start.6) | collective-permute-done | bytes 32800 | tf_op jit(solution)/shard_map/ppermute | solution.py:447
  13.4 0.9 %collective-permute-start.7 = (bf16[2,64,256]{2,1,0:T(8,128)(2,1)S(1)}, bf16[2,64,256]{2,1,0:T(8,128)(2,1)S(1)}, u32[]{:S(2)}, u32[]{:S(2)}) collective-permute-start(bf16[2,64,256]{2,1,0:T(8,128)(2,1)S(1)} %join.1.fours_a), channel_id=1, source_target_pairs={{0,4},{4,0},{8,12},{12,8},{16,20},{20,16},{24,28},{28,24},{1,5},{5... | collective-permute-start | bytes 196616 | tf_op jit(solution)/shard_map/ppermute | solution.py:447
  14.3 0.0 collective-permute-done.2.three_a
  14.4 0.6 %collective-permute-done.3.three_b = bf16[2,64,256]{2,1,0:T(8,128)(2,1)S(1)} collective-permute-done((bf16[2,64,256]{2,1,0:T(8,128)(2,1)S(1)}, bf16[2,64,256]{2,1,0:T(8,128)(2,1)S(1)}, u32[]{:S(2)}, u32[]{:S(2)}) %collective-permute-start.3) | collective-permute-done | bytes 65568 | tf_op jit(solution)/shard_map/ppermute | solution.py:447
  15.0 0.0 collective-permute-done.1.first_ref
  15.0 0.6 %coarse.1 = (f32[3,128,256]{2,1,0:T(8,128)S(1)}, bf16[2,32,256]{2,1,0:T(8,128)(2,1)S(1)}) custom-call(bf16[128,256]{1,0:T(8,128)(2,1)S(1)} %get-tuple-element.33.two_q, bf16[64,256]{1,0:T(8,128)(2,1)S(1)} %get-tuple-element.34.three_q, bf16[2,224,256]{2,1,0:T(8,128)(2,1)S(1)} %collective-permute-done.1.first_ref, ...), custom_call_target="tpu_custom_call" | custom-call | flops 2147483648 | bytes 2097152 | tf_op jit(solution)/shard_map/coarse/pallas_call | solution.py:532
  15.6 0.0 collective-permute-done.4.second_ref
  15.6 0.0 copy-start
  15.6 0.9 %mid.1 = (f32[2,512,256]{2,1,0:T(8,128)S(1)}, bf16[128,256]{1,0:T(8,128)(2,1)S(1)}) custom-call(bf16[2,128,256]{2,1,0:T(8,128)(2,1)S(1)} %get-tuple-element.32.edge_q, f32[3,128,256]{2,1,0:T(8,128)S(1)} %get-tuple-element.37.coarse, f32[3,512,256]{2,1,0:T(8,128)S(1)} %get-tuple-element.38.state, bf16[2,224,256]{2,1,0:T(8,128)(2,1)S(1)} %collective-permute-done.1.first_ref, ...), custom_call_target="tpu_custom_call" | custom-call | tf_op jit(solution)/shard_map/mid/pallas_call | solution.py:548
  16.5 0.1 collective-permute-start.5
  16.6 1.1 %collective-permute-done.7.fours_b = bf16[2,64,256]{2,1,0:T(8,128)(2,1)S(1)} collective-permute-done((bf16[2,64,256]{2,1,0:T(8,128)(2,1)S(1)}, bf16[2,64,256]{2,1,0:T(8,128)(2,1)S(1)}, u32[]{:S(2)}, u32[]{:S(2)}) %collective-permute-start.7) | collective-permute-done | bytes 65568 | tf_op jit(solution)/shard_map/ppermute | solution.py:447
  17.7 0.6 %finish.1 = (bf16[128,256]{1,0:T(8,128)(2,1)S(1)}, bf16[16,256]{1,0:T(8,128)(2,1)S(1)}, f32[2,32,256]{2,1,0:T(8,128)S(1)}) custom-call(bf16[32,256]{1,0:T(8,128)(2,1)S(1)} %get-tuple-element.42.query_ref.four_q, f32[2,512,256]{2,1,0:T(8,128)S(1)} %get-tuple-element.41.fine, bf16[2,32,256]{2,1,0:T(8,128)(2,1)S(1)} %get-tuple-element.31.four_ref, ...), custom_call_target="tpu_custom_call" | custom-call | tf_op jit(solution)/shard_map/finish/pallas_call | solution.py:573
  18.3 1.5 %collective-permute-start.8 = (bf16[128,256]{1,0:T(8,128)(2,1)S(1)}, bf16[128,256]{1,0:T(8,128)(2,1)S(1)}, u32[]{:S(2)}, u32[]{:S(2)}) collective-permute-start(bf16[128,256]{1,0:T(8,128)(2,1)S(1)} %get-tuple-element.46), channel_id=1, source_target_pairs={{0,2},{1,3},{2,0},{3,1},{4,6},{5,7},{6,4},{7,5},{8,10},{9,11},{10,... | collective-permute-start | bytes 196616 | tf_op jit(solution)/shard_map/ppermute | solution.py:447
  19.8 0.4 %collective-permute-start.9 = (bf16[16,256]{1,0:T(8,128)(2,1)S(1)}, bf16[16,256]{1,0:T(8,128)(2,1)S(1)}, u32[]{:S(2)}, u32[]{:S(2)}) collective-permute-start(bf16[16,256]{1,0:T(8,128)(2,1)S(1)} %get-tuple-element.47), channel_id=1, source_target_pairs={{0,3},{1,2},{2,1},{3,0},{4,7},{5,6},{6,5},{7,4},{8,11},{9,10},{10,... | collective-permute-start | bytes 24584 | tf_op jit(solution)/shard_map/ppermute | solution.py:447
  20.2 0.1 rest.1
  20.3 0.3 %collective-permute-start.10 = (bf16[128,256]{1,0:T(8,128)(2,1)S(1)}, bf16[128,256]{1,0:T(8,128)(2,1)S(1)}, u32[]{:S(2)}, u32[]{:S(2)}) collective-permute-start(bf16[128,256]{1,0:T(8,128)(2,1)S(1)} %get-tuple-element.48), channel_id=1, source_target_pairs={{0,1},{1,0},{2,3},{3,2},{4,5},{5,4},{6,7},{7,6},{8,9},{9,8},{10,11... | collective-permute-start | bytes 196616 | tf_op jit(solution)/shard_map/ppermute | solution.py:447
  20.6 0.0 copy-done
  20.6 0.2 partial.1.partial_ref
  20.8 0.1 collective-permute-done.5.refs_0_
  21.0 1.9 %collective-permute-done.8.refs_0_ = bf16[128,256]{1,0:T(8,128)(2,1)S(1)} collective-permute-done((bf16[128,256]{1,0:T(8,128)(2,1)S(1)}, bf16[128,256]{1,0:T(8,128)(2,1)S(1)}, u32[]{:S(2)}, u32[]{:S(2)}) %collective-permute-start.8) | collective-permute-done | bytes 65568 | tf_op jit(solution)/shard_map/ppermute | solution.py:447
  22.9 0.2 further.1.further_ref.partial_ref
  23.1 0.0 collective-permute-done.9.refs_1_
  23.1 0.2 rejoin.1.refs_0_
  23.4 0.0 collective-permute-done.10.refs_1_
  23.4 1.0 %project.1 = bf16[128,1024]{1,0:T(8,128)(2,1)} custom-call(f32[128,1024]{1,0:T(8,128)S(1)} %further.1.further_ref.partial_ref, bf16[128,256]{1,0:T(8,128)(2,1)S(1)} %rejoin.1.refs_0_, bf16[128,256]{1,0:T(8,128)(2,1)S(1)} %collective-permute-done.10.refs_1_, bf16[1024,1024]{1,0:T(8,128)(2,1)S(1)} %copy-done), custom_call_target="tpu_custom_call" | custom-call | tf_op jit(solution)/shard_map/project/pallas_call | solution.py:620
  (3 shorter events, 0.1 us)
Async XLA Ops:
  1.6 13.4 %collective-permute-start.1 = (bf16[2,224,256]{2,1,0:T(8,128)(2,1)S(1)}, bf16[2,224,256]{2,1,0:T(8,128)(2,1)S(1)}, u32[]{:S(2)}, u32[]{:S(2)}) collective-permute-start(bf16[2,224,256]{2,1,0:T(8,128)(2,1)S(1)} %get-tuple-element.35), channel_id=1, source_target_pairs={{0,4},{4,0},{8,12},{12,8},{16,20},{20,16},{24,28},{28,24},{1,5},{5... | collective-permute-start | bytes 688136 | tf_op jit(solution)/shard_map/ppermute | solution.py:447
  4.6 6.0 %copy-start.1 = (bf16[1,512,256]{2,1,0:T(8,128)(2,1)S(1)}, bf16[1,512,256]{2,1,0:T(8,128)(2,1)}, u32[]{:S(2)}) copy-start(bf16[1,512,256]{2,1,0:T(8,128)(2,1)} %param.4) | copy-start | bytes 786436
  4.7 6.0 %collective-permute-start = (bf16[2,32,256]{2,1,0:T(8,128)(2,1)S(1)}, bf16[2,32,256]{2,1,0:T(8,128)(2,1)S(1)}, u32[]{:S(2)}, u32[]{:S(2)}) collective-permute-start(bf16[2,32,256]{2,1,0:T(8,128)(2,1)S(1)} %get-tuple-element.31.four_ref), channel_id=1, source_target_pairs={{0,16},{4,20},{8,24},{12,28},{16,0},{20,4},{24,8},{28,12},{1,17},{... | collective-permute-start | bytes 98312 | tf_op jit(solution)/shard_map/ppermute | solution.py:447
  7.3 6.1 %collective-permute-start.6 = (bf16[2,32,256]{2,1,0:T(8,128)(2,1)S(1)}, bf16[2,32,256]{2,1,0:T(8,128)(2,1)S(1)}, u32[]{:S(2)}, u32[]{:S(2)}) collective-permute-start(bf16[2,32,256]{2,1,0:T(8,128)(2,1)S(1)} %get-tuple-element.31.four_ref), channel_id=1, source_target_pairs={{0,24},{4,28},{8,16},{12,20},{16,8},{20,12},{24,0},{28,4},{1,25},{... | collective-permute-start | bytes 98312 | tf_op jit(solution)/shard_map/ppermute | solution.py:447
  8.7 5.7 %collective-permute-start.2 = (bf16[2,64,256]{2,1,0:T(8,128)(2,1)S(1)}, bf16[2,64,256]{2,1,0:T(8,128)(2,1)S(1)}, u32[]{:S(2)}, u32[]{:S(2)}) collective-permute-start(bf16[2,64,256]{2,1,0:T(8,128)(2,1)S(1)} %get-tuple-element.36), channel_id=1, source_target_pairs={{0,12},{4,8},{8,4},{12,0},{16,28},{20,24},{24,20},{28,16},{1,13},{... | collective-permute-start | bytes 196616 | tf_op jit(solution)/shard_map/ppermute | solution.py:447
  8.9 6.1 %collective-permute-start.3 = (bf16[2,64,256]{2,1,0:T(8,128)(2,1)S(1)}, bf16[2,64,256]{2,1,0:T(8,128)(2,1)S(1)}, u32[]{:S(2)}, u32[]{:S(2)}) collective-permute-start(bf16[2,64,256]{2,1,0:T(8,128)(2,1)S(1)} %get-tuple-element.36), channel_id=1, source_target_pairs={{0,8},{4,12},{8,0},{12,4},{16,24},{20,28},{24,16},{28,20},{1,9},{5... | collective-permute-start | bytes 196616 | tf_op jit(solution)/shard_map/ppermute | solution.py:447
  10.7 4.9 %collective-permute-start.4 = (bf16[2,128,256]{2,1,0:T(8,128)(2,1)S(1)}, bf16[2,128,256]{2,1,0:T(8,128)(2,1)S(1)}, u32[]{:S(2)}, u32[]{:S(2)}) collective-permute-start(bf16[2,128,256]{2,1,0:T(8,128)(2,1)S(1)} %get-tuple-element.39), channel_id=1, source_target_pairs={{0,1},{1,0},{2,3},{3,2},{4,8},{5,9},{6,10},{7,11},{8,4},{9,5},{10,... | collective-permute-start | bytes 393224 | tf_op jit(solution)/shard_map/ppermute | solution.py:458
  13.4 4.3 %collective-permute-start.7 = (bf16[2,64,256]{2,1,0:T(8,128)(2,1)S(1)}, bf16[2,64,256]{2,1,0:T(8,128)(2,1)S(1)}, u32[]{:S(2)}, u32[]{:S(2)}) collective-permute-start(bf16[2,64,256]{2,1,0:T(8,128)(2,1)S(1)} %join.1.fours_a), channel_id=1, source_target_pairs={{0,4},{4,0},{8,12},{12,8},{16,20},{20,16},{24,28},{28,24},{1,5},{5... | collective-permute-start | bytes 196616 | tf_op jit(solution)/shard_map/ppermute | solution.py:447
  15.6 5.0 %copy-start = (bf16[1024,1024]{1,0:T(8,128)(2,1)S(1)}, bf16[1024,1024]{1,0:T(8,128)(2,1)}, u32[]{:S(2)}) copy-start(bf16[1024,1024]{1,0:T(8,128)(2,1)} %refs_2_.1) | copy-start | bytes 6291460
  16.5 4.4 %collective-permute-start.5 = (bf16[128,256]{1,0:T(8,128)(2,1)S(1)}, bf16[128,256]{1,0:T(8,128)(2,1)S(1)}, u32[]{:S(2)}, u32[]{:S(2)}) collective-permute-start(bf16[128,256]{1,0:T(8,128)(2,1)S(1)} %get-tuple-element.40), channel_id=1, source_target_pairs={{0,3},{1,2},{2,1},{3,0},{4,7},{5,6},{6,5},{7,4},{8,11},{9,10},{10,... | collective-permute-start | bytes 196616 | tf_op jit(solution)/shard_map/ppermute | solution.py:447
  18.3 4.6 %collective-permute-start.8 = (bf16[128,256]{1,0:T(8,128)(2,1)S(1)}, bf16[128,256]{1,0:T(8,128)(2,1)S(1)}, u32[]{:S(2)}, u32[]{:S(2)}) collective-permute-start(bf16[128,256]{1,0:T(8,128)(2,1)S(1)} %get-tuple-element.46), channel_id=1, source_target_pairs={{0,2},{1,3},{2,0},{3,1},{4,6},{5,7},{6,4},{7,5},{8,10},{9,11},{10,... | collective-permute-start | bytes 196616 | tf_op jit(solution)/shard_map/ppermute | solution.py:447
  19.8 3.4 %collective-permute-start.9 = (bf16[16,256]{1,0:T(8,128)(2,1)S(1)}, bf16[16,256]{1,0:T(8,128)(2,1)S(1)}, u32[]{:S(2)}, u32[]{:S(2)}) collective-permute-start(bf16[16,256]{1,0:T(8,128)(2,1)S(1)} %get-tuple-element.47), channel_id=1, source_target_pairs={{0,3},{1,2},{2,1},{3,0},{4,7},{5,6},{6,5},{7,4},{8,11},{9,10},{10,... | collective-permute-start | bytes 24584 | tf_op jit(solution)/shard_map/ppermute | solution.py:447
  20.3 3.1 %collective-permute-start.10 = (bf16[128,256]{1,0:T(8,128)(2,1)S(1)}, bf16[128,256]{1,0:T(8,128)(2,1)S(1)}, u32[]{:S(2)}, u32[]{:S(2)}) collective-permute-start(bf16[128,256]{1,0:T(8,128)(2,1)S(1)} %get-tuple-element.48), channel_id=1, source_target_pairs={{0,1},{1,0},{2,3},{3,2},{4,5},{5,4},{6,7},{7,6},{8,9},{9,8},{10,11... | collective-permute-start | bytes 196616 | tf_op jit(solution)/shard_map/ppermute | solution.py:447

commit v5 on v1

--- a/solution.py
+++ b/solution.py
@@ -16,7 +16,7 @@
 log2_e = 1.4426950408889634
 log2_scale = HD**-0.5 * log2_e
 least_share = 2.0**-100
-AHEAD = 3
+AHEAD = 2
 
 FAN = 2**LEVELS
 
@@ -361,7 +361,7 @@
     finish_blocks(fine, coarse, enumerate(outs))
 
 
-def rejoin_kernel(*refs):
+def rejoin_kernel(partial_ref, *refs):
     outs = refs[len(refs) // 3 * 2 :]
     for early, late_ref, out in zip(refs, refs[len(outs) :], outs):
         features = early.shape[1]
@@ -387,12 +387,6 @@
         out[...] = ref[...].astype(jnp.float32)
 
 
-def carry_kernel(whole_ref, *refs):
-    half = len(refs) // 2
-    for ref, out in zip(refs[:half], refs[half:]):
-        out[...] = ref[...]
-
-
 def partial_kernel(own_ref, weight_ref, out_ref):
     features = own_ref.shape[1]
     start = pl.multiple_of(lax.axis_index("head") * features, features)
@@ -410,7 +404,7 @@
     for index in range(staged.shape[0]):
         columns = pl.ds(index * chunk, chunk)
         total = partial_ref[:, columns]
-        for step, part in zip([*range(2, len(parts) + 1), 1], parts):
+        for step, part in zip([*range(AHEAD, AHEAD + len(parts) - 1), 1], parts):
             start = pl.multiple_of((own ^ step) * features, features)
             total += jnp.dot(
                 part[...],
@@ -569,15 +563,13 @@
     parts = [bf16(BLOCK, features) for _ in range(AHEAD)]
     *outs, level_four = pl.pallas_call(
         finish_kernel,
-        out_shape=parts[2:]
-        + [bf16(2 * SLAB, features) for _ in away]
+        out_shape=[bf16(2 * SLAB, features) for _ in away]
         + [jax.ShapeDtypeStruct((2, rows // 16, features), jnp.float32)],
         scratch_shapes=[pltpu.VMEM((pairs, rows // 8, rows // 16 * seq_count), jnp.float32)],
         compiler_params=params,
         name="finish",
     )(four_q, fine, four, near, *threes_in, fours, fours_in, *far)
-    whole_in = [swapped(part, "head", step) for step, part in zip(range(2, AHEAD), outs)]
-    late_in = [swapped(part, "head", step) for step, part in zip(away, outs[AHEAD - 2 :])]
+    late_in = [swapped(part, "head", step) for step, part in zip(away, outs)]
     own_part, next_part = pl.pallas_call(
         rest_kernel,
         out_shape=parts[:2],
@@ -599,24 +591,18 @@
         compiler_params=params,
         cost_estimate=pl.CostEstimate(flops=2**22, bytes_accessed=2**10, transcendentals=0),
         name="widen",
-    )(*early_in)
-    widened = pl.pallas_call(
-        carry_kernel,
-        out_shape=[jax.ShapeDtypeStruct((BLOCK, features), jnp.float32) for _ in away],
-        compiler_params=params,
-        name="carry",
-    )(whole_in[0], *widened)
+    )(*early_in[::-1])
     rejoined = pl.pallas_call(
         rejoin_kernel,
         out_shape=[bf16(BLOCK, features) for _ in away],
         compiler_params=params,
         cost_estimate=heavy,
         name="rejoin",
-    )(*widened, *late_in)
+    )(partial, *widened, *late_in[::-1])
     chunk = 2 * PAIR
     result = pl.pallas_call(
         project_kernel,
-        in_specs=[vmem] * (head_count + 1),
+        in_specs=[vmem] * (len(rejoined) + 3),
         out_specs=hbm,
         out_shape=bf16(BLOCK, width),
         scratch_shapes=[
@@ -626,7 +612,7 @@
         ],
         compiler_params=params,
         name="project",
-    )(partial, *whole_in, *rejoined, next_in, out_weight)
+    )(partial, *rejoined[::-1], next_in, out_weight)
     return result[None]
 
 

time: 24.2 us -> 24.6 us (1.017)
  the two profiles are of different devices: /device:TPU:0 before, /device:TPU:5 now
where the time goes in v5:
time: 24.6 us; the launch traced here: 24.5 us
  starting transfers between devices  13.6 us (55%)
  Pallas kernels  6.76 us (27%)
  waiting for transfers between devices  3.96 us (16%)
    ppermute x11, starting transfers between devices, swapped(): lax.ppermute(block, axis, [(i, i ^ mask) for i in range(lax.axis_size(axi...  13.5 us
    ppermute x11, waiting for transfers between devices, swapped(): lax.ppermute(block, axis, [(i, i ^ mask) for i in range(lax.axis_size(axi...  2.01 us
    ppermute x1, waiting for transfers between devices, across(): return lax.ppermute(block, ('seq', 'head'), route)  1.95 us
    pallas_call x1, Pallas kernels, per_device(): pl.pallas_call(local_kernel, out_shape=[bf16(2, BLOCK, features), bf16(ro...  1.54 us
    pallas_call x1, Pallas kernels, per_device(): pl.pallas_call(pool_kernel, in_specs=[hbm] * 2, out_shape=[bf16(rows, fea...  1.39 us
    pallas_call x1, Pallas kernels, per_device(): pl.pallas_call(project_kernel, in_specs=[vmem] * (len(rejoined) + 3), out...  1.12 us
    pallas_call x1, Pallas kernels, per_device(): pl.pallas_call(mid_kernel, out_shape=[jax.ShapeDtypeStruct((2, rows, feat...  0.93 us
    pallas_call x1, Pallas kernels, per_device(): pl.pallas_call(finish_kernel, out_shape=[bf16(2 * SLAB, features) for _ i...  0.62 us
  transfers between devices with their start and end apart: 12, of which 4 were waited for; matrix products, arithmetic and copies ran while one was open for 0% of the time, Pallas kernels for 17%

profile of v5, /device:TPU:5, one launch (start us, length us, event | category | flops | bytes accessed | tf_op | source)
XLA Modules:
  0.0 24.5 jit_solution(17088682389770552957)
XLA Ops:
  0.0 1.4 %pool.1 = (bf16[512,256]{1,0:T(8,128)(2,1)S(1)}, bf16[512,256]{1,0:T(8,128)(2,1)S(1)}, bf16[2,224,256]{2,1,0:T(8,128)(2,1)S(1)}, bf16[2,256,256]{2,1,0:T(8,128)(2,1)S(1)}, bf16[2,128,256]{2,1,0:T(8,128)(2,1)S(1)}) custom-call(bf16[1,512,256]{2,1,0:T(8,128)(2,1)} %k_hbm.1, bf16[1,512,256]{2,1,0:T(8,128)(2,1)} %v_hbm.1), custom_call_target="tpu_custom_call" | custom-call | tf_op jit(solution)/shard_map/pool/pallas_call | solution.py:462
  1.4 0.1 collective-permute-start.1
  1.5 0.0 copy-start.1
  1.5 2.6 %collective-permute-start = (bf16[2,32,256]{2,1,0:T(8,128)(2,1)S(1)}, bf16[2,32,256]{2,1,0:T(8,128)(2,1)S(1)}, u32[]{:S(2)}, u32[]{:S(2)}) collective-permute-start(bf16[2,32,256]{2,1,0:T(8,128)(2,1)S(1)} %get-tuple-element.36.four_ref), channel_id=1, source_target_pairs={{0,16},{4,20},{8,24},{12,28},{16,0},{20,4},{24,8},{28,12},{1,17},{... | collective-permute-start | bytes 98312 | tf_op jit(solution)/shard_map/ppermute | solution.py:436
  4.1 1.1 %collective-permute-start.5 = (bf16[2,32,256]{2,1,0:T(8,128)(2,1)S(1)}, bf16[2,32,256]{2,1,0:T(8,128)(2,1)S(1)}, u32[]{:S(2)}, u32[]{:S(2)}) collective-permute-start(bf16[2,32,256]{2,1,0:T(8,128)(2,1)S(1)} %get-tuple-element.36.four_ref), channel_id=1, source_target_pairs={{0,24},{4,28},{8,16},{12,20},{16,8},{20,12},{24,0},{28,4},{1,25},{... | collective-permute-start | bytes 98312 | tf_op jit(solution)/shard_map/ppermute | solution.py:436
  5.2 1.2 %collective-permute-start.2 = (bf16[2,64,256]{2,1,0:T(8,128)(2,1)S(1)}, bf16[2,64,256]{2,1,0:T(8,128)(2,1)S(1)}, u32[]{:S(2)}, u32[]{:S(2)}) collective-permute-start(bf16[2,64,256]{2,1,0:T(8,128)(2,1)S(1)} %get-tuple-element.41), channel_id=1, source_target_pairs={{0,12},{4,8},{8,4},{12,0},{16,28},{20,24},{24,20},{28,16},{1,13},{... | collective-permute-start | bytes 196616 | tf_op jit(solution)/shard_map/ppermute | solution.py:436
  6.4 1.3 %collective-permute-start.3 = (bf16[2,64,256]{2,1,0:T(8,128)(2,1)S(1)}, bf16[2,64,256]{2,1,0:T(8,128)(2,1)S(1)}, u32[]{:S(2)}, u32[]{:S(2)}) collective-permute-start(bf16[2,64,256]{2,1,0:T(8,128)(2,1)S(1)} %get-tuple-element.41), channel_id=1, source_target_pairs={{0,8},{4,12},{8,0},{12,4},{16,24},{20,28},{24,16},{28,20},{1,9},{5... | collective-permute-start | bytes 196616 | tf_op jit(solution)/shard_map/ppermute | solution.py:436
  7.6 0.0 collective-permute-done.four_ref
  7.6 0.2 collective-permute-start.4
  7.8 0.0 copy-done.1
  7.8 1.5 %local.1 = (bf16[2,128,256]{2,1,0:T(8,128)(2,1)S(1)}, bf16[128,256]{1,0:T(8,128)(2,1)S(1)}, bf16[64,256]{1,0:T(8,128)(2,1)S(1)}, bf16[32,256]{1,0:T(8,128)(2,1)S(1)}, f32[3,512,256]{2,1,0:T(8,128)S(1)}) custom-call(bf16[512,256]{1,0:T(8,128)(2,1)S(1)} %bitcast.2, bf16[512,256]{1,0:T(8,128)(2,1)S(1)} %get-tuple-element.32.k_ref, ...), custom_call_target="tpu_custom_call" | custom-call | tf_op jit(solution)/shard_map/local/pallas_call | solution.py:496
  9.3 0.0 collective-permute-done.5.six_ref
  9.4 2.2 %collective-permute-start.6 = (bf16[2,64,256]{2,1,0:T(8,128)(2,1)S(1)}, bf16[2,64,256]{2,1,0:T(8,128)(2,1)S(1)}, u32[]{:S(2)}, u32[]{:S(2)}) collective-permute-start(bf16[2,64,256]{2,1,0:T(8,128)(2,1)S(1)} %join.1.fours_a), channel_id=1, source_target_pairs={{0,4},{4,0},{8,12},{12,8},{16,20},{20,16},{24,28},{28,24},{1,5},{5... | collective-permute-start | bytes 196616 | tf_op jit(solution)/shard_map/ppermute | solution.py:436
  11.6 0.0 collective-permute-done.2.three_a
  11.6 0.0 collective-permute-done.3.three_b
  11.6 0.0 collective-permute-done.1.first_ref
  11.6 0.5 %coarse.1 = (f32[3,128,256]{2,1,0:T(8,128)S(1)}, bf16[2,32,256]{2,1,0:T(8,128)(2,1)S(1)}) custom-call(bf16[128,256]{1,0:T(8,128)(2,1)S(1)} %get-tuple-element.38.two_q, bf16[64,256]{1,0:T(8,128)(2,1)S(1)} %get-tuple-element.39.three_q, bf16[2,224,256]{2,1,0:T(8,128)(2,1)S(1)} %collective-permute-done.1.first_ref, ...), custom_call_target="tpu_custom_call" | custom-call | flops 2147483648 | bytes 2097152 | tf_op jit(solution)/shard_map/coarse/pallas_call | solution.py:522
  12.1 2.0 %collective-permute-done.4.second_ref = bf16[2,128,256]{2,1,0:T(8,128)(2,1)S(1)} collective-permute-done((bf16[2,128,256]{2,1,0:T(8,128)(2,1)S(1)}, bf16[2,128,256]{2,1,0:T(8,128)(2,1)S(1)}, u32[]{:S(2)}, u32[]{:S(2)}) %collective-permute-start.4) | collective-permute-done | bytes 131104 | tf_op jit(solution)/shard_map/ppermute | solution.py:447
  14.0 0.0 copy-start
  14.0 0.9 %mid.1 = (f32[2,512,256]{2,1,0:T(8,128)S(1)}, bf16[128,256]{1,0:T(8,128)(2,1)S(1)}, bf16[128,256]{1,0:T(8,128)(2,1)S(1)}) custom-call(bf16[2,128,256]{2,1,0:T(8,128)(2,1)S(1)} %get-tuple-element.37.edge_q, f32[3,128,256]{2,1,0:T(8,128)S(1)} %get-tuple-element.42.coarse, f32[3,512,256]{2,1,0:T(8,128)S(1)} %get-tuple-element.43.state, ...), custom_call_target="tpu_custom_call" | custom-call | tf_op jit(solution)/shard_map/mid/pallas_call | solution.py:539
  15.0 3.0 %collective-permute-start.7 = (bf16[128,256]{1,0:T(8,128)(2,1)S(1)}, bf16[128,256]{1,0:T(8,128)(2,1)S(1)}, u32[]{:S(2)}, u32[]{:S(2)}) collective-permute-start(bf16[128,256]{1,0:T(8,128)(2,1)S(1)} %get-tuple-element.50), channel_id=1, source_target_pairs={{0,3},{1,2},{2,1},{3,0},{4,7},{5,6},{6,5},{7,4},{8,11},{9,10},{10,... | collective-permute-start | bytes 196616 | tf_op jit(solution)/shard_map/ppermute | solution.py:436
  17.9 0.3 %collective-permute-start.8 = (bf16[128,256]{1,0:T(8,128)(2,1)S(1)}, bf16[128,256]{1,0:T(8,128)(2,1)S(1)}, u32[]{:S(2)}, u32[]{:S(2)}) collective-permute-start(bf16[128,256]{1,0:T(8,128)(2,1)S(1)} %get-tuple-element.51), channel_id=1, source_target_pairs={{0,2},{1,3},{2,0},{3,1},{4,6},{5,7},{6,4},{7,5},{8,10},{9,11},{10,... | collective-permute-start | bytes 196616 | tf_op jit(solution)/shard_map/ppermute | solution.py:436
  18.2 0.0 collective-permute-done.6.fours_b
  18.2 0.6 %finish.1 = (bf16[16,256]{1,0:T(8,128)(2,1)S(1)}, bf16[16,256]{1,0:T(8,128)(2,1)S(1)}, f32[2,32,256]{2,1,0:T(8,128)S(1)}) custom-call(bf16[32,256]{1,0:T(8,128)(2,1)S(1)} %get-tuple-element.46.query_ref.four_q, f32[2,512,256]{2,1,0:T(8,128)S(1)} %get-tuple-element.45.fine, bf16[2,32,256]{2,1,0:T(8,128)(2,1)S(1)} %get-tuple-element.36.four_ref, ...), custom_call_target="tpu_custom_call" | custom-call | tf_op jit(solution)/shard_map/finish/pallas_call | solution.py:564
  18.8 1.2 %collective-permute-start.10 = (bf16[16,256]{1,0:T(8,128)(2,1)S(1)}, bf16[16,256]{1,0:T(8,128)(2,1)S(1)}, u32[]{:S(2)}, u32[]{:S(2)}) collective-permute-start(bf16[16,256]{1,0:T(8,128)(2,1)S(1)} %get-tuple-element.55), channel_id=1, source_target_pairs={{0,2},{1,3},{2,0},{3,1},{4,6},{5,7},{6,4},{7,5},{8,10},{9,11},{10,... | collective-permute-start | bytes 24584 | tf_op jit(solution)/shard_map/ppermute | solution.py:436
  20.0 0.6 %collective-permute-start.9 = (bf16[16,256]{1,0:T(8,128)(2,1)S(1)}, bf16[16,256]{1,0:T(8,128)(2,1)S(1)}, u32[]{:S(2)}, u32[]{:S(2)}) collective-permute-start(bf16[16,256]{1,0:T(8,128)(2,1)S(1)} %get-tuple-element.54), channel_id=1, source_target_pairs={{0,3},{1,2},{2,1},{3,0},{4,7},{5,6},{6,5},{7,4},{8,11},{9,10},{10,... | collective-permute-start | bytes 24584 | tf_op jit(solution)/shard_map/ppermute | solution.py:436
  20.7 0.1 rest.1
  20.8 0.1 collective-permute-start.11
  20.8 0.0 copy-done
  20.8 0.2 partial.1.partial_ref
  21.1 0.0 collective-permute-done.7.refs_0_
  21.1 1.1 %collective-permute-done.8.refs_1_ = bf16[128,256]{1,0:T(8,128)(2,1)S(1)} collective-permute-done((bf16[128,256]{1,0:T(8,128)(2,1)S(1)}, bf16[128,256]{1,0:T(8,128)(2,1)S(1)}, u32[]{:S(2)}, u32[]{:S(2)}) %collective-permute-start.8) | collective-permute-done | bytes 65568 | tf_op jit(solution)/shard_map/ppermute | solution.py:436
  22.2 0.2 collective-permute-done.10.refs_3_
  22.4 0.7 %collective-permute-done.9.refs_2_ = bf16[16,256]{1,0:T(8,128)(2,1)S(1)} collective-permute-done((bf16[16,256]{1,0:T(8,128)(2,1)S(1)}, bf16[16,256]{1,0:T(8,128)(2,1)S(1)}, u32[]{:S(2)}, u32[]{:S(2)}) %collective-permute-start.9) | collective-permute-done | bytes 8224 | tf_op jit(solution)/shard_map/ppermute | solution.py:436
  23.1 0.3 %rejoin.1 = (bf16[128,256]{1,0:T(8,128)(2,1)S(1)}, bf16[128,256]{1,0:T(8,128)(2,1)S(1)}) custom-call(f32[128,1024]{1,0:T(8,128)S(1)} %partial.1.partial_ref, f32[128,256]{1,0:T(8,128)S(1)} %get-tuple-element.52.refs_0_, f32[128,256]{1,0:T(8,128)S(1)} %get-tuple-element.53.refs_1_, bf16[16,256]{1,0:T(8,128)(2,1)S(1)} %collective-permute-done.9.refs_2_, ...), custom_call_target="tpu_custom_call" | custom-call | flops 4294967296 | bytes 1048576 | tf_op jit(solution)/shard_map/rejoin/pallas_call | solution.py:595
  23.4 0.0 collective-permute-done.11.refs_2_
  23.4 1.1 %project.1 = bf16[128,1024]{1,0:T(8,128)(2,1)} custom-call(f32[128,1024]{1,0:T(8,128)S(1)} %partial.1.partial_ref, bf16[128,256]{1,0:T(8,128)(2,1)S(1)} %get-tuple-element.56.refs_0_, bf16[128,256]{1,0:T(8,128)(2,1)S(1)} %get-tuple-element.57.refs_1_, bf16[128,256]{1,0:T(8,128)(2,1)S(1)} %collective-permute-done.11.refs_2_, bf16[1024,1024]{1,0:T(8,128)(2,1)S(1)} %copy-done), custom_call_target="tpu_custom_call" | custom-call | tf_op jit(solution)/shard_map/project/pallas_call | solution.py:603
  (3 shorter events, 0.1 us)
Async XLA Ops:
  1.4 10.2 %collective-permute-start.1 = (bf16[2,224,256]{2,1,0:T(8,128)(2,1)S(1)}, bf16[2,224,256]{2,1,0:T(8,128)(2,1)S(1)}, u32[]{:S(2)}, u32[]{:S(2)}) collective-permute-start(bf16[2,224,256]{2,1,0:T(8,128)(2,1)S(1)} %get-tuple-element.40), channel_id=1, source_target_pairs={{0,4},{4,0},{8,12},{12,8},{16,20},{20,16},{24,28},{28,24},{1,5},{5... | collective-permute-start | bytes 688136 | tf_op jit(solution)/shard_map/ppermute | solution.py:436
  1.5 6.3 %copy-start.1 = (bf16[1,512,256]{2,1,0:T(8,128)(2,1)S(1)}, bf16[1,512,256]{2,1,0:T(8,128)(2,1)}, u32[]{:S(2)}) copy-start(bf16[1,512,256]{2,1,0:T(8,128)(2,1)} %param.4) | copy-start | bytes 786436
  1.5 6.1 %collective-permute-start = (bf16[2,32,256]{2,1,0:T(8,128)(2,1)S(1)}, bf16[2,32,256]{2,1,0:T(8,128)(2,1)S(1)}, u32[]{:S(2)}, u32[]{:S(2)}) collective-permute-start(bf16[2,32,256]{2,1,0:T(8,128)(2,1)S(1)} %get-tuple-element.36.four_ref), channel_id=1, source_target_pairs={{0,16},{4,20},{8,24},{12,28},{16,0},{20,4},{24,8},{28,12},{1,17},{... | collective-permute-start | bytes 98312 | tf_op jit(solution)/shard_map/ppermute | solution.py:436
  4.1 5.2 %collective-permute-start.5 = (bf16[2,32,256]{2,1,0:T(8,128)(2,1)S(1)}, bf16[2,32,256]{2,1,0:T(8,128)(2,1)S(1)}, u32[]{:S(2)}, u32[]{:S(2)}) collective-permute-start(bf16[2,32,256]{2,1,0:T(8,128)(2,1)S(1)} %get-tuple-element.36.four_ref), channel_id=1, source_target_pairs={{0,24},{4,28},{8,16},{12,20},{16,8},{20,12},{24,0},{28,4},{1,25},{... | collective-permute-start | bytes 98312 | tf_op jit(solution)/shard_map/ppermute | solution.py:436
  5.2 6.3 %collective-permute-start.2 = (bf16[2,64,256]{2,1,0:T(8,128)(2,1)S(1)}, bf16[2,64,256]{2,1,0:T(8,128)(2,1)S(1)}, u32[]{:S(2)}, u32[]{:S(2)}) collective-permute-start(bf16[2,64,256]{2,1,0:T(8,128)(2,1)S(1)} %get-tuple-element.41), channel_id=1, source_target_pairs={{0,12},{4,8},{8,4},{12,0},{16,28},{20,24},{24,20},{28,16},{1,13},{... | collective-permute-start | bytes 196616 | tf_op jit(solution)/shard_map/ppermute | solution.py:436
  6.4 5.2 %collective-permute-start.3 = (bf16[2,64,256]{2,1,0:T(8,128)(2,1)S(1)}, bf16[2,64,256]{2,1,0:T(8,128)(2,1)S(1)}, u32[]{:S(2)}, u32[]{:S(2)}) collective-permute-start(bf16[2,64,256]{2,1,0:T(8,128)(2,1)S(1)} %get-tuple-element.41), channel_id=1, source_target_pairs={{0,8},{4,12},{8,0},{12,4},{16,24},{20,28},{24,16},{28,20},{1,9},{5... | collective-permute-start | bytes 196616 | tf_op jit(solution)/shard_map/ppermute | solution.py:436
  7.6 6.4 %collective-permute-start.4 = (bf16[2,128,256]{2,1,0:T(8,128)(2,1)S(1)}, bf16[2,128,256]{2,1,0:T(8,128)(2,1)S(1)}, u32[]{:S(2)}, u32[]{:S(2)}) collective-permute-start(bf16[2,128,256]{2,1,0:T(8,128)(2,1)S(1)} %get-tuple-element.44), channel_id=1, source_target_pairs={{0,1},{1,0},{2,3},{3,2},{4,8},{5,9},{6,10},{7,11},{8,4},{9,5},{10,... | collective-permute-start | bytes 393224 | tf_op jit(solution)/shard_map/ppermute | solution.py:447
  9.4 8.8 %collective-permute-start.6 = (bf16[2,64,256]{2,1,0:T(8,128)(2,1)S(1)}, bf16[2,64,256]{2,1,0:T(8,128)(2,1)S(1)}, u32[]{:S(2)}, u32[]{:S(2)}) collective-permute-start(bf16[2,64,256]{2,1,0:T(8,128)(2,1)S(1)} %join.1.fours_a), channel_id=1, source_target_pairs={{0,4},{4,0},{8,12},{12,8},{16,20},{20,16},{24,28},{28,24},{1,5},{5... | collective-permute-start | bytes 196616 | tf_op jit(solution)/shard_map/ppermute | solution.py:436
  14.0 6.8 %copy-start = (bf16[1024,1024]{1,0:T(8,128)(2,1)S(1)}, bf16[1024,1024]{1,0:T(8,128)(2,1)}, u32[]{:S(2)}) copy-start(bf16[1024,1024]{1,0:T(8,128)(2,1)} %refs_3_.1) | copy-start | bytes 6291460
  15.0 6.1 %collective-permute-start.7 = (bf16[128,256]{1,0:T(8,128)(2,1)S(1)}, bf16[128,256]{1,0:T(8,128)(2,1)S(1)}, u32[]{:S(2)}, u32[]{:S(2)}) collective-permute-start(bf16[128,256]{1,0:T(8,128)(2,1)S(1)} %get-tuple-element.50), channel_id=1, source_target_pairs={{0,3},{1,2},{2,1},{3,0},{4,7},{5,6},{6,5},{7,4},{8,11},{9,10},{10,... | collective-permute-start | bytes 196616 | tf_op jit(solution)/shard_map/ppermute | solution.py:436
  17.9 4.3 %collective-permute-start.8 = (bf16[128,256]{1,0:T(8,128)(2,1)S(1)}, bf16[128,256]{1,0:T(8,128)(2,1)S(1)}, u32[]{:S(2)}, u32[]{:S(2)}) collective-permute-start(bf16[128,256]{1,0:T(8,128)(2,1)S(1)} %get-tuple-element.51), channel_id=1, source_target_pairs={{0,2},{1,3},{2,0},{3,1},{4,6},{5,7},{6,4},{7,5},{8,10},{9,11},{10,... | collective-permute-start | bytes 196616 | tf_op jit(solution)/shard_map/ppermute | solution.py:436
  18.8 3.6 %collective-permute-start.10 = (bf16[16,256]{1,0:T(8,128)(2,1)S(1)}, bf16[16,256]{1,0:T(8,128)(2,1)S(1)}, u32[]{:S(2)}, u32[]{:S(2)}) collective-permute-start(bf16[16,256]{1,0:T(8,128)(2,1)S(1)} %get-tuple-element.55), channel_id=1, source_target_pairs={{0,2},{1,3},{2,0},{3,1},{4,6},{5,7},{6,4},{7,5},{8,10},{9,11},{10,... | collective-permute-start | bytes 24584 | tf_op jit(solution)/shard_map/ppermute | solution.py:436
  20.0 3.1 %collective-permute-start.9 = (bf16[16,256]{1,0:T(8,128)(2,1)S(1)}, bf16[16,256]{1,0:T(8,128)(2,1)S(1)}, u32[]{:S(2)}, u32[]{:S(2)}) collective-permute-start(bf16[16,256]{1,0:T(8,128)(2,1)S(1)} %get-tuple-element.54), channel_id=1, source_target_pairs={{0,3},{1,2},{2,1},{3,0},{4,7},{5,6},{6,5},{7,4},{8,11},{9,10},{10,... | collective-permute-start | bytes 24584 | tf_op jit(solution)/shard_map/ppermute | solution.py:436
  20.8 2.6 %collective-permute-start.11 = (bf16[128,256]{1,0:T(8,128)(2,1)S(1)}, bf16[128,256]{1,0:T(8,128)(2,1)S(1)}, u32[]{:S(2)}, u32[]{:S(2)}) collective-permute-start(bf16[128,256]{1,0:T(8,128)(2,1)S(1)} %get-tuple-element.58), channel_id=1, source_target_pairs={{0,1},{1,0},{2,3},{3,2},{4,5},{5,4},{6,7},{7,6},{8,9},{9,8},{10,11... | collective-permute-start | bytes 196616 | tf_op jit(solution)/shard_map/ppermute | solution.py:436

commit v6 on v3

--- a/solution.py
+++ b/solution.py
@@ -354,7 +354,7 @@
         top, numer, rowsum = weigh(four_hold.at[pair], *steps[pair])
         coarse[0, :, lanes] = numer / rowsum
         coarse[1, :, lanes] = top + jnp.log(rowsum) * log2_e
-    finish_blocks(fine, coarse, zip(steps_out, outs))
+    finish_blocks(fine, coarse, [*zip(steps_out, outs)][::-1])
 
 
 def rest_kernel(fine, coarse, *outs):
@@ -620,14 +620,14 @@
         cost_estimate=heavy,
         name="rejoin",
     )(further, *widened, *late_in)
-    chunk = 2 * PAIR
+    chunk = 4 * PAIR
     result = pl.pallas_call(
         project_kernel,
         in_specs=[vmem] * (len(rejoined) + 3),
         out_specs=hbm,
         out_shape=bf16(BLOCK, width),
         scratch_shapes=[
-            pltpu.VMEM((width // chunk, 2, BLOCK, PAIR), jnp.float32),
+            pltpu.VMEM((width // chunk, chunk // PAIR, BLOCK, PAIR), jnp.float32),
             pltpu.VMEM((width // chunk, BLOCK, chunk), jnp.bfloat16),
             pltpu.SemaphoreType.DMA((width // chunk,)),
         ],

time: 24.2 us -> 24.2 us (level)
  no operation moved by 1% of the time
where the time goes in v6:
time: 24.2 us; the launch traced here: 24.1 us
  starting transfers between devices  12.2 us (50%)
  Pallas kernels  6.84 us (28%)
  waiting for transfers between devices  4.86 us (20%)
    ppermute x10, starting transfers between devices, swapped(): lax.ppermute(block, axis, [(i, i ^ mask) for i in range(lax.axis_size(axi...  12.2 us
    ppermute x10, waiting for transfers between devices, swapped(): lax.ppermute(block, axis, [(i, i ^ mask) for i in range(lax.axis_size(axi...  4.86 us
    pallas_call x1, Pallas kernels, per_device(): pl.pallas_call(local_kernel, out_shape=[bf16(2, BLOCK, features), bf16(ro...  1.54 us
    pallas_call x1, Pallas kernels, per_device(): pl.pallas_call(pool_kernel, in_specs=[hbm] * 2, out_shape=[bf16(rows, fea...  1.39 us
    pallas_call x1, Pallas kernels, per_device(): pl.pallas_call(project_kernel, in_specs=[vmem] * (len(rejoined) + 3), out...  1.04 us
    pallas_call x1, Pallas kernels, per_device(): pl.pallas_call(mid_kernel, out_shape=[jax.ShapeDtypeStruct((2, rows, feat...  0.93 us
    pallas_call x1, Pallas kernels, per_device(): pl.pallas_call(finish_kernel, out_shape=parts[2:] + [bf16(2 * SLAB, featu...  0.61 us
    pallas_call x1, Pallas kernels, per_device(): pl.pallas_call(coarse_kernel, out_shape=[jax.ShapeDtypeStruct((3, rows //...  0.5 us
  transfers between devices with their start and end apart: 11, of which 4 were waited for; matrix products, arithmetic and copies ran while one was open for 0% of the time, Pallas kernels for 18%

profile of v6, /device:TPU:0, one launch (start us, length us, event | category | flops | bytes accessed | tf_op | source)
XLA Modules:
  0.0 24.1 jit_solution(16547386862636921786)
XLA Ops:
  0.0 1.4 %pool.1 = (bf16[512,256]{1,0:T(8,128)(2,1)S(1)}, bf16[512,256]{1,0:T(8,128)(2,1)S(1)}, bf16[2,224,256]{2,1,0:T(8,128)(2,1)S(1)}, bf16[2,256,256]{2,1,0:T(8,128)(2,1)S(1)}, bf16[2,128,256]{2,1,0:T(8,128)(2,1)S(1)}) custom-call(bf16[1,512,256]{2,1,0:T(8,128)(2,1)} %k_hbm.1, bf16[1,512,256]{2,1,0:T(8,128)(2,1)} %v_hbm.1), custom_call_target="tpu_custom_call" | custom-call | tf_op jit(solution)/shard_map/pool/pallas_call | solution.py:475
  1.4 3.0 %collective-permute-start.1 = (bf16[2,224,256]{2,1,0:T(8,128)(2,1)S(1)}, bf16[2,224,256]{2,1,0:T(8,128)(2,1)S(1)}, u32[]{:S(2)}, u32[]{:S(2)}) collective-permute-start(bf16[2,224,256]{2,1,0:T(8,128)(2,1)S(1)} %get-tuple-element.35), channel_id=1, source_target_pairs={{0,4},{4,0},{8,12},{12,8},{16,20},{20,16},{24,28},{28,24},{1,5},{5... | collective-permute-start | bytes 688136 | tf_op jit(solution)/shard_map/ppermute | solution.py:449
  4.4 0.0 copy-start.1
  4.5 2.7 %collective-permute-start = (bf16[2,32,256]{2,1,0:T(8,128)(2,1)S(1)}, bf16[2,32,256]{2,1,0:T(8,128)(2,1)S(1)}, u32[]{:S(2)}, u32[]{:S(2)}) collective-permute-start(bf16[2,32,256]{2,1,0:T(8,128)(2,1)S(1)} %get-tuple-element.31.four_ref), channel_id=1, source_target_pairs={{0,16},{4,20},{8,24},{12,28},{16,0},{20,4},{24,8},{28,12},{1,17},{... | collective-permute-start | bytes 98312 | tf_op jit(solution)/shard_map/ppermute | solution.py:449
  7.1 1.3 %collective-permute-start.6 = (bf16[2,32,256]{2,1,0:T(8,128)(2,1)S(1)}, bf16[2,32,256]{2,1,0:T(8,128)(2,1)S(1)}, u32[]{:S(2)}, u32[]{:S(2)}) collective-permute-start(bf16[2,32,256]{2,1,0:T(8,128)(2,1)S(1)} %get-tuple-element.31.four_ref), channel_id=1, source_target_pairs={{0,24},{4,28},{8,16},{12,20},{16,8},{20,12},{24,0},{28,4},{1,25},{... | collective-permute-start | bytes 98312 | tf_op jit(solution)/shard_map/ppermute | solution.py:449
  8.5 0.2 collective-permute-start.2
  8.7 1.8 %collective-permute-start.3 = (bf16[2,64,256]{2,1,0:T(8,128)(2,1)S(1)}, bf16[2,64,256]{2,1,0:T(8,128)(2,1)S(1)}, u32[]{:S(2)}, u32[]{:S(2)}) collective-permute-start(bf16[2,64,256]{2,1,0:T(8,128)(2,1)S(1)} %get-tuple-element.36), channel_id=1, source_target_pairs={{0,8},{4,12},{8,0},{12,4},{16,24},{20,28},{24,16},{28,20},{1,9},{5... | collective-permute-start | bytes 196616 | tf_op jit(solution)/shard_map/ppermute | solution.py:449
  10.5 0.0 collective-permute-done.four_ref
  10.5 0.0 collective-permute-start.4
  10.5 0.0 copy-done.1
  10.5 1.5 %local.1 = (bf16[2,128,256]{2,1,0:T(8,128)(2,1)S(1)}, bf16[128,256]{1,0:T(8,128)(2,1)S(1)}, bf16[64,256]{1,0:T(8,128)(2,1)S(1)}, bf16[32,256]{1,0:T(8,128)(2,1)S(1)}, f32[3,512,256]{2,1,0:T(8,128)S(1)}) custom-call(bf16[512,256]{1,0:T(8,128)(2,1)S(1)} %bitcast.2, bf16[512,256]{1,0:T(8,128)(2,1)S(1)} %get-tuple-element.27.k_ref, ...), custom_call_target="tpu_custom_call" | custom-call | tf_op jit(solution)/shard_map/local/pallas_call | solution.py:509
  12.0 1.2 %collective-permute-done.6.six_ref = bf16[2,32,256]{2,1,0:T(8,128)(2,1)S(1)} collective-permute-done((bf16[2,32,256]{2,1,0:T(8,128)(2,1)S(1)}, bf16[2,32,256]{2,1,0:T(8,128)(2,1)S(1)}, u32[]{:S(2)}, u32[]{:S(2)}) %collective-permute-start.6) | collective-permute-done | bytes 32800 | tf_op jit(solution)/shard_map/ppermute | solution.py:449
  13.2 0.9 %collective-permute-start.7 = (bf16[2,64,256]{2,1,0:T(8,128)(2,1)S(1)}, bf16[2,64,256]{2,1,0:T(8,128)(2,1)S(1)}, u32[]{:S(2)}, u32[]{:S(2)}) collective-permute-start(bf16[2,64,256]{2,1,0:T(8,128)(2,1)S(1)} %join.1.fours_a), channel_id=1, source_target_pairs={{0,4},{4,0},{8,12},{12,8},{16,20},{20,16},{24,28},{28,24},{1,5},{5... | collective-permute-start | bytes 196616 | tf_op jit(solution)/shard_map/ppermute | solution.py:449
  14.2 0.0 collective-permute-done.2.three_a
  14.2 0.6 %collective-permute-done.3.three_b = bf16[2,64,256]{2,1,0:T(8,128)(2,1)S(1)} collective-permute-done((bf16[2,64,256]{2,1,0:T(8,128)(2,1)S(1)}, bf16[2,64,256]{2,1,0:T(8,128)(2,1)S(1)}, u32[]{:S(2)}, u32[]{:S(2)}) %collective-permute-start.3) | collective-permute-done | bytes 65568 | tf_op jit(solution)/shard_map/ppermute | solution.py:449
  14.8 0.0 collective-permute-done.1.first_ref
  14.8 0.5 %coarse.1 = (f32[3,128,256]{2,1,0:T(8,128)S(1)}, bf16[2,32,256]{2,1,0:T(8,128)(2,1)S(1)}) custom-call(bf16[128,256]{1,0:T(8,128)(2,1)S(1)} %get-tuple-element.33.two_q, bf16[64,256]{1,0:T(8,128)(2,1)S(1)} %get-tuple-element.34.three_q, bf16[2,224,256]{2,1,0:T(8,128)(2,1)S(1)} %collective-permute-done.1.first_ref, ...), custom_call_target="tpu_custom_call" | custom-call | flops 2147483648 | bytes 2097152 | tf_op jit(solution)/shard_map/coarse/pallas_call | solution.py:535
  15.3 0.0 collective-permute-done.4.second_ref
  15.3 0.0 copy-start
  15.3 0.9 %mid.1 = (f32[2,512,256]{2,1,0:T(8,128)S(1)}, bf16[128,256]{1,0:T(8,128)(2,1)S(1)}) custom-call(bf16[2,128,256]{2,1,0:T(8,128)(2,1)S(1)} %get-tuple-element.32.edge_q, f32[3,128,256]{2,1,0:T(8,128)S(1)} %get-tuple-element.37.coarse, f32[3,512,256]{2,1,0:T(8,128)S(1)} %get-tuple-element.38.state, bf16[2,224,256]{2,1,0:T(8,128)(2,1)S(1)} %collective-permute-done.1.first_ref, ...), custom_call_target="tpu_custom_call" | custom-call | tf_op jit(solution)/shard_map/mid/pallas_call | solution.py:552
  16.2 0.1 collective-permute-start.5
  16.3 1.2 %collective-permute-done.7.fours_b = bf16[2,64,256]{2,1,0:T(8,128)(2,1)S(1)} collective-permute-done((bf16[2,64,256]{2,1,0:T(8,128)(2,1)S(1)}, bf16[2,64,256]{2,1,0:T(8,128)(2,1)S(1)}, u32[]{:S(2)}, u32[]{:S(2)}) %collective-permute-start.7) | collective-permute-done | bytes 65568 | tf_op jit(solution)/shard_map/ppermute | solution.py:449
  17.5 0.6 %finish.1 = (bf16[128,256]{1,0:T(8,128)(2,1)S(1)}, bf16[16,256]{1,0:T(8,128)(2,1)S(1)}, f32[2,32,256]{2,1,0:T(8,128)S(1)}) custom-call(bf16[32,256]{1,0:T(8,128)(2,1)S(1)} %get-tuple-element.42.query_ref.four_q, f32[2,512,256]{2,1,0:T(8,128)S(1)} %get-tuple-element.41.fine, bf16[2,32,256]{2,1,0:T(8,128)(2,1)S(1)} %get-tuple-element.31.four_ref, ...), custom_call_target="tpu_custom_call" | custom-call | tf_op jit(solution)/shard_map/finish/pallas_call | solution.py:577
  18.1 1.5 %collective-permute-start.8 = (bf16[128,256]{1,0:T(8,128)(2,1)S(1)}, bf16[128,256]{1,0:T(8,128)(2,1)S(1)}, u32[]{:S(2)}, u32[]{:S(2)}) collective-permute-start(bf16[128,256]{1,0:T(8,128)(2,1)S(1)} %get-tuple-element.46), channel_id=1, source_target_pairs={{0,2},{1,3},{2,0},{3,1},{4,6},{5,7},{6,4},{7,5},{8,10},{9,11},{10,... | collective-permute-start | bytes 196616 | tf_op jit(solution)/shard_map/ppermute | solution.py:449
  19.6 0.3 %collective-permute-start.9 = (bf16[16,256]{1,0:T(8,128)(2,1)S(1)}, bf16[16,256]{1,0:T(8,128)(2,1)S(1)}, u32[]{:S(2)}, u32[]{:S(2)}) collective-permute-start(bf16[16,256]{1,0:T(8,128)(2,1)S(1)} %get-tuple-element.47), channel_id=1, source_target_pairs={{0,3},{1,2},{2,1},{3,0},{4,7},{5,6},{6,5},{7,4},{8,11},{9,10},{10,... | collective-permute-start | bytes 24584 | tf_op jit(solution)/shard_map/ppermute | solution.py:449
  19.9 0.1 rest.1
  20.0 0.4 %collective-permute-start.10 = (bf16[128,256]{1,0:T(8,128)(2,1)S(1)}, bf16[128,256]{1,0:T(8,128)(2,1)S(1)}, u32[]{:S(2)}, u32[]{:S(2)}) collective-permute-start(bf16[128,256]{1,0:T(8,128)(2,1)S(1)} %get-tuple-element.48), channel_id=1, source_target_pairs={{0,1},{1,0},{2,3},{3,2},{4,5},{5,4},{6,7},{7,6},{8,9},{9,8},{10,11... | collective-permute-start | bytes 196616 | tf_op jit(solution)/shard_map/ppermute | solution.py:449
  20.4 0.0 copy-done
  20.4 0.2 partial.1.partial_ref
  20.6 0.0 collective-permute-done.5.refs_0_
  20.7 1.9 %collective-permute-done.8.refs_0_ = bf16[128,256]{1,0:T(8,128)(2,1)S(1)} collective-permute-done((bf16[128,256]{1,0:T(8,128)(2,1)S(1)}, bf16[128,256]{1,0:T(8,128)(2,1)S(1)}, u32[]{:S(2)}, u32[]{:S(2)}) %collective-permute-start.8) | collective-permute-done | bytes 65568 | tf_op jit(solution)/shard_map/ppermute | solution.py:449
  22.5 0.2 further.1.further_ref.partial_ref
  22.8 0.0 collective-permute-done.9.refs_1_
  22.8 0.2 rejoin.1.refs_0_
  23.0 0.0 collective-permute-done.10.refs_1_
  23.0 1.0 %project.1 = bf16[128,1024]{1,0:T(8,128)(2,1)} custom-call(f32[128,1024]{1,0:T(8,128)S(1)} %further.1.further_ref.partial_ref, bf16[128,256]{1,0:T(8,128)(2,1)S(1)} %rejoin.1.refs_0_, bf16[128,256]{1,0:T(8,128)(2,1)S(1)} %collective-permute-done.10.refs_1_, bf16[1024,1024]{1,0:T(8,128)(2,1)S(1)} %copy-done), custom_call_target="tpu_custom_call" | custom-call | tf_op jit(solution)/shard_map/project/pallas_call | solution.py:624
  (3 shorter events, 0.1 us)
Async XLA Ops:
  1.4 13.4 %collective-permute-start.1 = (bf16[2,224,256]{2,1,0:T(8,128)(2,1)S(1)}, bf16[2,224,256]{2,1,0:T(8,128)(2,1)S(1)}, u32[]{:S(2)}, u32[]{:S(2)}) collective-permute-start(bf16[2,224,256]{2,1,0:T(8,128)(2,1)S(1)} %get-tuple-element.35), channel_id=1, source_target_pairs={{0,4},{4,0},{8,12},{12,8},{16,20},{20,16},{24,28},{28,24},{1,5},{5... | collective-permute-start | bytes 688136 | tf_op jit(solution)/shard_map/ppermute | solution.py:449
  4.4 6.0 %copy-start.1 = (bf16[1,512,256]{2,1,0:T(8,128)(2,1)S(1)}, bf16[1,512,256]{2,1,0:T(8,128)(2,1)}, u32[]{:S(2)}) copy-start(bf16[1,512,256]{2,1,0:T(8,128)(2,1)} %param.4) | copy-start | bytes 786436
  4.5 6.0 %collective-permute-start = (bf16[2,32,256]{2,1,0:T(8,128)(2,1)S(1)}, bf16[2,32,256]{2,1,0:T(8,128)(2,1)S(1)}, u32[]{:S(2)}, u32[]{:S(2)}) collective-permute-start(bf16[2,32,256]{2,1,0:T(8,128)(2,1)S(1)} %get-tuple-element.31.four_ref), channel_id=1, source_target_pairs={{0,16},{4,20},{8,24},{12,28},{16,0},{20,4},{24,8},{28,12},{1,17},{... | collective-permute-start | bytes 98312 | tf_op jit(solution)/shard_map/ppermute | solution.py:449
  7.1 6.1 %collective-permute-start.6 = (bf16[2,32,256]{2,1,0:T(8,128)(2,1)S(1)}, bf16[2,32,256]{2,1,0:T(8,128)(2,1)S(1)}, u32[]{:S(2)}, u32[]{:S(2)}) collective-permute-start(bf16[2,32,256]{2,1,0:T(8,128)(2,1)S(1)} %get-tuple-element.31.four_ref), channel_id=1, source_target_pairs={{0,24},{4,28},{8,16},{12,20},{16,8},{20,12},{24,0},{28,4},{1,25},{... | collective-permute-start | bytes 98312 | tf_op jit(solution)/shard_map/ppermute | solution.py:449
  8.5 5.7 %collective-permute-start.2 = (bf16[2,64,256]{2,1,0:T(8,128)(2,1)S(1)}, bf16[2,64,256]{2,1,0:T(8,128)(2,1)S(1)}, u32[]{:S(2)}, u32[]{:S(2)}) collective-permute-start(bf16[2,64,256]{2,1,0:T(8,128)(2,1)S(1)} %get-tuple-element.36), channel_id=1, source_target_pairs={{0,12},{4,8},{8,4},{12,0},{16,28},{20,24},{24,20},{28,16},{1,13},{... | collective-permute-start | bytes 196616 | tf_op jit(solution)/shard_map/ppermute | solution.py:449
  8.7 6.1 %collective-permute-start.3 = (bf16[2,64,256]{2,1,0:T(8,128)(2,1)S(1)}, bf16[2,64,256]{2,1,0:T(8,128)(2,1)S(1)}, u32[]{:S(2)}, u32[]{:S(2)}) collective-permute-start(bf16[2,64,256]{2,1,0:T(8,128)(2,1)S(1)} %get-tuple-element.36), channel_id=1, source_target_pairs={{0,8},{4,12},{8,0},{12,4},{16,24},{20,28},{24,16},{28,20},{1,9},{5... | collective-permute-start | bytes 196616 | tf_op jit(solution)/shard_map/ppermute | solution.py:449
  10.5 4.8 %collective-permute-start.4 = (bf16[2,128,256]{2,1,0:T(8,128)(2,1)S(1)}, bf16[2,128,256]{2,1,0:T(8,128)(2,1)S(1)}, u32[]{:S(2)}, u32[]{:S(2)}) collective-permute-start(bf16[2,128,256]{2,1,0:T(8,128)(2,1)S(1)} %get-tuple-element.39), channel_id=1, source_target_pairs={{0,1},{1,0},{2,3},{3,2},{4,8},{5,9},{6,10},{7,11},{8,4},{9,5},{10,... | collective-permute-start | bytes 393224 | tf_op jit(solution)/shard_map/ppermute | solution.py:460
  13.2 4.3 %collective-permute-start.7 = (bf16[2,64,256]{2,1,0:T(8,128)(2,1)S(1)}, bf16[2,64,256]{2,1,0:T(8,128)(2,1)S(1)}, u32[]{:S(2)}, u32[]{:S(2)}) collective-permute-start(bf16[2,64,256]{2,1,0:T(8,128)(2,1)S(1)} %join.1.fours_a), channel_id=1, source_target_pairs={{0,4},{4,0},{8,12},{12,8},{16,20},{20,16},{24,28},{28,24},{1,5},{5... | collective-permute-start | bytes 196616 | tf_op jit(solution)/shard_map/ppermute | solution.py:449
  15.3 5.1 %copy-start = (bf16[1024,1024]{1,0:T(8,128)(2,1)S(1)}, bf16[1024,1024]{1,0:T(8,128)(2,1)}, u32[]{:S(2)}) copy-start(bf16[1024,1024]{1,0:T(8,128)(2,1)} %refs_2_.1) | copy-start | bytes 6291460
  16.2 4.4 %collective-permute-start.5 = (bf16[128,256]{1,0:T(8,128)(2,1)S(1)}, bf16[128,256]{1,0:T(8,128)(2,1)S(1)}, u32[]{:S(2)}, u32[]{:S(2)}) collective-permute-start(bf16[128,256]{1,0:T(8,128)(2,1)S(1)} %get-tuple-element.40), channel_id=1, source_target_pairs={{0,3},{1,2},{2,1},{3,0},{4,7},{5,6},{6,5},{7,4},{8,11},{9,10},{10,... | collective-permute-start | bytes 196616 | tf_op jit(solution)/shard_map/ppermute | solution.py:449
  18.1 4.4 %collective-permute-start.8 = (bf16[128,256]{1,0:T(8,128)(2,1)S(1)}, bf16[128,256]{1,0:T(8,128)(2,1)S(1)}, u32[]{:S(2)}, u32[]{:S(2)}) collective-permute-start(bf16[128,256]{1,0:T(8,128)(2,1)S(1)} %get-tuple-element.46), channel_id=1, source_target_pairs={{0,2},{1,3},{2,0},{3,1},{4,6},{5,7},{6,4},{7,5},{8,10},{9,11},{10,... | collective-permute-start | bytes 196616 | tf_op jit(solution)/shard_map/ppermute | solution.py:449
  19.6 3.2 %collective-permute-start.9 = (bf16[16,256]{1,0:T(8,128)(2,1)S(1)}, bf16[16,256]{1,0:T(8,128)(2,1)S(1)}, u32[]{:S(2)}, u32[]{:S(2)}) collective-permute-start(bf16[16,256]{1,0:T(8,128)(2,1)S(1)} %get-tuple-element.47), channel_id=1, source_target_pairs={{0,3},{1,2},{2,1},{3,0},{4,7},{5,6},{6,5},{7,4},{8,11},{9,10},{10,... | collective-permute-start | bytes 24584 | tf_op jit(solution)/shard_map/ppermute | solution.py:449
  20.0 3.0 %collective-permute-start.10 = (bf16[128,256]{1,0:T(8,128)(2,1)S(1)}, bf16[128,256]{1,0:T(8,128)(2,1)S(1)}, u32[]{:S(2)}, u32[]{:S(2)}) collective-permute-start(bf16[128,256]{1,0:T(8,128)(2,1)S(1)} %get-tuple-element.48), channel_id=1, source_target_pairs={{0,1},{1,0},{2,3},{3,2},{4,5},{5,4},{6,7},{7,6},{8,9},{9,8},{10,11... | collective-permute-start | bytes 196616 | tf_op jit(solution)/shard_map/ppermute | solution.py:449

commit v7 on v6

--- a/solution.py
+++ b/solution.py
@@ -354,31 +354,35 @@
         top, numer, rowsum = weigh(four_hold.at[pair], *steps[pair])
         coarse[0, :, lanes] = numer / rowsum
         coarse[1, :, lanes] = top + jnp.log(rowsum) * log2_e
-    finish_blocks(fine, coarse, [*zip(steps_out, outs)][::-1])
+    finish_blocks(fine, coarse, zip(steps_out, outs))
 
 
 def rest_kernel(fine, coarse, *outs):
     finish_blocks(fine, coarse, enumerate(outs))
 
 
-def rejoin_kernel(further_ref, *refs):
-    outs = refs[len(refs) // 3 * 2 :]
-    for early, late_ref, out in zip(refs, refs[len(outs) :], outs):
-        features = early.shape[1]
-        late = late_ref[...].astype(jnp.float32)
-        spread = lax.broadcasted_iota(jnp.int32, (SLAB, features), 1) // HD == (
-            lax.broadcasted_iota(jnp.int32, (SLAB, features), 0)
-        )
-        signed = lax.dot_general(
-            late[SLAB:, :BLOCK].astype(jnp.bfloat16),
-            spread.astype(jnp.bfloat16),
-            (((0,), (0,)), ((), ())),
-            preferred_element_type=jnp.float32,
-        )
-        keep = jnp.where(signed >= 0, signed, 1.0 + signed)
-        join = jnp.where(signed >= 0, 1.0 - signed, -signed)
-        result = keep * early[...] + join * repeated(late[:SLAB])
-        out[...] = result.astype(jnp.bfloat16)
+def gate_kernel(further_ref, *refs):
+    half = len(refs) // 2
+    for ref, out in zip(refs[:half], refs[half:]):
+        out[...] = ref[...]
+
+
+def rejoined(early, late_ref):
+    features = early.shape[1]
+    late = late_ref[...].astype(jnp.float32)
+    spread = lax.broadcasted_iota(jnp.int32, (SLAB, features), 1) // HD == (
+        lax.broadcasted_iota(jnp.int32, (SLAB, features), 0)
+    )
+    signed = lax.dot_general(
+        late[SLAB:, :BLOCK].astype(jnp.bfloat16),
+        spread.astype(jnp.bfloat16),
+        (((0,), (0,)), ((), ())),
+        preferred_element_type=jnp.float32,
+    )
+    keep = jnp.where(signed >= 0, signed, 1.0 + signed)
+    join = jnp.where(signed >= 0, 1.0 - signed, -signed)
+    result = keep * early + join * repeated(late[:SLAB])
+    return result.astype(jnp.bfloat16)
 
 
 def widen_kernel(*refs):
@@ -409,18 +413,21 @@
 
 
 def project_kernel(partial_ref, *refs):
-    parts, (weight_ref, out_hbm, scratch, staged, sems) = refs[:-5], refs[-5:]
+    refs, (next_ref, weight_ref, out_hbm, scratch, staged, sems) = refs[:-6], refs[-6:]
     own = lax.axis_index("head")
-    features = parts[0].shape[1]
+    half = len(refs) // 2
+    parts = [next_ref[...]]
+    parts += [rejoined(early[...], late) for early, late in zip(refs[:half], refs[half:])]
+    features = next_ref.shape[1]
     chunk = staged.shape[2]
     copies = []
     for index in range(staged.shape[0]):
         columns = pl.ds(index * chunk, chunk)
         total = partial_ref[:, columns]
-        for step, part in zip([*range(AHEAD, AHEAD + len(parts) - 1), 1], parts):
+        for step, part in zip([1, *range(AHEAD, AHEAD + half)], parts):
             start = pl.multiple_of((own ^ step) * features, features)
             total += jnp.dot(
-                part[...],
+                part,
                 weight_ref[pl.ds(start, features), columns],
                 preferred_element_type=jnp.float32,
             )
@@ -613,17 +620,17 @@
         compiler_params=params,
         name="further",
     )(widened[0], partial, out_weight, *whole_in)
-    rejoined = pl.pallas_call(
-        rejoin_kernel,
-        out_shape=[bf16(BLOCK, features) for _ in away],
+    gated = pl.pallas_call(
+        gate_kernel,
+        out_shape=[bf16(2 * SLAB, features) for _ in away],
         compiler_params=params,
         cost_estimate=heavy,
-        name="rejoin",
-    )(further, *widened, *late_in)
+        name="gate",
+    )(further, *late_in)
     chunk = 4 * PAIR
     result = pl.pallas_call(
         project_kernel,
-        in_specs=[vmem] * (len(rejoined) + 3),
+        in_specs=[vmem] * (2 * len(gated) + 3),
         out_specs=hbm,
         out_shape=bf16(BLOCK, width),
         scratch_shapes=[
@@ -633,7 +640,7 @@
         ],
         compiler_params=params,
         name="project",
-    )(further, *rejoined, next_in, out_weight)
+    )(further, *widened, *gated, next_in, out_weight)
     return result[None]
 
 

time: 24.2 us -> 24.1 us (level)
  no operation moved by 1% of the time
where the time goes in v7:
time: 24.1 us; the launch traced here: 23.9 us
  starting transfers between devices  12.2 us (51%)
  Pallas kernels  6.72 us (28%)
  waiting for transfers between devices  4.86 us (20%)
    ppermute x10, starting transfers between devices, swapped(): lax.ppermute(block, axis, [(i, i ^ mask) for i in range(lax.axis_size(axi...  12.2 us
    ppermute x10, waiting for transfers between devices, swapped(): lax.ppermute(block, axis, [(i, i ^ mask) for i in range(lax.axis_size(axi...  4.86 us
    pallas_call x1, Pallas kernels, per_device(): pl.pallas_call(local_kernel, out_shape=[bf16(2, BLOCK, features), bf16(ro...  1.54 us
    pallas_call x1, Pallas kernels, per_device(): pl.pallas_call(pool_kernel, in_specs=[hbm] * 2, out_shape=[bf16(rows, fea...  1.39 us
    pallas_call x1, Pallas kernels, per_device(): pl.pallas_call(project_kernel, in_specs=[vmem] * (2 * len(gated) + 3), ou...  1.14 us
    pallas_call x1, Pallas kernels, per_device(): pl.pallas_call(mid_kernel, out_shape=[jax.ShapeDtypeStruct((2, rows, feat...  0.93 us
    pallas_call x1, Pallas kernels, per_device(): pl.pallas_call(finish_kernel, out_shape=parts[2:] + [bf16(2 * SLAB, featu...  0.61 us
    pallas_call x1, Pallas kernels, per_device(): pl.pallas_call(coarse_kernel, out_shape=[jax.ShapeDtypeStruct((3, rows //...  0.5 us
  transfers between devices with their start and end apart: 11, of which 4 were waited for; matrix products, arithmetic and copies ran while one was open for 0% of the time, Pallas kernels for 18%

profile of v7, /device:TPU:0, one launch (start us, length us, event | category | flops | bytes accessed | tf_op | source)
XLA Modules:
  0.0 23.9 jit_solution(15152003247427704561)
XLA Ops:
  0.0 1.4 %pool.1 = (bf16[512,256]{1,0:T(8,128)(2,1)S(1)}, bf16[512,256]{1,0:T(8,128)(2,1)S(1)}, bf16[2,224,256]{2,1,0:T(8,128)(2,1)S(1)}, bf16[2,256,256]{2,1,0:T(8,128)(2,1)S(1)}, bf16[2,128,256]{2,1,0:T(8,128)(2,1)S(1)}) custom-call(bf16[1,512,256]{2,1,0:T(8,128)(2,1)} %k_hbm.1, bf16[1,512,256]{2,1,0:T(8,128)(2,1)} %v_hbm.1), custom_call_target="tpu_custom_call" | custom-call | tf_op jit(solution)/shard_map/pool/pallas_call | solution.py:482
  1.4 3.0 %collective-permute-start.1 = (bf16[2,224,256]{2,1,0:T(8,128)(2,1)S(1)}, bf16[2,224,256]{2,1,0:T(8,128)(2,1)S(1)}, u32[]{:S(2)}, u32[]{:S(2)}) collective-permute-start(bf16[2,224,256]{2,1,0:T(8,128)(2,1)S(1)} %get-tuple-element.35), channel_id=1, source_target_pairs={{0,4},{4,0},{8,12},{12,8},{16,20},{20,16},{24,28},{28,24},{1,5},{5... | collective-permute-start | bytes 688136 | tf_op jit(solution)/shard_map/ppermute | solution.py:456
  4.4 0.0 copy-start.1
  4.5 2.7 %collective-permute-start = (bf16[2,32,256]{2,1,0:T(8,128)(2,1)S(1)}, bf16[2,32,256]{2,1,0:T(8,128)(2,1)S(1)}, u32[]{:S(2)}, u32[]{:S(2)}) collective-permute-start(bf16[2,32,256]{2,1,0:T(8,128)(2,1)S(1)} %get-tuple-element.31.four_ref), channel_id=1, source_target_pairs={{0,16},{4,20},{8,24},{12,28},{16,0},{20,4},{24,8},{28,12},{1,17},{... | collective-permute-start | bytes 98312 | tf_op jit(solution)/shard_map/ppermute | solution.py:456
  7.1 1.3 %collective-permute-start.6 = (bf16[2,32,256]{2,1,0:T(8,128)(2,1)S(1)}, bf16[2,32,256]{2,1,0:T(8,128)(2,1)S(1)}, u32[]{:S(2)}, u32[]{:S(2)}) collective-permute-start(bf16[2,32,256]{2,1,0:T(8,128)(2,1)S(1)} %get-tuple-element.31.four_ref), channel_id=1, source_target_pairs={{0,24},{4,28},{8,16},{12,20},{16,8},{20,12},{24,0},{28,4},{1,25},{... | collective-permute-start | bytes 98312 | tf_op jit(solution)/shard_map/ppermute | solution.py:456
  8.5 0.2 collective-permute-start.2
  8.7 1.8 %collective-permute-start.3 = (bf16[2,64,256]{2,1,0:T(8,128)(2,1)S(1)}, bf16[2,64,256]{2,1,0:T(8,128)(2,1)S(1)}, u32[]{:S(2)}, u32[]{:S(2)}) collective-permute-start(bf16[2,64,256]{2,1,0:T(8,128)(2,1)S(1)} %get-tuple-element.36), channel_id=1, source_target_pairs={{0,8},{4,12},{8,0},{12,4},{16,24},{20,28},{24,16},{28,20},{1,9},{5... | collective-permute-start | bytes 196616 | tf_op jit(solution)/shard_map/ppermute | solution.py:456
  10.5 0.0 collective-permute-done.four_ref
  10.5 0.0 collective-permute-start.4
  10.5 0.0 copy-done.1
  10.5 1.5 %local.1 = (bf16[2,128,256]{2,1,0:T(8,128)(2,1)S(1)}, bf16[128,256]{1,0:T(8,128)(2,1)S(1)}, bf16[64,256]{1,0:T(8,128)(2,1)S(1)}, bf16[32,256]{1,0:T(8,128)(2,1)S(1)}, f32[3,512,256]{2,1,0:T(8,128)S(1)}) custom-call(bf16[512,256]{1,0:T(8,128)(2,1)S(1)} %bitcast.2, bf16[512,256]{1,0:T(8,128)(2,1)S(1)} %get-tuple-element.27.k_ref, ...), custom_call_target="tpu_custom_call" | custom-call | tf_op jit(solution)/shard_map/local/pallas_call | solution.py:516
  12.0 1.2 %collective-permute-done.6.six_ref = bf16[2,32,256]{2,1,0:T(8,128)(2,1)S(1)} collective-permute-done((bf16[2,32,256]{2,1,0:T(8,128)(2,1)S(1)}, bf16[2,32,256]{2,1,0:T(8,128)(2,1)S(1)}, u32[]{:S(2)}, u32[]{:S(2)}) %collective-permute-start.6) | collective-permute-done | bytes 32800 | tf_op jit(solution)/shard_map/ppermute | solution.py:456
  13.2 0.9 %collective-permute-start.7 = (bf16[2,64,256]{2,1,0:T(8,128)(2,1)S(1)}, bf16[2,64,256]{2,1,0:T(8,128)(2,1)S(1)}, u32[]{:S(2)}, u32[]{:S(2)}) collective-permute-start(bf16[2,64,256]{2,1,0:T(8,128)(2,1)S(1)} %join.1.fours_a), channel_id=1, source_target_pairs={{0,4},{4,0},{8,12},{12,8},{16,20},{20,16},{24,28},{28,24},{1,5},{5... | collective-permute-start | bytes 196616 | tf_op jit(solution)/shard_map/ppermute | solution.py:456
  14.2 0.0 collective-permute-done.2.three_a
  14.2 0.6 %collective-permute-done.3.three_b = bf16[2,64,256]{2,1,0:T(8,128)(2,1)S(1)} collective-permute-done((bf16[2,64,256]{2,1,0:T(8,128)(2,1)S(1)}, bf16[2,64,256]{2,1,0:T(8,128)(2,1)S(1)}, u32[]{:S(2)}, u32[]{:S(2)}) %collective-permute-start.3) | collective-permute-done | bytes 65568 | tf_op jit(solution)/shard_map/ppermute | solution.py:456
  14.8 0.0 collective-permute-done.1.first_ref
  14.8 0.5 %coarse.1 = (f32[3,128,256]{2,1,0:T(8,128)S(1)}, bf16[2,32,256]{2,1,0:T(8,128)(2,1)S(1)}) custom-call(bf16[128,256]{1,0:T(8,128)(2,1)S(1)} %get-tuple-element.33.two_q, bf16[64,256]{1,0:T(8,128)(2,1)S(1)} %get-tuple-element.34.three_q, bf16[2,224,256]{2,1,0:T(8,128)(2,1)S(1)} %collective-permute-done.1.first_ref, ...), custom_call_target="tpu_custom_call" | custom-call | flops 2147483648 | bytes 2097152 | tf_op jit(solution)/shard_map/coarse/pallas_call | solution.py:542
  15.3 0.0 collective-permute-done.4.second_ref
  15.3 0.0 copy-start
  15.3 0.9 %mid.1 = (f32[2,512,256]{2,1,0:T(8,128)S(1)}, bf16[128,256]{1,0:T(8,128)(2,1)S(1)}) custom-call(bf16[2,128,256]{2,1,0:T(8,128)(2,1)S(1)} %get-tuple-element.32.edge_q, f32[3,128,256]{2,1,0:T(8,128)S(1)} %get-tuple-element.37.coarse, f32[3,512,256]{2,1,0:T(8,128)S(1)} %get-tuple-element.38.state, bf16[2,224,256]{2,1,0:T(8,128)(2,1)S(1)} %collective-permute-done.1.first_ref, ...), custom_call_target="tpu_custom_call" | custom-call | tf_op jit(solution)/shard_map/mid/pallas_call | solution.py:559
  16.2 0.1 collective-permute-start.5
  16.3 1.2 %collective-permute-done.7.fours_b = bf16[2,64,256]{2,1,0:T(8,128)(2,1)S(1)} collective-permute-done((bf16[2,64,256]{2,1,0:T(8,128)(2,1)S(1)}, bf16[2,64,256]{2,1,0:T(8,128)(2,1)S(1)}, u32[]{:S(2)}, u32[]{:S(2)}) %collective-permute-start.7) | collective-permute-done | bytes 65568 | tf_op jit(solution)/shard_map/ppermute | solution.py:456
  17.5 0.6 %finish.1 = (bf16[128,256]{1,0:T(8,128)(2,1)S(1)}, bf16[16,256]{1,0:T(8,128)(2,1)S(1)}, f32[2,32,256]{2,1,0:T(8,128)S(1)}) custom-call(bf16[32,256]{1,0:T(8,128)(2,1)S(1)} %get-tuple-element.42.query_ref.four_q, f32[2,512,256]{2,1,0:T(8,128)S(1)} %get-tuple-element.41.fine, bf16[2,32,256]{2,1,0:T(8,128)(2,1)S(1)} %get-tuple-element.31.four_ref, ...), custom_call_target="tpu_custom_call" | custom-call | tf_op jit(solution)/shard_map/finish/pallas_call | solution.py:584
  18.1 1.5 %collective-permute-start.8 = (bf16[128,256]{1,0:T(8,128)(2,1)S(1)}, bf16[128,256]{1,0:T(8,128)(2,1)S(1)}, u32[]{:S(2)}, u32[]{:S(2)}) collective-permute-start(bf16[128,256]{1,0:T(8,128)(2,1)S(1)} %get-tuple-element.46), channel_id=1, source_target_pairs={{0,2},{1,3},{2,0},{3,1},{4,6},{5,7},{6,4},{7,5},{8,10},{9,11},{10,... | collective-permute-start | bytes 196616 | tf_op jit(solution)/shard_map/ppermute | solution.py:456
  19.6 0.3 %collective-permute-start.9 = (bf16[16,256]{1,0:T(8,128)(2,1)S(1)}, bf16[16,256]{1,0:T(8,128)(2,1)S(1)}, u32[]{:S(2)}, u32[]{:S(2)}) collective-permute-start(bf16[16,256]{1,0:T(8,128)(2,1)S(1)} %get-tuple-element.47), channel_id=1, source_target_pairs={{0,3},{1,2},{2,1},{3,0},{4,7},{5,6},{6,5},{7,4},{8,11},{9,10},{10,... | collective-permute-start | bytes 24584 | tf_op jit(solution)/shard_map/ppermute | solution.py:456
  19.9 0.1 rest.1
  20.0 0.4 %collective-permute-start.10 = (bf16[128,256]{1,0:T(8,128)(2,1)S(1)}, bf16[128,256]{1,0:T(8,128)(2,1)S(1)}, u32[]{:S(2)}, u32[]{:S(2)}) collective-permute-start(bf16[128,256]{1,0:T(8,128)(2,1)S(1)} %get-tuple-element.48), channel_id=1, source_target_pairs={{0,1},{1,0},{2,3},{3,2},{4,5},{5,4},{6,7},{7,6},{8,9},{9,8},{10,11... | collective-permute-start | bytes 196616 | tf_op jit(solution)/shard_map/ppermute | solution.py:456
  20.4 0.0 copy-done
  20.4 0.2 partial.1.partial_ref
  20.6 0.0 collective-permute-done.5.refs_0_
  20.7 1.9 %collective-permute-done.8.refs_0_ = bf16[128,256]{1,0:T(8,128)(2,1)S(1)} collective-permute-done((bf16[128,256]{1,0:T(8,128)(2,1)S(1)}, bf16[128,256]{1,0:T(8,128)(2,1)S(1)}, u32[]{:S(2)}, u32[]{:S(2)}) %collective-permute-start.8) | collective-permute-done | bytes 65568 | tf_op jit(solution)/shard_map/ppermute | solution.py:456
  22.5 0.2 further.1.further_ref.partial_ref
  22.8 0.0 collective-permute-done.9.refs_0_
  22.8 0.0 collective-permute-done.10.refs_2_
  22.8 1.1 %project.1 = bf16[128,1024]{1,0:T(8,128)(2,1)} custom-call(f32[128,1024]{1,0:T(8,128)S(1)} %further.1.further_ref.partial_ref, f32[128,256]{1,0:T(8,128)S(1)} %widen.1.widened_ref.refs_0_, bf16[16,256]{1,0:T(8,128)(2,1)S(1)} %gate.1.refs_1_, bf16[128,256]{1,0:T(8,128)(2,1)S(1)} %collective-permute-done.10.refs_2_, bf16[1024,1024]{1,0:T(8,128)(2,1)S(1)} %copy-done), custom_call_target="tpu_custom_call" | custom-call | tf_op jit(solution)/shard_map/project/pallas_call | solution.py:631
  (4 shorter events, 0.1 us)
Async XLA Ops:
  1.4 13.4 %collective-permute-start.1 = (bf16[2,224,256]{2,1,0:T(8,128)(2,1)S(1)}, bf16[2,224,256]{2,1,0:T(8,128)(2,1)S(1)}, u32[]{:S(2)}, u32[]{:S(2)}) collective-permute-start(bf16[2,224,256]{2,1,0:T(8,128)(2,1)S(1)} %get-tuple-element.35), channel_id=1, source_target_pairs={{0,4},{4,0},{8,12},{12,8},{16,20},{20,16},{24,28},{28,24},{1,5},{5... | collective-permute-start | bytes 688136 | tf_op jit(solution)/shard_map/ppermute | solution.py:456
  4.4 6.0 %copy-start.1 = (bf16[1,512,256]{2,1,0:T(8,128)(2,1)S(1)}, bf16[1,512,256]{2,1,0:T(8,128)(2,1)}, u32[]{:S(2)}) copy-start(bf16[1,512,256]{2,1,0:T(8,128)(2,1)} %param.4) | copy-start | bytes 786436
  4.5 6.0 %collective-permute-start = (bf16[2,32,256]{2,1,0:T(8,128)(2,1)S(1)}, bf16[2,32,256]{2,1,0:T(8,128)(2,1)S(1)}, u32[]{:S(2)}, u32[]{:S(2)}) collective-permute-start(bf16[2,32,256]{2,1,0:T(8,128)(2,1)S(1)} %get-tuple-element.31.four_ref), channel_id=1, source_target_pairs={{0,16},{4,20},{8,24},{12,28},{16,0},{20,4},{24,8},{28,12},{1,17},{... | collective-permute-start | bytes 98312 | tf_op jit(solution)/shard_map/ppermute | solution.py:456
  7.1 6.1 %collective-permute-start.6 = (bf16[2,32,256]{2,1,0:T(8,128)(2,1)S(1)}, bf16[2,32,256]{2,1,0:T(8,128)(2,1)S(1)}, u32[]{:S(2)}, u32[]{:S(2)}) collective-permute-start(bf16[2,32,256]{2,1,0:T(8,128)(2,1)S(1)} %get-tuple-element.31.four_ref), channel_id=1, source_target_pairs={{0,24},{4,28},{8,16},{12,20},{16,8},{20,12},{24,0},{28,4},{1,25},{... | collective-permute-start | bytes 98312 | tf_op jit(solution)/shard_map/ppermute | solution.py:456
  8.5 5.7 %collective-permute-start.2 = (bf16[2,64,256]{2,1,0:T(8,128)(2,1)S(1)}, bf16[2,64,256]{2,1,0:T(8,128)(2,1)S(1)}, u32[]{:S(2)}, u32[]{:S(2)}) collective-permute-start(bf16[2,64,256]{2,1,0:T(8,128)(2,1)S(1)} %get-tuple-element.36), channel_id=1, source_target_pairs={{0,12},{4,8},{8,4},{12,0},{16,28},{20,24},{24,20},{28,16},{1,13},{... | collective-permute-start | bytes 196616 | tf_op jit(solution)/shard_map/ppermute | solution.py:456
  8.7 6.1 %collective-permute-start.3 = (bf16[2,64,256]{2,1,0:T(8,128)(2,1)S(1)}, bf16[2,64,256]{2,1,0:T(8,128)(2,1)S(1)}, u32[]{:S(2)}, u32[]{:S(2)}) collective-permute-start(bf16[2,64,256]{2,1,0:T(8,128)(2,1)S(1)} %get-tuple-element.36), channel_id=1, source_target_pairs={{0,8},{4,12},{8,0},{12,4},{16,24},{20,28},{24,16},{28,20},{1,9},{5... | collective-permute-start | bytes 196616 | tf_op jit(solution)/shard_map/ppermute | solution.py:456
  10.5 4.8 %collective-permute-start.4 = (bf16[2,128,256]{2,1,0:T(8,128)(2,1)S(1)}, bf16[2,128,256]{2,1,0:T(8,128)(2,1)S(1)}, u32[]{:S(2)}, u32[]{:S(2)}) collective-permute-start(bf16[2,128,256]{2,1,0:T(8,128)(2,1)S(1)} %get-tuple-element.39), channel_id=1, source_target_pairs={{0,1},{1,0},{2,3},{3,2},{4,8},{5,9},{6,10},{7,11},{8,4},{9,5},{10,... | collective-permute-start | bytes 393224 | tf_op jit(solution)/shard_map/ppermute | solution.py:467
  13.2 4.3 %collective-permute-start.7 = (bf16[2,64,256]{2,1,0:T(8,128)(2,1)S(1)}, bf16[2,64,256]{2,1,0:T(8,128)(2,1)S(1)}, u32[]{:S(2)}, u32[]{:S(2)}) collective-permute-start(bf16[2,64,256]{2,1,0:T(8,128)(2,1)S(1)} %join.1.fours_a), channel_id=1, source_target_pairs={{0,4},{4,0},{8,12},{12,8},{16,20},{20,16},{24,28},{28,24},{1,5},{5... | collective-permute-start | bytes 196616 | tf_op jit(solution)/shard_map/ppermute | solution.py:456
  15.3 5.1 %copy-start = (bf16[1024,1024]{1,0:T(8,128)(2,1)S(1)}, bf16[1024,1024]{1,0:T(8,128)(2,1)}, u32[]{:S(2)}) copy-start(bf16[1024,1024]{1,0:T(8,128)(2,1)} %refs_3_.1) | copy-start | bytes 6291460
  16.2 4.4 %collective-permute-start.5 = (bf16[128,256]{1,0:T(8,128)(2,1)S(1)}, bf16[128,256]{1,0:T(8,128)(2,1)S(1)}, u32[]{:S(2)}, u32[]{:S(2)}) collective-permute-start(bf16[128,256]{1,0:T(8,128)(2,1)S(1)} %get-tuple-element.40), channel_id=1, source_target_pairs={{0,3},{1,2},{2,1},{3,0},{4,7},{5,6},{6,5},{7,4},{8,11},{9,10},{10,... | collective-permute-start | bytes 196616 | tf_op jit(solution)/shard_map/ppermute | solution.py:456
  18.1 4.4 %collective-permute-start.8 = (bf16[128,256]{1,0:T(8,128)(2,1)S(1)}, bf16[128,256]{1,0:T(8,128)(2,1)S(1)}, u32[]{:S(2)}, u32[]{:S(2)}) collective-permute-start(bf16[128,256]{1,0:T(8,128)(2,1)S(1)} %get-tuple-element.46), channel_id=1, source_target_pairs={{0,2},{1,3},{2,0},{3,1},{4,6},{5,7},{6,4},{7,5},{8,10},{9,11},{10,... | collective-permute-start | bytes 196616 | tf_op jit(solution)/shard_map/ppermute | solution.py:456
  19.6 3.2 %collective-permute-start.9 = (bf16[16,256]{1,0:T(8,128)(2,1)S(1)}, bf16[16,256]{1,0:T(8,128)(2,1)S(1)}, u32[]{:S(2)}, u32[]{:S(2)}) collective-permute-start(bf16[16,256]{1,0:T(8,128)(2,1)S(1)} %get-tuple-element.47), channel_id=1, source_target_pairs={{0,3},{1,2},{2,1},{3,0},{4,7},{5,6},{6,5},{7,4},{8,11},{9,10},{10,... | collective-permute-start | bytes 24584 | tf_op jit(solution)/shard_map/ppermute | solution.py:456
  20.0 2.8 %collective-permute-start.10 = (bf16[128,256]{1,0:T(8,128)(2,1)S(1)}, bf16[128,256]{1,0:T(8,128)(2,1)S(1)}, u32[]{:S(2)}, u32[]{:S(2)}) collective-permute-start(bf16[128,256]{1,0:T(8,128)(2,1)S(1)} %get-tuple-element.48), channel_id=1, source_target_pairs={{0,1},{1,0},{2,3},{3,2},{4,5},{5,4},{6,7},{7,6},{8,9},{9,8},{10,11... | collective-permute-start | bytes 196616 | tf_op jit(solution)/shard_map/ppermute | solution.py:456

commit v8 on v3

--- a/solution.py
+++ b/solution.py
@@ -42,7 +42,8 @@
 
 
 def pool_kernel(
-    k_hbm, v_hbm, k_ref, v_ref, first_ref, one_ref, two_ref, scratch, sems
+    k_hbm, v_hbm, k_ref, v_ref, first_ref, one_ref, second_ref, three_ref, four_ref,
+    two_ref, scratch, sems,
 ):
     rows = k_ref.shape[0]
     blocks = rows // BLOCK
@@ -73,18 +74,6 @@
         first_ref[which, BLOCK:, :] = jnp.where(
             even, two_ref[which, :inner, :], two_ref[which, BLOCK // 4 :, :]
         )
-
-
-def repooled(field):
-    rows, lanes = field.shape
-    slabs = field.astype(jnp.float32).reshape(rows // (2 * SLAB), 2, SLAB, lanes)
-    return ((slabs[:, 0] + slabs[:, 1]) * root_half).reshape(rows // 2, lanes).astype(jnp.bfloat16)
-
-
-def deeper_kernel(k_ref, v_ref, two_ref, second_ref, three_ref, four_ref):
-    rows = k_ref.shape[0]
-    even = lax.rem(lax.axis_index("seq"), 2) == 0
-    for which, ref in enumerate((k_ref, v_ref)):
         second_ref[which] = jnp.where(even, ref[:BLOCK, :], ref[rows - BLOCK :, :])
         three = repooled(two_ref[which])
         three_ref[which] = three
@@ -472,7 +461,7 @@
 
     hbm = pl.BlockSpec(memory_space=pltpu.HBM)
     vmem = pl.BlockSpec(memory_space=pltpu.VMEM)
-    keys, values, first, one, two = pl.pallas_call(
+    keys, values, first, one, second, three, four = pl.pallas_call(
         pool_kernel,
         in_specs=[hbm] * 2,
         out_shape=[
@@ -480,27 +469,18 @@
             bf16(rows, features),
             bf16(2, BLOCK + rows // 4 - BLOCK // 4, features),
             bf16(2, rows // 2, features),
-            bf16(2, rows // 4, features),
-        ],
-        scratch_shapes=[
-            pltpu.VMEM((2, rows // BLOCK, pairs, BLOCK, PAIR), jnp.float32),
-            pltpu.SemaphoreType.DMA((2, 2)),
-        ],
-        compiler_params=params,
-        name="pool",
-    )(key_vectors, value_vectors)
-    second, three, four = pl.pallas_call(
-        deeper_kernel,
-        out_shape=[
             bf16(2, BLOCK, features),
             bf16(2, rows // 8, features),
             bf16(2, rows // 16, features),
         ],
-        compiler_params=params,
-        cost_estimate=pl.CostEstimate(flops=2**31, bytes_accessed=2**23, transcendentals=0),
-        name="deeper",
-    )(keys, values, two)
-
+        scratch_shapes=[
+            pltpu.VMEM((2, rows // 4, features), jnp.bfloat16),
+            pltpu.VMEM((2, rows // BLOCK, pairs, BLOCK, PAIR), jnp.float32),
+            pltpu.SemaphoreType.DMA((2, 2)),
+        ],
+        compiler_params=params,
+        name="pool",
+    )(key_vectors, value_vectors)
     first_in = swapped(first, "seq", 1)
     second_in = across(second)
     four_in = swapped(four, "seq", 4)

time: 24.2 us -> 24.6 us (1.017)
  waiting for transfers between devices: 4.86 us -> 3.4 us
  local copies, waits for them, and re-layouts: 0.01 us -> 0.95 us
  starting transfers between devices: 12.2 us -> 13.1 us
    ppermute x10, waiting for transfers between devices: 4.86 us -> 3.4 us  [swapped(): lax.ppermute(block, axis, [(i, i ^ mask) for i in range(lax.axis_size(axi...]
    unnamed x4, local copies, waits for them, and re-layouts: 0.01 us -> 0.95 us
    ppermute x10, starting transfers between devices: 12.2 us -> 13.1 us  [swapped(): lax.ppermute(block, axis, [(i, i ^ mask) for i in range(lax.axis_size(axi...]
where the time goes in v8:
time: 24.6 us; the launch traced here: 24.4 us
  starting transfers between devices  13.1 us (53%)
  Pallas kernels  6.83 us (28%)
  waiting for transfers between devices  3.4 us (14%)
  local copies, waits for them, and re-layouts  0.95 us (4%)
    ppermute x10, starting transfers between devices, swapped(): lax.ppermute(block, axis, [(i, i ^ mask) for i in range(lax.axis_size(axi...  13.1 us
    ppermute x10, waiting for transfers between devices, swapped(): lax.ppermute(block, axis, [(i, i ^ mask) for i in range(lax.axis_size(axi...  3.4 us
    pallas_call x1, Pallas kernels, per_device(): pl.pallas_call(local_kernel, out_shape=[bf16(2, BLOCK, features), bf16(ro...  1.54 us
    pallas_call x1, Pallas kernels, per_device(): pl.pallas_call(pool_kernel, in_specs=[hbm] * 2, out_shape=[bf16(rows, fea...  1.42 us
    pallas_call x1, Pallas kernels, per_device(): pl.pallas_call(project_kernel, in_specs=[vmem] * (len(rejoined) + 3), out...  1.05 us
    unnamed x4, local copies, waits for them, and re-layouts  0.95 us
    pallas_call x1, Pallas kernels, per_device(): pl.pallas_call(mid_kernel, out_shape=[jax.ShapeDtypeStruct((2, rows, feat...  0.93 us
    pallas_call x1, Pallas kernels, per_device(): pl.pallas_call(finish_kernel, out_shape=parts[2:] + [bf16(2 * SLAB, featu...  0.61 us
  transfers between devices with their start and end apart: 11, of which 4 were waited for; matrix products, arithmetic and copies ran while one was open for 0% of the time, Pallas kernels for 18%

profile of v8, /device:TPU:0, one launch (start us, length us, event | category | flops | bytes accessed | tf_op | source)
XLA Modules:
  0.0 24.4 jit_solution(8922559384680739629)
XLA Ops:
  0.0 1.4 %pool.1 = (bf16[512,256]{1,0:T(8,128)(2,1)S(1)}, bf16[512,256]{1,0:T(8,128)(2,1)S(1)}, bf16[2,224,256]{2,1,0:T(8,128)(2,1)S(1)}, bf16[2,256,256]{2,1,0:T(8,128)(...) custom-call(bf16[1,512,256]{2,1,0:T(8,128)(2,1)} %k_hbm.1, ...), custom_call_target="tpu_custom_call" | custom-call | tf_op jit(solution)/shard_map/pool/pallas_call | solution.py:464
  1.4 3.0 %collective-permute-start.1 = (bf16[2,224,256]{2,1,0:T(8,128)(2,1)S(1)}, bf16[2,224,256]{2,1,0:T(8,128)(2,1)S(1)}, u32[]{:S(2)}, u32[]{:S(2)}) collective-permute-start(bf16[2,224,256]{2,1,0:T(8,128)(2,1)S(1)} %get-tuple-element.33), channel_id=1, source_target_pairs={{0,4},{4,0},{8,12},{12,8},{16,20},{20,16},{24,28},{28,24},{1,5},{5... | collective-permute-start | bytes 688136 | tf_op jit(solution)/shard_map/ppermute | solution.py:438
  4.5 2.6 %collective-permute-start = (bf16[2,32,256]{2,1,0:T(8,128)(2,1)S(1)}, bf16[2,32,256]{2,1,0:T(8,128)(2,1)S(1)}, u32[]{:S(2)}, u32[]{:S(2)}) collective-permute-start(bf16[2,32,256]{2,1,0:T(8,128)(2,1)S(1)} %get-tuple-element.29.four_ref), channel_id=1, source_target_pairs={{0,16},{4,20},{8,24},{12,28},{16,0},{20,4},{24,8},{28,12},{1,17},{... | collective-permute-start | bytes 98312 | tf_op jit(solution)/shard_map/ppermute | solution.py:438
  7.1 1.3 %collective-permute-start.6 = (bf16[2,32,256]{2,1,0:T(8,128)(2,1)S(1)}, bf16[2,32,256]{2,1,0:T(8,128)(2,1)S(1)}, u32[]{:S(2)}, u32[]{:S(2)}) collective-permute-start(bf16[2,32,256]{2,1,0:T(8,128)(2,1)S(1)} %get-tuple-element.29.four_ref), channel_id=1, source_target_pairs={{0,24},{4,28},{8,16},{12,20},{16,8},{20,12},{24,0},{28,4},{1,25},{... | collective-permute-start | bytes 98312 | tf_op jit(solution)/shard_map/ppermute | solution.py:438
  8.4 0.2 collective-permute-start.2
  8.6 1.8 %collective-permute-start.3 = (bf16[2,64,256]{2,1,0:T(8,128)(2,1)S(1)}, bf16[2,64,256]{2,1,0:T(8,128)(2,1)S(1)}, u32[]{:S(2)}, u32[]{:S(2)}) collective-permute-start(bf16[2,64,256]{2,1,0:T(8,128)(2,1)S(1)} %get-tuple-element.34), channel_id=1, source_target_pairs={{0,8},{4,12},{8,0},{12,4},{16,24},{20,28},{24,16},{28,20},{1,9},{5... | collective-permute-start | bytes 196616 | tf_op jit(solution)/shard_map/ppermute | solution.py:438
  10.4 0.0 collective-permute-done.four_ref
  10.4 0.0 collective-permute-start.4
  10.4 0.0 copy-start.1
  10.4 0.9 %copy-done.1 = bf16[1,512,256]{2,1,0:T(8,128)(2,1)S(1)} copy-done((bf16[1,512,256]{2,1,0:T(8,128)(2,1)S(1)}, bf16[1,512,256]{2,1,0:T(8,128)(2,1)}, u32[]{:S(2)}) %copy-start.1) | copy-done | bytes 262168
  11.3 1.5 %local.1 = (bf16[2,128,256]{2,1,0:T(8,128)(2,1)S(1)}, bf16[128,256]{1,0:T(8,128)(2,1)S(1)}, bf16[64,256]{1,0:T(8,128)(2,1)S(1)}, bf16[32,256]{1,0:T(8,128)(2,1)S(1)}, f32[3,512,256]{2,1,0:T(8,128)S(1)}) custom-call(bf16[512,256]{1,0:T(8,128)(2,1)S(1)} %bitcast.2, bf16[512,256]{1,0:T(8,128)(2,1)S(1)} %get-tuple-element.26.k_ref, ...), custom_call_target="tpu_custom_call" | custom-call | tf_op jit(solution)/shard_map/local/pallas_call | solution.py:489
  12.9 0.2 %collective-permute-done.6.six_ref = bf16[2,32,256]{2,1,0:T(8,128)(2,1)S(1)} collective-permute-done((bf16[2,32,256]{2,1,0:T(8,128)(2,1)S(1)}, bf16[2,32,256]{2,1,0:T(8,128)(2,1)S(1)}, u32[]{:S(2)}, u32[]{:S(2)}) %collective-permute-start.6) | collective-permute-done | bytes 32800 | tf_op jit(solution)/shard_map/ppermute | solution.py:438
  13.1 1.9 %collective-permute-start.7 = (bf16[2,64,256]{2,1,0:T(8,128)(2,1)S(1)}, bf16[2,64,256]{2,1,0:T(8,128)(2,1)S(1)}, u32[]{:S(2)}, u32[]{:S(2)}) collective-permute-start(bf16[2,64,256]{2,1,0:T(8,128)(2,1)S(1)} %join.1.fours_a), channel_id=1, source_target_pairs={{0,4},{4,0},{8,12},{12,8},{16,20},{20,16},{24,28},{28,24},{1,5},{5... | collective-permute-start | bytes 196616 | tf_op jit(solution)/shard_map/ppermute | solution.py:438
  15.0 0.0 collective-permute-done.2.three_a
  15.0 0.0 collective-permute-done.3.three_b
  15.0 0.0 collective-permute-done.1.first_ref
  15.0 0.5 %coarse.1 = (f32[3,128,256]{2,1,0:T(8,128)S(1)}, bf16[2,32,256]{2,1,0:T(8,128)(2,1)S(1)}) custom-call(bf16[128,256]{1,0:T(8,128)(2,1)S(1)} %get-tuple-element.31.two_q, bf16[64,256]{1,0:T(8,128)(2,1)S(1)} %get-tuple-element.32.three_q, bf16[2,224,256]{2,1,0:T(8,128)(2,1)S(1)} %collective-permute-done.1.first_ref, ...), custom_call_target="tpu_custom_call" | custom-call | flops 2147483648 | bytes 2097152 | tf_op jit(solution)/shard_map/coarse/pallas_call | solution.py:515
  15.5 0.0 collective-permute-done.4.second_ref
  15.5 0.0 copy-start
  15.6 0.9 %mid.1 = (f32[2,512,256]{2,1,0:T(8,128)S(1)}, bf16[128,256]{1,0:T(8,128)(2,1)S(1)}) custom-call(bf16[2,128,256]{2,1,0:T(8,128)(2,1)S(1)} %get-tuple-element.30.edge_q, f32[3,128,256]{2,1,0:T(8,128)S(1)} %get-tuple-element.35.coarse, f32[3,512,256]{2,1,0:T(8,128)S(1)} %get-tuple-element.36.state, bf16[2,224,256]{2,1,0:T(8,128)(2,1)S(1)} %collective-permute-done.1.first_ref, ...), custom_call_target="tpu_custom_call" | custom-call | tf_op jit(solution)/shard_map/mid/pallas_call | solution.py:532
  16.5 0.1 collective-permute-start.5
  16.6 0.9 %collective-permute-done.7.fours_b = bf16[2,64,256]{2,1,0:T(8,128)(2,1)S(1)} collective-permute-done((bf16[2,64,256]{2,1,0:T(8,128)(2,1)S(1)}, bf16[2,64,256]{2,1,0:T(8,128)(2,1)S(1)}, u32[]{:S(2)}, u32[]{:S(2)}) %collective-permute-start.7) | collective-permute-done | bytes 65568 | tf_op jit(solution)/shard_map/ppermute | solution.py:438
  17.5 0.6 %finish.1 = (bf16[128,256]{1,0:T(8,128)(2,1)S(1)}, bf16[16,256]{1,0:T(8,128)(2,1)S(1)}, f32[2,32,256]{2,1,0:T(8,128)S(1)}) custom-call(bf16[32,256]{1,0:T(8,128)(2,1)S(1)} %get-tuple-element.40.query_ref.four_q, f32[2,512,256]{2,1,0:T(8,128)S(1)} %get-tuple-element.39.fine, bf16[2,32,256]{2,1,0:T(8,128)(2,1)S(1)} %get-tuple-element.29.four_ref, ...), custom_call_target="tpu_custom_call" | custom-call | tf_op jit(solution)/shard_map/finish/pallas_call | solution.py:557
  18.1 1.5 %collective-permute-start.8 = (bf16[128,256]{1,0:T(8,128)(2,1)S(1)}, bf16[128,256]{1,0:T(8,128)(2,1)S(1)}, u32[]{:S(2)}, u32[]{:S(2)}) collective-permute-start(bf16[128,256]{1,0:T(8,128)(2,1)S(1)} %get-tuple-element.44), channel_id=1, source_target_pairs={{0,2},{1,3},{2,0},{3,1},{4,6},{5,7},{6,4},{7,5},{8,10},{9,11},{10,... | collective-permute-start | bytes 196616 | tf_op jit(solution)/shard_map/ppermute | solution.py:438
  19.6 0.6 %collective-permute-start.9 = (bf16[16,256]{1,0:T(8,128)(2,1)S(1)}, bf16[16,256]{1,0:T(8,128)(2,1)S(1)}, u32[]{:S(2)}, u32[]{:S(2)}) collective-permute-start(bf16[16,256]{1,0:T(8,128)(2,1)S(1)} %get-tuple-element.45), channel_id=1, source_target_pairs={{0,3},{1,2},{2,1},{3,0},{4,7},{5,6},{6,5},{7,4},{8,11},{9,10},{10,... | collective-permute-start | bytes 24584 | tf_op jit(solution)/shard_map/ppermute | solution.py:438
  20.2 0.1 rest.1
  20.2 0.1 collective-permute-start.10
  20.4 0.0 copy-done
  20.4 0.2 partial.1.partial_ref
  20.6 0.3 %collective-permute-done.5.refs_0_ = bf16[128,256]{1,0:T(8,128)(2,1)S(1)} collective-permute-done((bf16[128,256]{1,0:T(8,128)(2,1)S(1)}, bf16[128,256]{1,0:T(8,128)(2,1)S(1)}, u32[]{:S(2)}, u32[]{:S(2)}) %collective-permute-start.5) | collective-permute-done | bytes 65568 | tf_op jit(solution)/shard_map/ppermute | solution.py:438
  20.9 2.0 %collective-permute-done.8.refs_0_ = bf16[128,256]{1,0:T(8,128)(2,1)S(1)} collective-permute-done((bf16[128,256]{1,0:T(8,128)(2,1)S(1)}, bf16[128,256]{1,0:T(8,128)(2,1)S(1)}, u32[]{:S(2)}, u32[]{:S(2)}) %collective-permute-start.8) | collective-permute-done | bytes 65568 | tf_op jit(solution)/shard_map/ppermute | solution.py:438
  22.9 0.2 further.1.further_ref.partial_ref
  23.1 0.0 collective-permute-done.9.refs_1_
  23.1 0.2 rejoin.1.refs_0_
  23.4 0.0 collective-permute-done.10.refs_1_
  23.4 1.0 %project.1 = bf16[128,1024]{1,0:T(8,128)(2,1)} custom-call(f32[128,1024]{1,0:T(8,128)S(1)} %further.1.further_ref.partial_ref, bf16[128,256]{1,0:T(8,128)(2,1)S(1)} %rejoin.1.refs_0_, bf16[128,256]{1,0:T(8,128)(2,1)S(1)} %collective-permute-done.10.refs_1_, bf16[1024,1024]{1,0:T(8,128)(2,1)S(1)} %copy-done), custom_call_target="tpu_custom_call" | custom-call | tf_op jit(solution)/shard_map/project/pallas_call | solution.py:604
  (2 shorter events, 0.0 us)
Async XLA Ops:
  1.4 13.6 %collective-permute-start.1 = (bf16[2,224,256]{2,1,0:T(8,128)(2,1)S(1)}, bf16[2,224,256]{2,1,0:T(8,128)(2,1)S(1)}, u32[]{:S(2)}, u32[]{:S(2)}) collective-permute-start(bf16[2,224,256]{2,1,0:T(8,128)(2,1)S(1)} %get-tuple-element.33), channel_id=1, source_target_pairs={{0,4},{4,0},{8,12},{12,8},{16,20},{20,16},{24,28},{28,24},{1,5},{5... | collective-permute-start | bytes 688136 | tf_op jit(solution)/shard_map/ppermute | solution.py:438
  4.5 5.9 %collective-permute-start = (bf16[2,32,256]{2,1,0:T(8,128)(2,1)S(1)}, bf16[2,32,256]{2,1,0:T(8,128)(2,1)S(1)}, u32[]{:S(2)}, u32[]{:S(2)}) collective-permute-start(bf16[2,32,256]{2,1,0:T(8,128)(2,1)S(1)} %get-tuple-element.29.four_ref), channel_id=1, source_target_pairs={{0,16},{4,20},{8,24},{12,28},{16,0},{20,4},{24,8},{28,12},{1,17},{... | collective-permute-start | bytes 98312 | tf_op jit(solution)/shard_map/ppermute | solution.py:438
  7.1 6.1 %collective-permute-start.6 = (bf16[2,32,256]{2,1,0:T(8,128)(2,1)S(1)}, bf16[2,32,256]{2,1,0:T(8,128)(2,1)S(1)}, u32[]{:S(2)}, u32[]{:S(2)}) collective-permute-start(bf16[2,32,256]{2,1,0:T(8,128)(2,1)S(1)} %get-tuple-element.29.four_ref), channel_id=1, source_target_pairs={{0,24},{4,28},{8,16},{12,20},{16,8},{20,12},{24,0},{28,4},{1,25},{... | collective-permute-start | bytes 98312 | tf_op jit(solution)/shard_map/ppermute | solution.py:438
  8.4 6.6 %collective-permute-start.2 = (bf16[2,64,256]{2,1,0:T(8,128)(2,1)S(1)}, bf16[2,64,256]{2,1,0:T(8,128)(2,1)S(1)}, u32[]{:S(2)}, u32[]{:S(2)}) collective-permute-start(bf16[2,64,256]{2,1,0:T(8,128)(2,1)S(1)} %get-tuple-element.34), channel_id=1, source_target_pairs={{0,12},{4,8},{8,4},{12,0},{16,28},{20,24},{24,20},{28,16},{1,13},{... | collective-permute-start | bytes 196616 | tf_op jit(solution)/shard_map/ppermute | solution.py:438
  8.6 6.4 %collective-permute-start.3 = (bf16[2,64,256]{2,1,0:T(8,128)(2,1)S(1)}, bf16[2,64,256]{2,1,0:T(8,128)(2,1)S(1)}, u32[]{:S(2)}, u32[]{:S(2)}) collective-permute-start(bf16[2,64,256]{2,1,0:T(8,128)(2,1)S(1)} %get-tuple-element.34), channel_id=1, source_target_pairs={{0,8},{4,12},{8,0},{12,4},{16,24},{20,28},{24,16},{28,20},{1,9},{5... | collective-permute-start | bytes 196616 | tf_op jit(solution)/shard_map/ppermute | solution.py:438
  10.4 5.2 %collective-permute-start.4 = (bf16[2,128,256]{2,1,0:T(8,128)(2,1)S(1)}, bf16[2,128,256]{2,1,0:T(8,128)(2,1)S(1)}, u32[]{:S(2)}, u32[]{:S(2)}) collective-permute-start(bf16[2,128,256]{2,1,0:T(8,128)(2,1)S(1)} %get-tuple-element.37), channel_id=1, source_target_pairs={{0,1},{1,0},{2,3},{3,2},{4,8},{5,9},{6,10},{7,11},{8,4},{9,5},{10,... | collective-permute-start | bytes 393224 | tf_op jit(solution)/shard_map/ppermute | solution.py:449
  10.4 1.0 %copy-start.1 = (bf16[1,512,256]{2,1,0:T(8,128)(2,1)S(1)}, bf16[1,512,256]{2,1,0:T(8,128)(2,1)}, u32[]{:S(2)}) copy-start(bf16[1,512,256]{2,1,0:T(8,128)(2,1)} %param.4) | copy-start | bytes 786436
  13.1 4.3 %collective-permute-start.7 = (bf16[2,64,256]{2,1,0:T(8,128)(2,1)S(1)}, bf16[2,64,256]{2,1,0:T(8,128)(2,1)S(1)}, u32[]{:S(2)}, u32[]{:S(2)}) collective-permute-start(bf16[2,64,256]{2,1,0:T(8,128)(2,1)S(1)} %join.1.fours_a), channel_id=1, source_target_pairs={{0,4},{4,0},{8,12},{12,8},{16,20},{20,16},{24,28},{28,24},{1,5},{5... | collective-permute-start | bytes 196616 | tf_op jit(solution)/shard_map/ppermute | solution.py:438
  15.5 4.8 %copy-start = (bf16[1024,1024]{1,0:T(8,128)(2,1)S(1)}, bf16[1024,1024]{1,0:T(8,128)(2,1)}, u32[]{:S(2)}) copy-start(bf16[1024,1024]{1,0:T(8,128)(2,1)} %refs_2_.1) | copy-start | bytes 6291460
  16.5 4.4 %collective-permute-start.5 = (bf16[128,256]{1,0:T(8,128)(2,1)S(1)}, bf16[128,256]{1,0:T(8,128)(2,1)S(1)}, u32[]{:S(2)}, u32[]{:S(2)}) collective-permute-start(bf16[128,256]{1,0:T(8,128)(2,1)S(1)} %get-tuple-element.38), channel_id=1, source_target_pairs={{0,3},{1,2},{2,1},{3,0},{4,7},{5,6},{6,5},{7,4},{8,11},{9,10},{10,... | collective-permute-start | bytes 196616 | tf_op jit(solution)/shard_map/ppermute | solution.py:438
  18.1 4.8 %collective-permute-start.8 = (bf16[128,256]{1,0:T(8,128)(2,1)S(1)}, bf16[128,256]{1,0:T(8,128)(2,1)S(1)}, u32[]{:S(2)}, u32[]{:S(2)}) collective-permute-start(bf16[128,256]{1,0:T(8,128)(2,1)S(1)} %get-tuple-element.44), channel_id=1, source_target_pairs={{0,2},{1,3},{2,0},{3,1},{4,6},{5,7},{6,4},{7,5},{8,10},{9,11},{10,... | collective-permute-start | bytes 196616 | tf_op jit(solution)/shard_map/ppermute | solution.py:438
  19.6 3.5 %collective-permute-start.9 = (bf16[16,256]{1,0:T(8,128)(2,1)S(1)}, bf16[16,256]{1,0:T(8,128)(2,1)S(1)}, u32[]{:S(2)}, u32[]{:S(2)}) collective-permute-start(bf16[16,256]{1,0:T(8,128)(2,1)S(1)} %get-tuple-element.45), channel_id=1, source_target_pairs={{0,3},{1,2},{2,1},{3,0},{4,7},{5,6},{6,5},{7,4},{8,11},{9,10},{10,... | collective-permute-start | bytes 24584 | tf_op jit(solution)/shard_map/ppermute | solution.py:438
  20.2 3.1 %collective-permute-start.10 = (bf16[128,256]{1,0:T(8,128)(2,1)S(1)}, bf16[128,256]{1,0:T(8,128)(2,1)S(1)}, u32[]{:S(2)}, u32[]{:S(2)}) collective-permute-start(bf16[128,256]{1,0:T(8,128)(2,1)S(1)} %get-tuple-element.46), channel_id=1, source_target_pairs={{0,1},{1,0},{2,3},{3,2},{4,5},{5,4},{6,7},{7,6},{8,9},{9,8},{10,11... | collective-permute-start | bytes 196616 | tf_op jit(solution)/shard_map/ppermute | solution.py:438
